TPU v7x, 32 devices: a whole 2x2x4 slice. The times are simulated.
32 devices in a mesh: row: 8 (over z, core), col: 2 (over x), vec: 2 (over y).
Axes of the slice: x: 2, y: 2, z: 4, core: 2. Of those that a mesh axis runs over, the one named last changes fastest.
Arguments:
- vectors: bfloat16 [16, 16384], P('vec', ('row', 'col')), may hold values from -6 to 6
- tile_vals: bfloat16 [8, 2, 256, 128, 128], P('row', 'col'), may hold values from -0.09375 to 0.09375
- tile_rows: int32 [8, 2, 256], P('row', 'col'), may hold values from 0 to 127, as said below
- tile_cols: int32 [8, 2, 256], P('row', 'col'), may hold values from 0 to 127, as said below
- tile_counts: int32 [8, 2], P('row', 'col'), may hold values from 1 to 256, as said below
Outputs:
- product: bfloat16 [16, 16384], P('vec', ('row', 'col'))
- gram: float32 [16, 16], P(None, 'vec')
Inputs may be any that keep to these rules, and one draw needn't show every extreme that they name: `tile_rows`: list [i, j] names tiles whose row index r has i * 16 <= r < (i + 1) * 16 and whose column index c has (c // 8) % (2) == j, that is the column's block of 8 tile rows, numbered c // 8, is held by column group j; live slots name distinct tiles with r >= c; slots at or beyond the count hold in-range indices that must be ignored. `tile_cols`: see tile_rows; the same slots. `tile_counts`: some lists are full in every draw; lists near the top of the triangle hold few tiles.
All inputs are finite; a program needn't handle non-finite values.
Results may differ from a plain program's by a relative error of at most 0.001.
Values may be sent and summed in bfloat16 or wider, within the bound.
No kernel may reach another device: no remote copies, remote signals or barrier semaphores. Data moves between devices by JAX's collectives and lax.ppermute only.
A program may use at most 64 MiB of HBM per device.

v0:
```python
import math

import jax
import jax.numpy as jnp
from jax import lax
from jax.sharding import PartitionSpec as P


def shards(vectors, tile_vals, tile_rows, tile_cols, tile_counts):
    nrow = lax.axis_size("row")
    ncol = lax.axis_size("col")
    vlocal, width = vectors.shape
    tile = tile_vals.shape[-1]
    stretch = width // tile
    span = ncol * stretch
    colspan = nrow * stretch
    row_x = lax.all_gather(vectors, "col", axis=1, tiled=True)
    col_x = lax.all_gather(vectors, "row", axis=1, tiled=True)
    tiles = tile_vals[0, 0]
    rows = tile_rows[0, 0]
    cols = tile_cols[0, 0]
    count = tile_counts[0, 0]
    slots = jnp.arange(rows.shape[0], dtype=jnp.int32)
    live = slots < count
    mirror = live & (rows != cols)
    row_place = rows % span
    col_place = cols // span * stretch + cols % stretch
    row_blocks = row_x.reshape(vlocal, span, tile)
    col_blocks = col_x.reshape(vlocal, colspan, tile)
    picked_cols = jnp.take(col_blocks, col_place, axis=1)
    picked_rows = jnp.take(row_blocks, row_place, axis=1)
    down = jnp.einsum("tij,vtj->vti", tiles, picked_cols, preferred_element_type=jnp.float32)
    upper = jnp.einsum("tij,vti->vtj", tiles, picked_rows, preferred_element_type=jnp.float32)
    row_hit = (
        (row_place[None, :] == jnp.arange(span, dtype=jnp.int32)[:, None]) & live[None, :]
    ).astype(jnp.float32)
    col_hit = (
        (col_place[None, :] == jnp.arange(colspan, dtype=jnp.int32)[:, None]) & mirror[None, :]
    ).astype(jnp.float32)
    row_part = jnp.einsum("at,vti->vai", row_hit, down, precision=lax.Precision.HIGHEST).reshape(
        vlocal, span * tile
    )
    col_part = jnp.einsum("at,vti->vai", col_hit, upper, precision=lax.Precision.HIGHEST).reshape(
        vlocal, colspan * tile
    )
    row_share = lax.psum_scatter(row_part, "col", scatter_dimension=1, tiled=True)
    col_share = lax.psum_scatter(col_part, "row", scatter_dimension=1, tiled=True)
    image = row_share + col_share
    every_vector = lax.all_gather(vectors, "vec", axis=0, tiled=True)
    partial_gram = jnp.dot(
        every_vector.astype(jnp.float32), image.T, precision=lax.Precision.HIGHEST
    )
    gram = lax.psum(partial_gram, ("row", "col")) / math.sqrt(width * nrow * ncol)
    return (image.astype(jnp.bfloat16), gram)


def solution(mesh):
    return jax.shard_map(
        shards,
        mesh=mesh,
        in_specs=(
            P("vec", ("row", "col")),
            P("row", "col", None, None, None),
            P("row", "col", None),
            P("row", "col", None),
            P("row", "col"),
        ),
        out_specs=(P("vec", ("row", "col")), P(None, "vec")),
        check_vma=False,
    )
```

profile of v0, /device:TPU:0, one launch (start us, length us, event | category | flops | bytes accessed | tf_op | source)
XLA Modules:
  0.0 118.5 jit_solution(5008786864088258881)
XLA Ops:
  7.2 0.0 copy-start
  7.2 0.0 copy-start.1
  7.2 0.0 reduce-scatter.3.cloned.1.call-start
  7.9 15.9 %all_gather.9 = bf16[8,8192]{1,0:T(8,128)(2,1)S(1)} all-gather(bf16[8,1024]{1,0:T(8,128)(2,1)} %param.5), channel_id=1, replica_groups=mesh['row'=8,'col'=2,'vec'=2] {'row'}, dimensions={1}, use_global_device_ids=true | all-gather | bytes 147456 | tf_op jit(solution)/shard_map/all_gather | solution.py:18
  23.8 0.7 compare_select_fusion.1
  24.5 0.8 gather_fusion
  25.3 0.7 compare_and_fusion.1
  26.1 6.8 %fusion.2 = f32[256,8,128]{2,1,0:T(8,128)S(1)} fusion(bf16[1,1,256,128,128]{4,3,2,1,0:T(8,128)(2,1)} %param.6, bf16[256,8,128]{2,1,0:T(8,128)(2,1)S(1)} %gather_fusion, pred[256]{0:T(512)(128)(4,1)S(1)} %get-tuple-element.8), kind=kOutput, calls=%fused_computation.4 | convolution fusion | flops 67371008 | bytes 9961728 | tf_op jit(solution)/shard_map/tij,vtj->vti/dot_general | solution.py:32
  32.9 0.6 convolution_bitcast_fusion.1
  33.4 0.6 copy.22
  34.1 0.0 reduce-scatter.3.cloned.1.call-update
  34.1 0.0 reduce-scatter.5.cloned.1.call-start
  34.2 0.0 copy-done
  34.2 4.4 %all_gather.10 = bf16[8,2048]{1,0:T(8,128)(2,1)S(1)} all-gather(bf16[8,1024]{1,0:T(8,128)(2,1)S(1)} %copy-done), channel_id=1, replica_groups=mesh['row'=8,'col'=2,'vec'=2] {'col'}, dimensions={1}, use_global_device_ids=true | all-gather | bytes 49152 | tf_op jit(solution)/shard_map/all_gather | solution.py:17
  38.6 0.0 copy-done.1
  38.6 0.8 gather_fusion.1
  39.4 4.8 %fusion = f32[256,8,128]{2,1,0:T(8,128)S(1)} fusion(bf16[1,1,256,128,128]{4,3,2,1,0:T(8,128)(2,1)} %param.6, bf16[256,8,128]{2,1,0:T(8,128)(2,1)S(1)} %gather_fusion.1, pred[256]{0:T(512)(128)(4,1)S(1)} %get-tuple-element.2), kind=kOutput, calls=%fused_computation.2 | convolution fusion | flops 67371008 | bytes 9961728 | tf_op jit(solution)/shard_map/tij,vti->vtj/dot_general | solution.py:33
  44.2 0.6 convolution_bitcast_fusion
  44.8 0.9 copy.21
  45.6 0.0 reduce-scatter.5.cloned.1.call-update
  45.7 4.4 %all_gather.11 = bf16[16,1024]{1,0:T(8,128)(2,1)S(1)} all-gather(bf16[8,1024]{1,0:T(8,128)(2,1)S(1)} %copy-done), channel_id=1, replica_groups=mesh['row'=8,'col'=2,'vec'=2] {'vec'}, dimensions={0}, use_global_device_ids=true | all-gather | bytes 49152 | tf_op jit(solution)/shard_map/all_gather | solution.py:49
  50.1 0.0 reduce-scatter.3.cloned.1.call-done
  50.1 27.7 %reduce-scatter.5.cloned.1.call-done = f32[8,1024]{1,0:T(8,128)} async-done(((f32[8,8192]{1,0:T(8,128)}), f32[8,1024]{1,0:T(8,128)}) %reduce-scatter.5.cloned.1.call-update) | async-done | bytes 32784 | tf_op jit(solution)/shard_map/reduce_scatter | solution.py:47
  77.8 0.9 convolution_bitcast_fusion.2
  78.7 31.0 %psum.7 = f32[16,8]{0,1:T(8,128)S(1)} all-reduce(f32[16,8]{0,1:T(8,128)S(1)} %convolution_bitcast_fusion.2), channel_id=1, replica_groups=mesh['row'=8,'col'=2,'vec'=2] {'row','col'}, use_global_device_ids=true, to_apply=%region_2.3 | all-reduce | flops 128 | bytes 1024 | tf_op jit(solution)/shard_map/psum | solution.py:53
  109.7 0.6 broadcast_multiply_fusion
  110.3 1.4 %add_convert_fusion = bf16[8,1024]{1,0:T(8,128)(2,1)} fusion(f32[8,1024]{1,0:T(8,128)} %reduce-scatter.3.cloned.1.call-done, f32[8,1024]{1,0:T(8,128)} %reduce-scatter.5.cloned.1.call-done), kind=kLoop, calls=%fused_computation.32 | loop fusion | flops 16384 | bytes 81920 | tf_op jit(solution)/shard_map/convert_element_type | solution.py:54
  (4 shorter events, 0.0 us)
Async XLA Ops:
  7.2 27.0 %copy-start = (bf16[8,1024]{1,0:T(8,128)(2,1)S(1)}, bf16[8,1024]{1,0:T(8,128)(2,1)}, u32[]{:S(2)}) copy-start(bf16[8,1024]{1,0:T(8,128)(2,1)} %param.5) | copy-start | bytes 49156
  7.2 31.4 %copy-start.1 = (s32[1,1,256]{2,1,0:T(1,128)S(1)}, s32[1,1,256]{2,1,0:T(1,128)}, u32[]{:S(2)}) copy-start(s32[1,1,256]{2,1,0:T(1,128)} %param.7) | copy-start | bytes 3076
  7.2 42.9 %reduce-scatter.3.cloned.1.call-start = ((), (), s32[]{:S(2)}) async-start(), calls=%async_computation.2 | async-start | bytes 98304 | tf_op jit(solution)/shard_map/reduce_scatter | solution.py:46
  34.1 43.7 %reduce-scatter.5.cloned.1.call-start = ((), (), s32[]{:S(2)}) async-start(), calls=%async_computation.3 | async-start | bytes 294912 | tf_op jit(solution)/shard_map/reduce_scatter | solution.py:47
Sparse Core Ops, SparseCore 0:
  34.2 10.8 reduce-scatter.2
  47.4 30.3 reduce-scatter.4
where the time goes:
time: 119 us; the launch traced here: 118 us
  blocking collectives  55.8 us (47%)
  waiting for transfers between devices  27.7 us (23%)
  between operations  14.7 us (12%)
  matrix products  13.6 us (11%)
  other arithmetic  3.42 us (3%)
  local copies, waits for them, and re-layouts  3.15 us (3%)
    psum x1, blocking collectives, shards(): lax.psum(partial_gram, ('row', 'col')) / math.sqrt(width * nrow * ncol)  31 us
    reduce_scatter x1, waiting for transfers between devices, shards(): lax.psum_scatter(col_part, 'row', scatter_dimension=1, tiled=True)  27.7 us
    all_gather x1, blocking collectives, shards(): col_x = lax.all_gather(vectors, 'row', axis=1, tiled=True)  15.9 us
    dot_general x1, matrix products, shards(): jnp.einsum('tij,vtj->vti', tiles, picked_cols, preferred_element_type=jnp...  6.82 us
    dot_general x1, matrix products, shards(): jnp.einsum('tij,vti->vtj', tiles, picked_rows, preferred_element_type=jnp...  4.76 us
    all_gather x1, blocking collectives, shards(): row_x = lax.all_gather(vectors, 'col', axis=1, tiled=True)  4.42 us
    all_gather x1, blocking collectives, shards(): every_vector = lax.all_gather(vectors, 'vec', axis=0, tiled=True)  4.42 us
  transfers between devices with their start and end apart: 2, of which 1 were waited for; matrix products, arithmetic and copies ran while one was open for 6% of the time, Pallas kernels for 0%

commit v1 on v0

v1 whole, which is shorter than its diff:
```python
import functools
import math

import jax
import jax.numpy as jnp
from jax import lax
from jax.experimental import pallas as pl
from jax.experimental.pallas import tpu as pltpu
from jax.sharding import PartitionSpec as P

CHUNK = 64
GROUP = 8
SMEM = pl.BlockSpec(memory_space=pltpu.SMEM)
VMEM = pl.BlockSpec(memory_space=pltpu.VMEM)
F32 = jnp.float32
HIGHEST = lax.Precision.HIGHEST


def params(mib):
    return pltpu.CompilerParams(vmem_limit_bytes=mib * 2**20)


def place_block(low, high, block, first, stretch, tile):
    vlocal = block.shape[0]
    zero = jnp.zeros((vlocal, tile), block.dtype)
    for q in range(stretch):
        part = block[:, q * tile : (q + 1) * tile]
        low[first + q] = jnp.concatenate([part, zero], axis=0)
        high[first + q] = jnp.concatenate([zero, part], axis=0)


def multiply_tiles(pick, forward, count, tiles, low, high, sums):
    slots = tiles.shape[0]
    tile = tiles.shape[-1]
    vlocal = sums[0].shape[1]
    for acc in sums:
        acc[...] = jnp.zeros_like(acc)

    def chunk(step, carry):
        for g in range(CHUNK // (2 * GROUP)):
            results = []
            for u in range(GROUP):
                s = step * CHUNK + g * 2 * GROUP + 2 * u
                in0, out0 = pick(s)
                in1, out1 = pick(s + 1)
                left = jnp.concatenate([low[in0], high[in1]], axis=1)
                if forward:
                    right = jnp.concatenate([tiles[s], tiles[s + 1]], axis=1)
                    dims = (((1,), (1,)), ((), ()))
                else:
                    right = tiles[pl.ds(s, 2)].reshape(2 * tile, tile)
                    dims = (((1,), (0,)), ((), ()))
                both = lax.dot_general(left, right, dims, preferred_element_type=F32)
                results.append((both, out0, out1))
            for u, (both, out0, out1) in enumerate(results):
                a, b = sums[(2 * u) % len(sums)], sums[(2 * u + 1) % len(sums)]
                a[out0] += both[:vlocal]
                b[out1] += both[vlocal:]
        return carry

    assert slots % CHUNK == 0
    lax.fori_loop(0, pl.cdiv(count, CHUNK), chunk, 0)


def places(rows, cols, span, stretch):
    def get(s):
        r, c = rows[s], cols[s]
        return r, c, lax.rem(r, span), lax.div(c, span) * stretch + lax.rem(c, stretch)

    return get


def mirror_kernel(sizes, pos, rows, cols, counts, tiles, *refs):
    nz, ncol, stretch = sizes
    span = ncol * stretch
    blocks, (mine, other), (low, high, *sums) = refs[:ncol], refs[ncol : ncol + 2], refs[ncol + 2 :]
    tile = tiles.shape[-1]
    width = stretch * tile
    count = counts[0]
    z, core, j = pos[0], pos[1], pos[2]
    for t in range(ncol):
        place_block(low, high, blocks[t], lax.rem(j + ncol - t, ncol) * stretch, stretch, tile)
    low[span] = jnp.zeros(low.shape[1:], low.dtype)
    high[span] = jnp.zeros(high.shape[1:], high.dtype)
    get = places(rows, cols, span, stretch)

    def pick(s):
        r, c, row_place, col_place = get(s)
        return jnp.where((s < count) & (r != c), row_place, span), col_place

    multiply_tiles(pick, False, count, tiles, low, high, sums)
    for s in range(nz):
        target = 2 * lax.rem(z + s, nz)
        for out, c in ((mine, core), (other, 1 - core)):
            for q in range(stretch):
                at = (target + c) * stretch + q
                total = sums[0][at]
                for acc in sums[1:]:
                    total += acc[at]
                out[:, s * width + q * tile : s * width + (q + 1) * tile] = total


def forward_kernel(sizes, pos, rows, cols, counts, tiles, near, far, *refs):
    nz, ncol, stretch = sizes
    span = ncol * stretch
    outs, (low, high, *sums) = refs[:ncol], refs[ncol:]
    tile = tiles.shape[-1]
    width = stretch * tile
    count = counts[0]
    z, core, j = pos[0], pos[1], pos[2]
    for s in range(nz):
        source = 2 * lax.rem(z + nz - s, nz)
        for ref, c in ((near, core), (far, 1 - core)):
            place_block(low, high, ref[:, s * width : (s + 1) * width], (source + c) * stretch, stretch, tile)
    dead = 2 * nz * stretch
    low[dead] = jnp.zeros(low.shape[1:], low.dtype)
    high[dead] = jnp.zeros(high.shape[1:], high.dtype)
    get = places(rows, cols, span, stretch)

    def pick(s):
        _, _, row_place, col_place = get(s)
        return jnp.where(s < count, col_place, dead), row_place

    multiply_tiles(pick, True, count, tiles, low, high, sums)
    for t in range(ncol):
        first = lax.rem(j + t, ncol) * stretch
        for q in range(stretch):
            total = sums[0][first + q]
            for acc in sums[1:]:
                total += acc[first + q]
            outs[t][:, q * tile : (q + 1) * tile] = total


def pair_kernel(nz, mine, theirs, *outs):
    width = mine.shape[1] // nz
    for s in range(nz):
        at = slice(s * width, (s + 1) * width)
        outs[s][...] = mine[:, at] + theirs[:, at]


def gram_kernel(nz, ncol, nvec, *refs):
    cols, refs = refs[:nz], refs[nz:]
    parts, refs = refs[:ncol], refs[ncol:]
    xs, (image, share) = refs[: nvec * ncol], refs[nvec * ncol :]
    total = parts[0][...]
    for ref in cols:
        total += ref[...]
    image[...] = total
    terms = [total] + [ref[...] for ref in parts[1:]]
    for k in range(nvec):
        product = None
        for t in range(ncol):
            one = lax.dot_general(
                xs[k * ncol + t][...].astype(F32),
                terms[t],
                (((1,), (1,)), ((), ())),
                precision=HIGHEST,
                preferred_element_type=F32,
            )
            product = one if product is None else product + one
        share[k] = product


def shards(sizes, vectors, tile_vals, tile_rows, tile_cols, tile_counts):
    nz, ncol, nvec = sizes
    nrow = 2 * nz
    vlocal, width = vectors.shape
    slots, tile = tile_vals.shape[2], tile_vals.shape[-1]
    stretch = width // tile
    span = ncol * stretch
    tiles, rows, cols, counts = tile_vals[0, 0], tile_rows[0, 0], tile_cols[0, 0], tile_counts[0]
    i, j, k = lax.axis_index("row"), lax.axis_index("col"), lax.axis_index("vec")
    pos = jnp.stack([i // 2, i % 2, j]).astype(jnp.int32)

    def core_swap(x):
        return lax.ppermute(x, "row", [(a, a ^ 1) for a in range(nrow)])

    def z_shift(x, s):
        return lax.ppermute(x, "row", [(a, (a + 2 * s) % nrow) for a in range(nrow)])

    def col_shift(x, t):
        return lax.ppermute(x, "col", [(a, (a + t) % ncol) for a in range(ncol)])

    def vec_shift(x, t):
        return lax.ppermute(x, "vec", [(a, (a + t) % nvec) for a in range(nvec)])

    row_x = [vectors] + [col_shift(vectors, t) for t in range(1, ncol)]
    near = jnp.concatenate([vectors] + [z_shift(vectors, s) for s in range(1, nz)], axis=1)
    far = core_swap(near)

    def tables(count):
        shape = pltpu.VMEM((count + 1, 2 * vlocal, tile), vectors.dtype)
        return [shape, shape]

    def sums(count):
        return [pltpu.VMEM((count, vlocal, tile), F32)] * 2

    block = jax.ShapeDtypeStruct((vlocal, width), F32)
    ring = jax.ShapeDtypeStruct((vlocal, nz * width), F32)
    step = (nz, ncol, stretch)
    cost = pl.CostEstimate(
        flops=2 * slots * tile * tile * 2 * vlocal, bytes_accessed=slots * tile * tile * 2, transcendentals=0
    )
    mine, other = pl.pallas_call(
        functools.partial(mirror_kernel, step),
        out_shape=[ring, ring],
        in_specs=[SMEM] * 4 + [VMEM] * (1 + ncol),
        out_specs=[VMEM] * 2,
        scratch_shapes=tables(span) + sums(nrow * stretch),
        compiler_params=params(24),
        cost_estimate=cost,
        name="mirror",
    )(pos, rows, cols, counts, tiles, *row_x)
    theirs = core_swap(other)
    pieces = pl.pallas_call(
        functools.partial(pair_kernel, nz),
        out_shape=[block] * nz,
        in_specs=[VMEM] * 2,
        out_specs=[VMEM] * nz,
        compiler_params=params(8),
        name="pair",
    )(mine, theirs)
    col_parts = [pieces[0]] + [z_shift(pieces[s], s) for s in range(1, nz)]
    row_parts = pl.pallas_call(
        functools.partial(forward_kernel, step),
        out_shape=[block] * ncol,
        in_specs=[SMEM] * 4 + [VMEM] * 3,
        out_specs=[VMEM] * ncol,
        scratch_shapes=tables(nrow * stretch) + sums(span),
        compiler_params=params(24),
        cost_estimate=cost,
        name="forward",
    )(pos, rows, cols, counts, tiles, near, far)
    others = [vec_shift(x, t) for t in range(1, nvec) for x in [row_x[0]] + row_x[1:]]
    def by_target(xs):
        return [xs[(ncol - t) % ncol] for t in range(ncol)]

    xs = by_target(row_x)
    for t in range(1, nvec):
        xs += by_target(others[(t - 1) * ncol : t * ncol])
    image, share = pl.pallas_call(
        functools.partial(gram_kernel, nz, ncol, nvec),
        out_shape=[block, jax.ShapeDtypeStruct((nvec, vlocal, vlocal), F32)],
        in_specs=[VMEM] * (nz + ncol + nvec * ncol),
        out_specs=[VMEM] * 2,
        compiler_params=params(8),
        name="gram",
    )(*col_parts, *row_parts, *xs)
    for t in range(1, ncol):
        image = image + col_shift(row_parts[t], t)
    share = all_sum(share, nz, ncol)
    order = lax.rem(k + nvec - jnp.arange(nvec), nvec)
    gram = jnp.take(share, order, axis=0).reshape(nvec * vlocal, vlocal)
    gram = gram / math.sqrt(width * nrow * ncol)
    return (image.astype(jnp.bfloat16), gram)


def all_sum(share, nz, ncol):
    if nz * ncol > 8:
        return lax.psum(share, ("row", "col"))
    nrow = 2 * nz
    share = share + lax.ppermute(share, "row", [(a, a ^ 1) for a in range(nrow)])
    shifts = [(s, t) for s in range(nz) for t in range(ncol) if (s, t) != (0, 0)]
    got = None
    core = lax.axis_index("row") % 2
    for n in range(0, len(shifts), 2):
        pair = shifts[n : n + 2]
        perm = []
        for a in range(nrow):
            for b in range(ncol):
                s, t = pair[(a % 2) % len(pair)]
                perm.append((a * ncol + b, (a + 2 * s) % nrow * ncol + (b + t) % ncol))
        part = lax.ppermute(share, ("row", "col"), perm)
        if len(pair) == 1:
            part = jnp.where(core == 0, part, 0.0)
        got = part if got is None else got + part
    if got is None:
        return share
    return share + got + lax.ppermute(got, "row", [(a, a ^ 1) for a in range(nrow)])


def solution(mesh):
    assert mesh.shape["row"] % 2 == 0
    sizes = (mesh.shape["row"] // 2, mesh.shape["col"], mesh.shape["vec"])
    return jax.shard_map(
        functools.partial(shards, sizes),
        mesh=mesh,
        in_specs=(
            P("vec", ("row", "col")),
            P("row", "col", None, None, None),
            P("row", "col", None),
            P("row", "col", None),
            P("row", "col"),
        ),
        out_specs=(P("vec", ("row", "col")), P(None, "vec")),
        check_vma=False,
    )
```

time: 119 us -> 45.6 us (0.38)
  blocking collectives: 55.8 us -> 0 us
  starting transfers between devices: 0.08 us -> 24 us
  waiting for transfers between devices: 27.7 us -> 4.82 us
  matrix products: 13.6 us -> 0 us
  between operations: 14.7 us -> 1.49 us
  local copies, waits for them, and re-layouts: 3.15 us -> 9.66 us
  Pallas kernels: 0 us -> 3.84 us
  other arithmetic: 3.42 us -> 1.34 us
    psum x1 -> x0, blocking collectives: 31 us -> none  [shards(): lax.psum(partial_gram, ('row', 'col')) / math.sqrt(width * nrow * ncol)]
    reduce_scatter x2 -> x0, waiting for transfers between devices: 27.7 us -> none  [the longest x1 27.7 us: shards(): lax.psum_scatter(col_part, 'row', scatter_dimension=1, tiled=True)]
    all_gather x3 -> x0, blocking collectives: 24.8 us -> none  [the longest x1 15.9 us: shards(): col_x = lax.all_gather(vectors, 'row', axis=1, tiled=True)]
    ppermute x0 -> x18, starting transfers between devices: none -> 24 us  [the longest x6 10.5 us: z_shift(): lax.ppermute(x, 'row', [(a, (a + 2 * s) % nrow) for a in range(nrow)])]
    dot_general x5 -> x0, matrix products: 13.6 us -> none  [the longest x1 6.82 us: shards(): jnp.einsum('tij,vtj->vti', tiles, picked_cols, preferred_element_type=jnp...]
    unnamed x6 -> x15, local copies, waits for them, and re-layouts: 1.51 us -> 8.88 us
    ppermute x0 -> x18, waiting for transfers between devices: none -> 4.82 us  [the longest x4 3.07 us: all_sum(): part = lax.ppermute(share, ('row', 'col'), perm)]
    pallas_call x0 -> x4, Pallas kernels: none -> 3.84 us  [the longest x1 1.39 us: shards(): pl.pallas_call(functools.partial(mirror_kernel, step), out_shape=[ring, r...]
  transfers between devices with their start and end apart: 2 -> 18, of which waited for: 1 -> 5; matrix products, arithmetic and copies ran while one was open for 6% -> 4% of each run, Pallas kernels for 0% -> 6%
where the time goes in v1:
time: 45.6 us; the launch traced here: 45.1 us
  starting transfers between devices  24 us (53%)
  local copies, waits for them, and re-layouts  9.66 us (21%)
  waiting for transfers between devices  4.82 us (11%)
  Pallas kernels  3.84 us (8%)
  between operations  1.49 us (3%)
  other arithmetic  1.34 us (3%)
    ppermute x6, starting transfers between devices, z_shift(): lax.ppermute(x, 'row', [(a, (a + 2 * s) % nrow) for a in range(nrow)])  10.5 us
    unnamed x15, local copies, waits for them, and re-layouts  8.88 us
    ppermute x4, starting transfers between devices, all_sum(): part = lax.ppermute(share, ('row', 'col'), perm)  7.26 us
    ppermute x2, starting transfers between devices, col_shift(): return lax.ppermute(x, 'col', [(a, (a + t) % ncol) for a in range(ncol)])  3.53 us
    ppermute x4, waiting for transfers between devices, all_sum(): part = lax.ppermute(share, ('row', 'col'), perm)  3.07 us
    ppermute x2, starting transfers between devices, vec_shift(): return lax.ppermute(x, 'vec', [(a, (a + t) % nvec) for a in range(nvec)])  2.03 us
    pallas_call x1, Pallas kernels, shards(): pl.pallas_call(functools.partial(mirror_kernel, step), out_shape=[ring, r...  1.39 us
    pallas_call x1, Pallas kernels, shards(): pl.pallas_call(functools.partial(forward_kernel, step), out_shape=[block]...  1.34 us
  transfers between devices with their start and end apart: 18, of which 5 were waited for; matrix products, arithmetic and copies ran while one was open for 4% of the time, Pallas kernels for 6%

profile of v1, /device:TPU:0, one launch (start us, length us, event | category | flops | bytes accessed | tf_op | source)
XLA Modules:
  0.0 45.1 jit_solution(288048866911244936)
XLA Ops:
  0.7 3.0 %collective-permute-start = (bf16[8,1024]{1,0:T(8,128)(2,1)}, bf16[8,1024]{1,0:T(8,128)(2,1)S(1)}, u32[]{:S(2)}, u32[]{:S(2)}) collective-permute-start(bf16[8,1024]{1,0:T(8,128)(2,1)} %refs_6_.1), channel_id=1, source_target_pairs={{0,2},{2,0},{1,3},{3,1},{4,6},{6,4},{5,7},{7,5},{8,10},{10,8},{9,1... | collective-permute-start | bytes 49160 | tf_op jit(solution)/shard_map/ppermute | solution.py:182
  3.7 1.6 %collective-permute-start.5 = (bf16[8,1024]{1,0:T(8,128)(2,1)}, bf16[8,1024]{1,0:T(8,128)(2,1)S(1)}, u32[]{:S(2)}, u32[]{:S(2)}) collective-permute-start(bf16[8,1024]{1,0:T(8,128)(2,1)} %refs_6_.1), channel_id=1, source_target_pairs={{0,8},{4,12},{8,16},{12,20},{16,24},{20,28},{24,0},{28,4},{1,9},{5... | collective-permute-start | bytes 49160 | tf_op jit(solution)/shard_map/ppermute | solution.py:179
  5.2 2.6 %collective-permute-start.6 = (bf16[8,1024]{1,0:T(8,128)(2,1)}, bf16[8,1024]{1,0:T(8,128)(2,1)S(1)}, u32[]{:S(2)}, u32[]{:S(2)}) collective-permute-start(bf16[8,1024]{1,0:T(8,128)(2,1)} %refs_6_.1), channel_id=1, source_target_pairs={{0,16},{4,20},{8,24},{12,28},{16,0},{20,4},{24,8},{28,12},{1,17},{... | collective-permute-start | bytes 49160 | tf_op jit(solution)/shard_map/ppermute | solution.py:179
  7.8 1.3 %collective-permute-start.7 = (bf16[8,1024]{1,0:T(8,128)(2,1)}, bf16[8,1024]{1,0:T(8,128)(2,1)S(1)}, u32[]{:S(2)}, u32[]{:S(2)}) collective-permute-start(bf16[8,1024]{1,0:T(8,128)(2,1)} %refs_6_.1), channel_id=1, source_target_pairs={{0,24},{4,28},{8,0},{12,4},{16,8},{20,12},{24,16},{28,20},{1,25},{... | collective-permute-start | bytes 49160 | tf_op jit(solution)/shard_map/ppermute | solution.py:179
  9.2 0.8 %constant_dynamic-update-slice_fusion.3 = bf16[8,4096]{1,0:T(8,128)(2,1)S(1)} fusion(bf16[8,1024]{1,0:T(8,128)(2,1)} %refs_6_.1), kind=kLoop, calls=%fused_computation.5 | loop fusion | bytes 32768
  10.7 3.4 %copy-done = bf16[1,1,256,128,128]{4,3,2,1,0:T(8,128)(2,1)S(1)} copy-done((bf16[1,1,256,128,128]{4,3,2,1,0:T(8,128)(2,1)S(1)}, bf16[1,1,256,128,128]{4,3,2,1,0:T(8,128)(2,1)}, u32[]{:S(2)}) %copy-start) | copy-done | bytes 8388632
  14.1 0.7 %copy-done.2 = s32[1,1,256]{2,1,0:T(1,128)S(1)} copy-done((s32[1,1,256]{2,1,0:T(1,128)S(1)}, s32[1,1,256]{2,1,0:T(1,128)}, u32[]{:S(2)}) %copy-start.2) | copy-done | bytes 1048
  14.7 0.7 %copy-done.4 = s32[1,1,256]{2,1,0:T(1,128)S(1)} copy-done((s32[1,1,256]{2,1,0:T(1,128)S(1)}, s32[1,1,256]{2,1,0:T(1,128)}, u32[]{:S(2)}) %copy-start.4) | copy-done | bytes 1048
  15.4 1.4 %mirror.1 = (f32[8,4096]{1,0:T(8,128)S(1)}, f32[8,4096]{1,0:T(8,128)S(1)}) custom-call(s32[3]{0:T(128)S(1)} %pad_add_fusion.pos, s32[256]{0:T(256)S(1)} %bitcast.14, s32[256]{0:T(256)S(1)} %bitcast.16, s32[1]{0:T(128)} %bitcast.10.counts, bf16[256,128,128]{2,1,0:T(8,128)(2,1)S(1)} %bitcast.12, bf16[8,1024]{1,0:T(8,128)(2,1)} %refs_6_.1, ...), custom_call_target="tpu_custom_call" | custom-call | flops 134217728 | bytes 8388608 | tf_op jit(solution)/shard_map/mirror/pallas_call | solution.py:204
  17.0 0.5 %collective-permute-start.8 = (bf16[8,4096]{1,0:T(8,128)(2,1)S(1)}, bf16[8,4096]{1,0:T(8,128)(2,1)S(1)}, u32[]{:S(2)}, u32[]{:S(2)}) collective-permute-start(bf16[8,4096]{1,0:T(8,128)(2,1)S(1)} %constant_dynamic-update-slice_fusion.near), channel_id=1, source_target_pairs={{0,4},{4,0},{8,12},{12,8},{16,20},{20,16},{24,28},{28,24},{1,5},{5... | collective-permute-start | bytes 196616 | tf_op jit(solution)/shard_map/ppermute | solution.py:176
  17.5 1.5 %collective-permute-start.9 = (bf16[8,1024]{1,0:T(8,128)(2,1)}, bf16[8,1024]{1,0:T(8,128)(2,1)S(1)}, u32[]{:S(2)}, u32[]{:S(2)}) collective-permute-start(bf16[8,1024]{1,0:T(8,128)(2,1)} %refs_6_.1), channel_id=1, source_target_pairs={{0,1},{1,0},{2,3},{3,2},{4,5},{5,4},{6,7},{7,6},{8,9},{9,8},{10,11... | collective-permute-start | bytes 49160 | tf_op jit(solution)/shard_map/ppermute | solution.py:185
  19.0 0.5 %collective-permute-start.10 = (bf16[8,1024]{1,0:T(8,128)(2,1)S(1)}, bf16[8,1024]{1,0:T(8,128)(2,1)S(1)}, u32[]{:S(2)}, u32[]{:S(2)}) collective-permute-start(bf16[8,1024]{1,0:T(8,128)(2,1)S(1)} %collective-permute-done.refs_1_.refs_7_), channel_id=1, source_target_pairs={{0,1},{1,0},{2,3},{3,2},{4,5},{5,4},{6,7},{7,6},{8,9},{9,8},{10,11... | collective-permute-start | bytes 49160 | tf_op jit(solution)/shard_map/ppermute | solution.py:185
  19.5 1.9 %collective-permute-start.2 = (f32[8,1024]{1,0:T(8,128)S(1)}, f32[8,1024]{1,0:T(8,128)S(1)}, u32[]{:S(2)}, u32[]{:S(2)}) collective-permute-start(f32[8,1024]{1,0:T(8,128)S(1)} %get-tuple-element.15), channel_id=1, source_target_pairs={{0,8},{4,12},{8,16},{12,20},{16,24},{20,28},{24,0},{28,4},{1,9},{5... | collective-permute-start | bytes 98312 | tf_op jit(solution)/shard_map/ppermute | solution.py:179
  21.4 0.9 %collective-permute-start.3 = (f32[8,1024]{1,0:T(8,128)S(1)}, f32[8,1024]{1,0:T(8,128)S(1)}, u32[]{:S(2)}, u32[]{:S(2)}) collective-permute-start(f32[8,1024]{1,0:T(8,128)S(1)} %get-tuple-element.16), channel_id=1, source_target_pairs={{0,16},{4,20},{8,24},{12,28},{16,0},{20,4},{24,8},{28,12},{1,17},{... | collective-permute-start | bytes 98312 | tf_op jit(solution)/shard_map/ppermute | solution.py:179
  22.3 2.2 %collective-permute-start.4 = (f32[8,1024]{1,0:T(8,128)S(1)}, f32[8,1024]{1,0:T(8,128)S(1)}, u32[]{:S(2)}, u32[]{:S(2)}) collective-permute-start(f32[8,1024]{1,0:T(8,128)S(1)} %get-tuple-element.17), channel_id=1, source_target_pairs={{0,24},{4,28},{8,0},{12,4},{16,8},{20,12},{24,16},{28,20},{1,25},{... | collective-permute-start | bytes 98312 | tf_op jit(solution)/shard_map/ppermute | solution.py:179
  24.6 3.4 %copy-done.1 = bf16[1,1,256,128,128]{4,3,2,1,0:T(8,128)(2,1)S(1)} copy-done((bf16[1,1,256,128,128]{4,3,2,1,0:T(8,128)(2,1)S(1)}, bf16[1,1,256,128,128]{4,3,2,1,0:T(8,128)(2,1)}, u32[]{:S(2)}) %copy-start.1) | copy-done | bytes 8388632
  28.0 1.3 %forward.1 = (f32[8,1024]{1,0:T(8,128)S(1)}, f32[8,1024]{1,0:T(8,128)S(1)}) custom-call(s32[3]{0:T(128)S(1)} %pad_add_fusion.pos, s32[256]{0:T(256)S(1)} %bitcast.15, s32[256]{0:T(256)S(1)} %bitcast.17, s32[1]{0:T(128)} %bitcast.11.counts, bf16[256,128,128]{2,1,0:T(8,128)(2,1)S(1)} %bitcast.13, bf16[8,4096]{1,0:T(8,128)(2,1)S(1)} %constant_dynamic-update-slice_fusion.near, ...), custom_call_target="tpu_custom_call" | custom-call | flops 134217728 | bytes 8388608 | tf_op jit(solution)/shard_map/forward/pallas_call | solution.py:224
  29.4 1.1 %gram.1 = (f32[8,1024]{1,0:T(8,128)S(1)}, f32[2,8,8]{2,1,0:T(8,128)S(1)}) custom-call(f32[8,1024]{1,0:T(8,128)S(1)} %get-tuple-element.14.refs_0_, f32[8,1024]{1,0:T(8,128)S(1)} %collective-permute-done.2.refs_1_, f32[8,1024]{1,0:T(8,128)S(1)} %collective-permute-done.3.refs_2_, f32[8,1024]{1,0:T(8,128)S(1)} %collective-permute-done.4.refs_3_, ...), custom_call_target="tpu_custom_call" | custom-call | tf_op jit(solution)/shard_map/gram/pallas_call | solution.py:241
  30.5 1.2 %collective-permute-done.12 = f32[2,8,8]{2,1,0:T(8,128)S(1)} collective-permute-done((f32[2,8,8]{2,1,0:T(8,128)S(1)}, f32[2,8,8]{2,1,0:T(8,128)S(1)}, u32[]{:S(2)}, u32[]{:S(2)}) %collective-permute-start.12) | collective-permute-done | bytes 544 | tf_op jit(solution)/shard_map/ppermute | solution.py:262
  31.7 2.6 %collective-permute-start.16 = (f32[2,8,8]{2,1,0:T(8,128)S(1)}, f32[2,8,8]{2,1,0:T(8,128)S(1)}, u32[]{:S(2)}, u32[]{:S(2)}) collective-permute-start(f32[2,8,8]{2,1,0:T(8,128)S(1)} %add.49), channel_id=1, source_target_pairs={{0,26},{2,24},{4,30},{6,28},{8,2},{10,0},{12,6},{14,4},{16,10},{18... | collective-permute-start | bytes 1544 | tf_op jit(solution)/shard_map/ppermute | solution.py:273
  34.3 0.8 %collective-permute-start.15 = (f32[2,8,8]{2,1,0:T(8,128)S(1)}, f32[2,8,8]{2,1,0:T(8,128)S(1)}, u32[]{:S(2)}, u32[]{:S(2)}) collective-permute-start(f32[2,8,8]{2,1,0:T(8,128)S(1)} %add.49), channel_id=1, source_target_pairs={{0,18},{2,16},{4,28},{6,30},{8,26},{10,24},{12,4},{14,6},{16,2},{1... | collective-permute-start | bytes 1544 | tf_op jit(solution)/shard_map/ppermute | solution.py:273
  35.1 1.2 %collective-permute-start.13 = (f32[2,8,8]{2,1,0:T(8,128)S(1)}, f32[2,8,8]{2,1,0:T(8,128)S(1)}, u32[]{:S(2)}, u32[]{:S(2)}) collective-permute-start(f32[2,8,8]{2,1,0:T(8,128)S(1)} %add.49), channel_id=1, source_target_pairs={{0,2},{2,0},{4,12},{6,14},{8,10},{10,8},{12,20},{14,22},{16,18},{1... | collective-permute-start | bytes 1544 | tf_op jit(solution)/shard_map/ppermute | solution.py:273
  36.4 2.6 %collective-permute-start.14 = (f32[2,8,8]{2,1,0:T(8,128)S(1)}, f32[2,8,8]{2,1,0:T(8,128)S(1)}, u32[]{:S(2)}, u32[]{:S(2)}) collective-permute-start(f32[2,8,8]{2,1,0:T(8,128)S(1)} %add.49), channel_id=1, source_target_pairs={{0,10},{2,8},{4,20},{6,22},{8,18},{10,16},{12,28},{14,30},{16,26},... | collective-permute-start | bytes 1544 | tf_op jit(solution)/shard_map/ppermute | solution.py:273
  39.0 0.1 broadcast_in_dim.19
  39.1 0.5 %collective-permute-start.11 = (f32[8,1024]{1,0:T(8,128)S(1)}, f32[8,1024]{1,0:T(8,128)S(1)}, u32[]{:S(2)}, u32[]{:S(2)}) collective-permute-start(f32[8,1024]{1,0:T(8,128)S(1)} %get-tuple-element.19.refs_5_), channel_id=1, source_target_pairs={{0,2},{2,0},{1,3},{3,1},{4,6},{6,4},{5,7},{7,5},{8,10},{10,8},{9,1... | collective-permute-start | bytes 98312 | tf_op jit(solution)/shard_map/ppermute | solution.py:182
  39.6 0.1 collective-permute-done.15
  39.7 3.0 %collective-permute-done.14 = f32[2,8,8]{2,1,0:T(8,128)S(1)} collective-permute-done((f32[2,8,8]{2,1,0:T(8,128)S(1)}, f32[2,8,8]{2,1,0:T(8,128)S(1)}, u32[]{:S(2)}, u32[]{:S(2)}) %collective-permute-start.14) | collective-permute-done | bytes 544 | tf_op jit(solution)/shard_map/ppermute | solution.py:273
  42.7 0.3 collective-permute-done.11
  43.1 0.6 %add_convert_fusion = bf16[8,1024]{1,0:T(8,128)(2,1)} fusion(f32[8,1024]{1,0:T(8,128)S(1)} %get-tuple-element.20, f32[8,1024]{1,0:T(8,128)S(1)} %collective-permute-done.11), kind=kLoop, calls=%fused_computation.1 | loop fusion | flops 16384 | bytes 81920 | tf_op jit(solution)/shard_map/convert_element_type | solution.py:255
  43.7 0.2 collective-permute-done.17
  43.9 0.5 %gather_fusion = f32[2,8,8]{2,1,0:T(8,128)S(1)} fusion(f32[2,8,8]{2,1,0:T(8,128)S(1)} %add_add_fusion, s32[1024]{0:T(1024)S(1)} %pad_clamp_fusion), kind=kCustom, calls=%fused_computation | custom fusion | bytes 1032 | tf_op jit(solution)/shard_map/jit(_take)/gather | solution.py:253
  44.5 0.6 %select_multiply_fusion = f32[16,8]{0,1:T(8,128)} fusion(f32[16,8]{0,1:T(8,128)S(1)} %copy.8, pred[16]{0:T(512)(128)(4,1)S(1)} %broadcast_in_dim.19), kind=kLoop, calls=%fused_computation.9 | loop fusion | flops 256 | bytes 1040 | tf_op jit(solution)/shard_map/div | solution.py:254
  (37 shorter events, 0.4 us)
Async XLA Ops:
  0.6 24.0 %copy-start.3 = (s32[1,1,256]{2,1,0:T(1,128)S(1)}, s32[1,1,256]{2,1,0:T(1,128)}, u32[]{:S(2)}) copy-start(s32[1,1,256]{2,1,0:T(1,128)} %param.7) | copy-start | bytes 3076
  0.6 24.0 %copy-start.5 = (s32[1,1,256]{2,1,0:T(1,128)S(1)}, s32[1,1,256]{2,1,0:T(1,128)}, u32[]{:S(2)}) copy-start(s32[1,1,256]{2,1,0:T(1,128)} %param.8) | copy-start | bytes 3076
  0.7 10.0 %collective-permute-start = (bf16[8,1024]{1,0:T(8,128)(2,1)}, bf16[8,1024]{1,0:T(8,128)(2,1)S(1)}, u32[]{:S(2)}, u32[]{:S(2)}) collective-permute-start(bf16[8,1024]{1,0:T(8,128)(2,1)} %refs_6_.1), channel_id=1, source_target_pairs={{0,2},{2,0},{1,3},{3,1},{4,6},{6,4},{5,7},{7,5},{8,10},{10,8},{9,1... | collective-permute-start | bytes 49160 | tf_op jit(solution)/shard_map/ppermute | solution.py:182
  3.7 13.2 %collective-permute-start.5 = (bf16[8,1024]{1,0:T(8,128)(2,1)}, bf16[8,1024]{1,0:T(8,128)(2,1)S(1)}, u32[]{:S(2)}, u32[]{:S(2)}) collective-permute-start(bf16[8,1024]{1,0:T(8,128)(2,1)} %refs_6_.1), channel_id=1, source_target_pairs={{0,8},{4,12},{8,16},{12,20},{16,24},{20,28},{24,0},{28,4},{1,9},{5... | collective-permute-start | bytes 49160 | tf_op jit(solution)/shard_map/ppermute | solution.py:179
  5.2 11.7 %collective-permute-start.6 = (bf16[8,1024]{1,0:T(8,128)(2,1)}, bf16[8,1024]{1,0:T(8,128)(2,1)S(1)}, u32[]{:S(2)}, u32[]{:S(2)}) collective-permute-start(bf16[8,1024]{1,0:T(8,128)(2,1)} %refs_6_.1), channel_id=1, source_target_pairs={{0,16},{4,20},{8,24},{12,28},{16,0},{20,4},{24,8},{28,12},{1,17},{... | collective-permute-start | bytes 49160 | tf_op jit(solution)/shard_map/ppermute | solution.py:179
  7.8 9.1 %collective-permute-start.7 = (bf16[8,1024]{1,0:T(8,128)(2,1)}, bf16[8,1024]{1,0:T(8,128)(2,1)S(1)}, u32[]{:S(2)}, u32[]{:S(2)}) collective-permute-start(bf16[8,1024]{1,0:T(8,128)(2,1)} %refs_6_.1), channel_id=1, source_target_pairs={{0,24},{4,28},{8,0},{12,4},{16,8},{20,12},{24,16},{28,20},{1,25},{... | collective-permute-start | bytes 49160 | tf_op jit(solution)/shard_map/ppermute | solution.py:179
  10.7 3.4 %copy-start = (bf16[1,1,256,128,128]{4,3,2,1,0:T(8,128)(2,1)S(1)}, bf16[1,1,256,128,128]{4,3,2,1,0:T(8,128)(2,1)}, u32[]{:S(2)}) copy-start(bf16[1,1,256,128,128]{4,3,2,1,0:T(8,128)(2,1)} %param.6) | copy-start | bytes 25165828
  14.0 0.7 %copy-start.2 = (s32[1,1,256]{2,1,0:T(1,128)S(1)}, s32[1,1,256]{2,1,0:T(1,128)}, u32[]{:S(2)}) copy-start(s32[1,1,256]{2,1,0:T(1,128)} %param.7) | copy-start | bytes 3076
  14.7 0.7 %copy-start.4 = (s32[1,1,256]{2,1,0:T(1,128)S(1)}, s32[1,1,256]{2,1,0:T(1,128)}, u32[]{:S(2)}) copy-start(s32[1,1,256]{2,1,0:T(1,128)} %param.8) | copy-start | bytes 3076
  16.8 2.7 %collective-permute-start.1 = (f32[8,4096]{1,0:T(8,128)S(1)}, f32[8,4096]{1,0:T(8,128)S(1)}, u32[]{:S(2)}, u32[]{:S(2)}) collective-permute-start(f32[8,4096]{1,0:T(8,128)S(1)} %get-tuple-element.13), channel_id=1, source_target_pairs={{0,4},{4,0},{8,12},{12,8},{16,20},{20,16},{24,28},{28,24},{1,5},{5... | collective-permute-start | bytes 393224 | tf_op jit(solution)/shard_map/ppermute | solution.py:176
  17.0 5.4 %collective-permute-start.8 = (bf16[8,4096]{1,0:T(8,128)(2,1)S(1)}, bf16[8,4096]{1,0:T(8,128)(2,1)S(1)}, u32[]{:S(2)}, u32[]{:S(2)}) collective-permute-start(bf16[8,4096]{1,0:T(8,128)(2,1)S(1)} %constant_dynamic-update-slice_fusion.near), channel_id=1, source_target_pairs={{0,4},{4,0},{8,12},{12,8},{16,20},{20,16},{24,28},{28,24},{1,5},{5... | collective-permute-start | bytes 196616 | tf_op jit(solution)/shard_map/ppermute | solution.py:176
  17.5 11.8 %collective-permute-start.9 = (bf16[8,1024]{1,0:T(8,128)(2,1)}, bf16[8,1024]{1,0:T(8,128)(2,1)S(1)}, u32[]{:S(2)}, u32[]{:S(2)}) collective-permute-start(bf16[8,1024]{1,0:T(8,128)(2,1)} %refs_6_.1), channel_id=1, source_target_pairs={{0,1},{1,0},{2,3},{3,2},{4,5},{5,4},{6,7},{7,6},{8,9},{9,8},{10,11... | collective-permute-start | bytes 49160 | tf_op jit(solution)/shard_map/ppermute | solution.py:185
  19.0 10.3 %collective-permute-start.10 = (bf16[8,1024]{1,0:T(8,128)(2,1)S(1)}, bf16[8,1024]{1,0:T(8,128)(2,1)S(1)}, u32[]{:S(2)}, u32[]{:S(2)}) collective-permute-start(bf16[8,1024]{1,0:T(8,128)(2,1)S(1)} %collective-permute-done.refs_1_.refs_7_), channel_id=1, source_target_pairs={{0,1},{1,0},{2,3},{3,2},{4,5},{5,4},{6,7},{7,6},{8,9},{9,8},{10,11... | collective-permute-start | bytes 49160 | tf_op jit(solution)/shard_map/ppermute | solution.py:185
  19.5 9.8 %collective-permute-start.2 = (f32[8,1024]{1,0:T(8,128)S(1)}, f32[8,1024]{1,0:T(8,128)S(1)}, u32[]{:S(2)}, u32[]{:S(2)}) collective-permute-start(f32[8,1024]{1,0:T(8,128)S(1)} %get-tuple-element.15), channel_id=1, source_target_pairs={{0,8},{4,12},{8,16},{12,20},{16,24},{20,28},{24,0},{28,4},{1,9},{5... | collective-permute-start | bytes 98312 | tf_op jit(solution)/shard_map/ppermute | solution.py:179
  21.4 7.9 %collective-permute-start.3 = (f32[8,1024]{1,0:T(8,128)S(1)}, f32[8,1024]{1,0:T(8,128)S(1)}, u32[]{:S(2)}, u32[]{:S(2)}) collective-permute-start(f32[8,1024]{1,0:T(8,128)S(1)} %get-tuple-element.16), channel_id=1, source_target_pairs={{0,16},{4,20},{8,24},{12,28},{16,0},{20,4},{24,8},{28,12},{1,17},{... | collective-permute-start | bytes 98312 | tf_op jit(solution)/shard_map/ppermute | solution.py:179
  22.3 7.0 %collective-permute-start.4 = (f32[8,1024]{1,0:T(8,128)S(1)}, f32[8,1024]{1,0:T(8,128)S(1)}, u32[]{:S(2)}, u32[]{:S(2)}) collective-permute-start(f32[8,1024]{1,0:T(8,128)S(1)} %get-tuple-element.17), channel_id=1, source_target_pairs={{0,24},{4,28},{8,0},{12,4},{16,8},{20,12},{24,16},{28,20},{1,25},{... | collective-permute-start | bytes 98312 | tf_op jit(solution)/shard_map/ppermute | solution.py:179
  24.6 3.4 %copy-start.1 = (bf16[1,1,256,128,128]{4,3,2,1,0:T(8,128)(2,1)S(1)}, bf16[1,1,256,128,128]{4,3,2,1,0:T(8,128)(2,1)}, u32[]{:S(2)}) copy-start(bf16[1,1,256,128,128]{4,3,2,1,0:T(8,128)(2,1)} %param.6) | copy-start | bytes 25165828
  30.5 1.2 %collective-permute-start.12 = (f32[2,8,8]{2,1,0:T(8,128)S(1)}, f32[2,8,8]{2,1,0:T(8,128)S(1)}, u32[]{:S(2)}, u32[]{:S(2)}) collective-permute-start(f32[2,8,8]{2,1,0:T(8,128)S(1)} %get-tuple-element.21), channel_id=1, source_target_pairs={{0,4},{4,0},{8,12},{12,8},{16,20},{20,16},{24,28},{28,24},{1,5},{5... | collective-permute-start | bytes 1544 | tf_op jit(solution)/shard_map/ppermute | solution.py:262
  31.7 8.0 %collective-permute-start.16 = (f32[2,8,8]{2,1,0:T(8,128)S(1)}, f32[2,8,8]{2,1,0:T(8,128)S(1)}, u32[]{:S(2)}, u32[]{:S(2)}) collective-permute-start(f32[2,8,8]{2,1,0:T(8,128)S(1)} %add.49), channel_id=1, source_target_pairs={{0,26},{2,24},{4,30},{6,28},{8,2},{10,0},{12,6},{14,4},{16,10},{18... | collective-permute-start | bytes 1544 | tf_op jit(solution)/shard_map/ppermute | solution.py:273
  34.3 5.4 %collective-permute-start.15 = (f32[2,8,8]{2,1,0:T(8,128)S(1)}, f32[2,8,8]{2,1,0:T(8,128)S(1)}, u32[]{:S(2)}, u32[]{:S(2)}) collective-permute-start(f32[2,8,8]{2,1,0:T(8,128)S(1)} %add.49), channel_id=1, source_target_pairs={{0,18},{2,16},{4,28},{6,30},{8,26},{10,24},{12,4},{14,6},{16,2},{1... | collective-permute-start | bytes 1544 | tf_op jit(solution)/shard_map/ppermute | solution.py:273
  35.1 4.6 %collective-permute-start.13 = (f32[2,8,8]{2,1,0:T(8,128)S(1)}, f32[2,8,8]{2,1,0:T(8,128)S(1)}, u32[]{:S(2)}, u32[]{:S(2)}) collective-permute-start(f32[2,8,8]{2,1,0:T(8,128)S(1)} %add.49), channel_id=1, source_target_pairs={{0,2},{2,0},{4,12},{6,14},{8,10},{10,8},{12,20},{14,22},{16,18},{1... | collective-permute-start | bytes 1544 | tf_op jit(solution)/shard_map/ppermute | solution.py:273
  36.4 6.3 %collective-permute-start.14 = (f32[2,8,8]{2,1,0:T(8,128)S(1)}, f32[2,8,8]{2,1,0:T(8,128)S(1)}, u32[]{:S(2)}, u32[]{:S(2)}) collective-permute-start(f32[2,8,8]{2,1,0:T(8,128)S(1)} %add.49), channel_id=1, source_target_pairs={{0,10},{2,8},{4,20},{6,22},{8,18},{10,16},{12,28},{14,30},{16,26},... | collective-permute-start | bytes 1544 | tf_op jit(solution)/shard_map/ppermute | solution.py:273
  39.1 4.0 %collective-permute-start.11 = (f32[8,1024]{1,0:T(8,128)S(1)}, f32[8,1024]{1,0:T(8,128)S(1)}, u32[]{:S(2)}, u32[]{:S(2)}) collective-permute-start(f32[8,1024]{1,0:T(8,128)S(1)} %get-tuple-element.19.refs_5_), channel_id=1, source_target_pairs={{0,2},{2,0},{1,3},{3,1},{4,6},{6,4},{5,7},{7,5},{8,10},{10,8},{9,1... | collective-permute-start | bytes 98312 | tf_op jit(solution)/shard_map/ppermute | solution.py:182
  42.7 1.2 %collective-permute-start.17 = (f32[2,8,8]{2,1,0:T(8,128)S(1)}, f32[2,8,8]{2,1,0:T(8,128)S(1)}, u32[]{:S(2)}, u32[]{:S(2)}) collective-permute-start(f32[2,8,8]{2,1,0:T(8,128)S(1)} %select_add_fusion), channel_id=1, source_target_pairs={{0,4},{4,0},{8,12},{12,8},{16,20},{20,16},{24,28},{28,24},{1,5},{5... | collective-permute-start | bytes 1544 | tf_op jit(solution)/shard_map/ppermute | solution.py:279

commit v2 on v1

--- a/solution.py
+++ b/solution.py
@@ -8,10 +8,12 @@
 from jax.experimental.pallas import tpu as pltpu
 from jax.sharding import PartitionSpec as P
 
-CHUNK = 64
+CHUNK = 32
+AHEAD = 2
 GROUP = 8
 SMEM = pl.BlockSpec(memory_space=pltpu.SMEM)
 VMEM = pl.BlockSpec(memory_space=pltpu.VMEM)
+HBM = pl.BlockSpec(memory_space=pltpu.HBM)
 F32 = jnp.float32
 HIGHEST = lax.Precision.HIGHEST
 
@@ -29,7 +31,7 @@
         high[first + q] = jnp.concatenate([zero, part], axis=0)
 
 
-def multiply_tiles(pick, forward, count, tiles, low, high, sums):
+def multiply_tiles(pick, forward, count, tiles, low, high, sums, arrive=None):
     slots = tiles.shape[0]
     tile = tiles.shape[-1]
     vlocal = sums[0].shape[1]
@@ -37,6 +39,8 @@
         acc[...] = jnp.zeros_like(acc)
 
     def chunk(step, carry):
+        if arrive is not None:
+            arrive(step)
         for g in range(CHUNK // (2 * GROUP)):
             results = []
             for u in range(GROUP):
@@ -70,14 +74,42 @@
     return get
 
 
-def mirror_kernel(sizes, pos, rows, cols, counts, tiles, *refs):
+def position():
+    i = lax.axis_index("row")
+    return lax.div(i, 2), lax.rem(i, 2), lax.axis_index("col")
+
+
+def start_lists(lists, held, sems):
+    copies = [pltpu.make_async_copy(a, b, sems.at[n]) for n, (a, b) in enumerate(zip(lists, held))]
+    for copy in copies:
+        copy.start()
+    return copies
+
+
+def mirror_kernel(sizes, counts, rows_hbm, cols_hbm, tiles_hbm, *refs):
     nz, ncol, stretch = sizes
     span = ncol * stretch
-    blocks, (mine, other), (low, high, *sums) = refs[:ncol], refs[ncol : ncol + 2], refs[ncol + 2 :]
+    blocks, (mine, other, tiles), refs = refs[:ncol], refs[ncol : ncol + 3], refs[ncol + 3 :]
+    rows, cols, list_sems, tile_sems, low, high, *sums = refs
+    slots = tiles.shape[0]
     tile = tiles.shape[-1]
     width = stretch * tile
+    copies = start_lists((rows_hbm, cols_hbm), (rows, cols), list_sems)
     count = counts[0]
-    z, core, j = pos[0], pos[1], pos[2]
+    chunks = pl.cdiv(count, CHUNK)
+
+    def load(step):
+        at = pl.ds(step * CHUNK, CHUNK)
+        return pltpu.make_async_copy(tiles_hbm.at[at], tiles.at[at], tile_sems.at[step])
+
+    def start(step):
+        @pl.when(step < chunks)
+        def _():
+            load(step).start()
+
+    for step in range(AHEAD):
+        start(step)
+    z, core, j = position()
     for t in range(ncol):
         place_block(low, high, blocks[t], lax.rem(j + ncol - t, ncol) * stretch, stretch, tile)
     low[span] = jnp.zeros(low.shape[1:], low.dtype)
@@ -88,7 +120,13 @@
         r, c, row_place, col_place = get(s)
         return jnp.where((s < count) & (r != c), row_place, span), col_place
 
-    multiply_tiles(pick, False, count, tiles, low, high, sums)
+    def arrive(step):
+        load(step).wait()
+        start(step + AHEAD)
+
+    for copy in copies:
+        copy.wait()
+    multiply_tiles(pick, False, count, tiles, low, high, sums, arrive)
     for s in range(nz):
         target = 2 * lax.rem(z + s, nz)
         for out, c in ((mine, core), (other, 1 - core)):
@@ -100,14 +138,15 @@
                 out[:, s * width + q * tile : s * width + (q + 1) * tile] = total
 
 
-def forward_kernel(sizes, pos, rows, cols, counts, tiles, near, far, *refs):
+def forward_kernel(sizes, counts, rows_hbm, cols_hbm, tiles, near, far, *refs):
     nz, ncol, stretch = sizes
     span = ncol * stretch
-    outs, (low, high, *sums) = refs[:ncol], refs[ncol:]
+    outs, (rows, cols, list_sems, low, high, *sums) = refs[:ncol], refs[ncol:]
     tile = tiles.shape[-1]
     width = stretch * tile
+    copies = start_lists((rows_hbm, cols_hbm), (rows, cols), list_sems)
     count = counts[0]
-    z, core, j = pos[0], pos[1], pos[2]
+    z, core, j = position()
     for s in range(nz):
         source = 2 * lax.rem(z + nz - s, nz)
         for ref, c in ((near, core), (far, 1 - core)):
@@ -121,6 +160,8 @@
         _, _, row_place, col_place = get(s)
         return jnp.where(s < count, col_place, dead), row_place
 
+    for copy in copies:
+        copy.wait()
     multiply_tiles(pick, True, count, tiles, low, high, sums)
     for t in range(ncol):
         first = lax.rem(j + t, ncol) * stretch
@@ -138,7 +179,7 @@
         outs[s][...] = mine[:, at] + theirs[:, at]
 
 
-def gram_kernel(nz, ncol, nvec, *refs):
+def gram_kernel(nz, ncol, nvec, scale, *refs):
     cols, refs = refs[:nz], refs[nz:]
     parts, refs = refs[:ncol], refs[ncol:]
     xs, (image, share) = refs[: nvec * ncol], refs[nvec * ncol :]
@@ -158,7 +199,7 @@
                 preferred_element_type=F32,
             )
             product = one if product is None else product + one
-        share[k] = product
+        share[lax.rem(lax.axis_index("vec") + nvec - k, nvec)] = product * scale
 
 
 def shards(sizes, vectors, tile_vals, tile_rows, tile_cols, tile_counts):
@@ -169,8 +210,6 @@
     stretch = width // tile
     span = ncol * stretch
     tiles, rows, cols, counts = tile_vals[0, 0], tile_rows[0, 0], tile_cols[0, 0], tile_counts[0]
-    i, j, k = lax.axis_index("row"), lax.axis_index("col"), lax.axis_index("vec")
-    pos = jnp.stack([i // 2, i % 2, j]).astype(jnp.int32)
 
     def core_swap(x):
         return lax.ppermute(x, "row", [(a, a ^ 1) for a in range(nrow)])
@@ -201,16 +240,20 @@
     cost = pl.CostEstimate(
         flops=2 * slots * tile * tile * 2 * vlocal, bytes_accessed=slots * tile * tile * 2, transcendentals=0
     )
-    mine, other = pl.pallas_call(
+    lists = [pltpu.SMEM((slots,), jnp.int32)] * 2 + [pltpu.SemaphoreType.DMA((2,))]
+    mine, other, held = pl.pallas_call(
         functools.partial(mirror_kernel, step),
-        out_shape=[ring, ring],
-        in_specs=[SMEM] * 4 + [VMEM] * (1 + ncol),
-        out_specs=[VMEM] * 2,
-        scratch_shapes=tables(span) + sums(nrow * stretch),
+        out_shape=[ring, ring, jax.ShapeDtypeStruct(tiles.shape, tiles.dtype)],
+        in_specs=[SMEM] + [HBM] * 3 + [VMEM] * ncol,
+        out_specs=[VMEM] * 3,
+        scratch_shapes=lists
+        + [pltpu.SemaphoreType.DMA((slots // CHUNK,))]
+        + tables(span)
+        + sums(nrow * stretch),
         compiler_params=params(24),
         cost_estimate=cost,
         name="mirror",
-    )(pos, rows, cols, counts, tiles, *row_x)
+    )(counts, rows, cols, tiles, *row_x)
     theirs = core_swap(other)
     pieces = pl.pallas_call(
         functools.partial(pair_kernel, nz),
@@ -224,13 +267,13 @@
     row_parts = pl.pallas_call(
         functools.partial(forward_kernel, step),
         out_shape=[block] * ncol,
-        in_specs=[SMEM] * 4 + [VMEM] * 3,
+        in_specs=[SMEM] + [HBM] * 2 + [VMEM] * 3,
         out_specs=[VMEM] * ncol,
-        scratch_shapes=tables(nrow * stretch) + sums(span),
+        scratch_shapes=lists + tables(nrow * stretch) + sums(span),
         compiler_params=params(24),
         cost_estimate=cost,
         name="forward",
-    )(pos, rows, cols, counts, tiles, near, far)
+    )(counts, rows, cols, held, near, far)
     others = [vec_shift(x, t) for t in range(1, nvec) for x in [row_x[0]] + row_x[1:]]
     def by_target(xs):
         return [xs[(ncol - t) % ncol] for t in range(ncol)]
@@ -239,7 +282,7 @@
     for t in range(1, nvec):
         xs += by_target(others[(t - 1) * ncol : t * ncol])
     image, share = pl.pallas_call(
-        functools.partial(gram_kernel, nz, ncol, nvec),
+        functools.partial(gram_kernel, nz, ncol, nvec, 1.0 / math.sqrt(width * nrow * ncol)),
         out_shape=[block, jax.ShapeDtypeStruct((nvec, vlocal, vlocal), F32)],
         in_specs=[VMEM] * (nz + ncol + nvec * ncol),
         out_specs=[VMEM] * 2,
@@ -249,18 +292,16 @@
     for t in range(1, ncol):
         image = image + col_shift(row_parts[t], t)
     share = all_sum(share, nz, ncol)
-    order = lax.rem(k + nvec - jnp.arange(nvec), nvec)
-    gram = jnp.take(share, order, axis=0).reshape(nvec * vlocal, vlocal)
-    gram = gram / math.sqrt(width * nrow * ncol)
+    gram = share.reshape(nvec * vlocal, vlocal)
     return (image.astype(jnp.bfloat16), gram)
 
 
 def all_sum(share, nz, ncol):
-    if nz * ncol > 8:
+    if nz * ncol > 8 or nz & (nz - 1):
         return lax.psum(share, ("row", "col"))
     nrow = 2 * nz
     share = share + lax.ppermute(share, "row", [(a, a ^ 1) for a in range(nrow)])
-    shifts = [(s, t) for s in range(nz) for t in range(ncol) if (s, t) != (0, 0)]
+    shifts = sorted(((s, t) for s in range(nz) for t in range(ncol)), key=sum)[1:]
     got = None
     core = lax.axis_index("row") % 2
     for n in range(0, len(shifts), 2):
@@ -269,7 +310,7 @@
         for a in range(nrow):
             for b in range(ncol):
                 s, t = pair[(a % 2) % len(pair)]
-                perm.append((a * ncol + b, (a + 2 * s) % nrow * ncol + (b + t) % ncol))
+                perm.append((a * ncol + b, (a ^ (2 * s)) * ncol + (b + t) % ncol))
         part = lax.ppermute(share, ("row", "col"), perm)
         if len(pair) == 1:
             part = jnp.where(core == 0, part, 0.0)

time: 45.6 us -> 50 us (1.096)
  local copies, waits for them, and re-layouts: 9.66 us -> 12.8 us
  waiting for transfers between devices: 4.82 us -> 6.35 us
  other arithmetic: 1.34 us -> 0.62 us
  Pallas kernels: 3.84 us -> 4.5 us
    unnamed x15 -> x17, local copies, waits for them, and re-layouts: 8.88 us -> 12.2 us
    ppermute x4, waiting for transfers between devices: 3.07 us -> 3.87 us  [all_sum(): part = lax.ppermute(share, ('row', 'col'), perm)]
    ppermute x2, waiting for transfers between devices: 0.01 us -> 0.73 us  [core_swap(): return lax.ppermute(x, 'row', [(a, a ^ 1) for a in range(nrow)])]
    reshape x0 -> x1, local copies, waits for them, and re-layouts: none -> 0.66 us  [shards(): gram = share.reshape(nvec * vlocal, vlocal)]
    gather x2 -> x0, local copies, waits for them, and re-layouts: 0.62 us -> none  [shards(): gram = jnp.take(share, order, axis=0).reshape(nvec * vlocal, vlocal)]
    pallas_call x1, Pallas kernels: 1.39 us -> 2 us  [shards(): pl.pallas_call(functools.partial(mirror_kernel, step), out_shape=[ring, r...]
    div x1 -> x0, other arithmetic: 0.6 us -> none  [shards(): gram = gram / math.sqrt(width * nrow * ncol)]
    ppermute x4, starting transfers between devices: 7.26 us -> 6.75 us  [all_sum(): part = lax.ppermute(share, ('row', 'col'), perm)]
  transfers between devices with their start and end apart: 18 -> 18, of which waited for: 5 -> 5; matrix products, arithmetic and copies ran while one was open for 4% -> 3% of each run, Pallas kernels for 6% -> 7%
where the time goes in v2:
time: 50 us; the launch traced here: 49.5 us
  starting transfers between devices  23.8 us (48%)
  local copies, waits for them, and re-layouts  12.8 us (26%)
  waiting for transfers between devices  6.35 us (13%)
  Pallas kernels  4.5 us (9%)
  between operations  1.45 us (3%)
  other arithmetic  0.62 us (1%)
    unnamed x17, local copies, waits for them, and re-layouts  12.2 us
    ppermute x6, starting transfers between devices, z_shift(): lax.ppermute(x, 'row', [(a, (a + 2 * s) % nrow) for a in range(nrow)])  10.9 us
    ppermute x4, starting transfers between devices, all_sum(): part = lax.ppermute(share, ('row', 'col'), perm)  6.75 us
    ppermute x4, waiting for transfers between devices, all_sum(): part = lax.ppermute(share, ('row', 'col'), perm)  3.87 us
    ppermute x2, starting transfers between devices, col_shift(): return lax.ppermute(x, 'col', [(a, (a + t) % ncol) for a in range(ncol)])  3.49 us
    ppermute x2, starting transfers between devices, vec_shift(): return lax.ppermute(x, 'vec', [(a, (a + t) % nvec) for a in range(nvec)])  2.03 us
    pallas_call x1, Pallas kernels, shards(): pl.pallas_call(functools.partial(mirror_kernel, step), out_shape=[ring, r...  2 us
    pallas_call x1, Pallas kernels, shards(): pl.pallas_call(functools.partial(forward_kernel, step), out_shape=[block]...  1.4 us
  transfers between devices with their start and end apart: 18, of which 5 were waited for; matrix products, arithmetic and copies ran while one was open for 3% of the time, Pallas kernels for 7%

profile of v2, /device:TPU:0, one launch (start us, length us, event | category | flops | bytes accessed | tf_op | source)
XLA Modules:
  0.0 49.5 jit_solution(9152949939552402561)
XLA Ops:
  0.6 0.0 copy-start.4
  0.6 0.0 copy-start.6
  0.7 3.0 %collective-permute-start = (bf16[8,1024]{1,0:T(8,128)(2,1)}, bf16[8,1024]{1,0:T(8,128)(2,1)S(1)}, u32[]{:S(2)}, u32[]{:S(2)}) collective-permute-start(bf16[8,1024]{1,0:T(8,128)(2,1)} %refs_6_.1), channel_id=1, source_target_pairs={{0,2},{2,0},{1,3},{3,1},{4,6},{6,4},{5,7},{7,5},{8,10},{10,8},{9,1... | collective-permute-start | bytes 49160 | tf_op jit(solution)/shard_map/ppermute | solution.py:221
  3.7 1.6 %collective-permute-start.5 = (bf16[8,1024]{1,0:T(8,128)(2,1)}, bf16[8,1024]{1,0:T(8,128)(2,1)S(1)}, u32[]{:S(2)}, u32[]{:S(2)}) collective-permute-start(bf16[8,1024]{1,0:T(8,128)(2,1)} %refs_6_.1), channel_id=1, source_target_pairs={{0,8},{4,12},{8,16},{12,20},{16,24},{20,28},{24,0},{28,4},{1,9},{5... | collective-permute-start | bytes 49160 | tf_op jit(solution)/shard_map/ppermute | solution.py:218
  5.2 2.6 %collective-permute-start.6 = (bf16[8,1024]{1,0:T(8,128)(2,1)}, bf16[8,1024]{1,0:T(8,128)(2,1)S(1)}, u32[]{:S(2)}, u32[]{:S(2)}) collective-permute-start(bf16[8,1024]{1,0:T(8,128)(2,1)} %refs_6_.1), channel_id=1, source_target_pairs={{0,16},{4,20},{8,24},{12,28},{16,0},{20,4},{24,8},{28,12},{1,17},{... | collective-permute-start | bytes 49160 | tf_op jit(solution)/shard_map/ppermute | solution.py:218
  7.8 1.3 %collective-permute-start.7 = (bf16[8,1024]{1,0:T(8,128)(2,1)}, bf16[8,1024]{1,0:T(8,128)(2,1)S(1)}, u32[]{:S(2)}, u32[]{:S(2)}) collective-permute-start(bf16[8,1024]{1,0:T(8,128)(2,1)} %refs_6_.1), channel_id=1, source_target_pairs={{0,24},{4,28},{8,0},{12,4},{16,8},{20,12},{24,16},{28,20},{1,25},{... | collective-permute-start | bytes 49160 | tf_op jit(solution)/shard_map/ppermute | solution.py:218
  9.2 0.8 %constant_dynamic-update-slice_fusion.3 = bf16[8,4096]{1,0:T(8,128)(2,1)S(1)} fusion(bf16[8,1024]{1,0:T(8,128)(2,1)} %refs_6_.1), kind=kLoop, calls=%fused_computation.4 | loop fusion | bytes 32768
  10.6 3.4 %copy-done = bf16[1,1,256,128,128]{4,3,2,1,0:T(8,128)(2,1)S(1)} copy-done((bf16[1,1,256,128,128]{4,3,2,1,0:T(8,128)(2,1)S(1)}, bf16[1,1,256,128,128]{4,3,2,1,0:T(8,128)(2,1)}, u32[]{:S(2)}) %copy-start) | copy-done | bytes 8388632
  14.0 0.7 %copy-done.3 = s32[1,1,256]{2,1,0:T(1,128)S(1)} copy-done((s32[1,1,256]{2,1,0:T(1,128)S(1)}, s32[1,1,256]{2,1,0:T(1,128)}, u32[]{:S(2)}) %copy-start.3) | copy-done | bytes 1048
  14.7 0.7 %copy-done.5 = s32[1,1,256]{2,1,0:T(1,128)S(1)} copy-done((s32[1,1,256]{2,1,0:T(1,128)S(1)}, s32[1,1,256]{2,1,0:T(1,128)}, u32[]{:S(2)}) %copy-start.5) | copy-done | bytes 1048
  15.3 2.0 %mirror.1 = (f32[8,4096]{1,0:T(8,128)S(1)}, f32[8,4096]{1,0:T(8,128)S(1)}, bf16[256,128,128]{2,1,0:T(8,128)(2,1)S(1)}) custom-call(s32[1]{0:T(128)} %bitcast.6.counts, s32[256]{0:T(256)S(1)} %bitcast.9, s32[256]{0:T(256)S(1)} %bitcast.11, bf16[256,128,128]{2,1,0:T(8,128)(2,1)S(1)} %bitcast.8, bf16[8,1024]{1,0:T(8,128)(2,1)} %refs_6_.1, ...), custom_call_target="tpu_custom_call" | custom-call | flops 134217728 | bytes 8388608 | tf_op jit(solution)/shard_map/mirror/pallas_call | solution.py:244
  17.4 3.3 %copy-done.1 = bf16[256,128,128]{2,1,0:T(8,128)(2,1)} copy-done((bf16[256,128,128]{2,1,0:T(8,128)(2,1)}, bf16[256,128,128]{2,1,0:T(8,128)(2,1)S(1)}, u32[]{:S(2)}) %copy-start.1) | copy-done | bytes 8388632
  20.7 0.6 %collective-permute-start.8 = (bf16[8,4096]{1,0:T(8,128)(2,1)S(1)}, bf16[8,4096]{1,0:T(8,128)(2,1)S(1)}, u32[]{:S(2)}, u32[]{:S(2)}) collective-permute-start(bf16[8,4096]{1,0:T(8,128)(2,1)S(1)} %constant_dynamic-update-slice_fusion.near), channel_id=1, source_target_pairs={{0,4},{4,0},{8,12},{12,8},{16,20},{20,16},{24,28},{28,24},{1,5},{5... | collective-permute-start | bytes 196616 | tf_op jit(solution)/shard_map/ppermute | solution.py:215
  21.2 0.7 %collective-permute-done.1.theirs = f32[8,4096]{1,0:T(8,128)S(1)} collective-permute-done((f32[8,4096]{1,0:T(8,128)S(1)}, f32[8,4096]{1,0:T(8,128)S(1)}, u32[]{:S(2)}, u32[]{:S(2)}) %collective-permute-start.1) | collective-permute-done | bytes 131104 | tf_op jit(solution)/shard_map/ppermute | solution.py:215
  22.0 1.8 %collective-permute-start.2 = (f32[8,1024]{1,0:T(8,128)S(1)}, f32[8,1024]{1,0:T(8,128)S(1)}, u32[]{:S(2)}, u32[]{:S(2)}) collective-permute-start(f32[8,1024]{1,0:T(8,128)S(1)} %get-tuple-element.16), channel_id=1, source_target_pairs={{0,8},{4,12},{8,16},{12,20},{16,24},{20,28},{24,0},{28,4},{1,9},{5... | collective-permute-start | bytes 98312 | tf_op jit(solution)/shard_map/ppermute | solution.py:218
  23.8 1.4 %collective-permute-start.3 = (f32[8,1024]{1,0:T(8,128)S(1)}, f32[8,1024]{1,0:T(8,128)S(1)}, u32[]{:S(2)}, u32[]{:S(2)}) collective-permute-start(f32[8,1024]{1,0:T(8,128)S(1)} %get-tuple-element.17), channel_id=1, source_target_pairs={{0,16},{4,20},{8,24},{12,28},{16,0},{20,4},{24,8},{28,12},{1,17},{... | collective-permute-start | bytes 98312 | tf_op jit(solution)/shard_map/ppermute | solution.py:218
  25.2 2.3 %collective-permute-start.4 = (f32[8,1024]{1,0:T(8,128)S(1)}, f32[8,1024]{1,0:T(8,128)S(1)}, u32[]{:S(2)}, u32[]{:S(2)}) collective-permute-start(f32[8,1024]{1,0:T(8,128)S(1)} %get-tuple-element.18), channel_id=1, source_target_pairs={{0,24},{4,28},{8,0},{12,4},{16,8},{20,12},{24,16},{28,20},{1,25},{... | collective-permute-start | bytes 98312 | tf_op jit(solution)/shard_map/ppermute | solution.py:218
  27.4 1.5 %collective-permute-start.9 = (bf16[8,1024]{1,0:T(8,128)(2,1)}, bf16[8,1024]{1,0:T(8,128)(2,1)S(1)}, u32[]{:S(2)}, u32[]{:S(2)}) collective-permute-start(bf16[8,1024]{1,0:T(8,128)(2,1)} %refs_6_.1), channel_id=1, source_target_pairs={{0,1},{1,0},{2,3},{3,2},{4,5},{5,4},{6,7},{7,6},{8,9},{9,8},{10,11... | collective-permute-start | bytes 49160 | tf_op jit(solution)/shard_map/ppermute | solution.py:224
  28.9 0.5 %collective-permute-start.10 = (bf16[8,1024]{1,0:T(8,128)(2,1)S(1)}, bf16[8,1024]{1,0:T(8,128)(2,1)S(1)}, u32[]{:S(2)}, u32[]{:S(2)}) collective-permute-start(bf16[8,1024]{1,0:T(8,128)(2,1)S(1)} %collective-permute-done.refs_1_.refs_7_), channel_id=1, source_target_pairs={{0,1},{1,0},{2,3},{3,2},{4,5},{5,4},{6,7},{7,6},{8,9},{9,8},{10,11... | collective-permute-start | bytes 49160 | tf_op jit(solution)/shard_map/ppermute | solution.py:224
  29.4 3.4 %copy-done.2 = bf16[256,128,128]{2,1,0:T(8,128)(2,1)S(1)} copy-done((bf16[256,128,128]{2,1,0:T(8,128)(2,1)S(1)}, bf16[256,128,128]{2,1,0:T(8,128)(2,1)}, u32[]{:S(2)}) %copy-start.2) | copy-done | bytes 8388632
  32.8 1.4 %forward.1 = (f32[8,1024]{1,0:T(8,128)S(1)}, f32[8,1024]{1,0:T(8,128)S(1)}) custom-call(s32[1]{0:T(128)} %bitcast.7.counts, s32[256]{0:T(256)S(1)} %bitcast.10, s32[256]{0:T(256)S(1)} %bitcast.12, bf16[256,128,128]{2,1,0:T(8,128)(2,1)S(1)} %copy-done.2, bf16[8,4096]{1,0:T(8,128)(2,1)S(1)} %constant_dynamic-update-slice_fusion.near, ...), custom_call_target="tpu_custom_call" | custom-call | flops 134217728 | bytes 8388608 | tf_op jit(solution)/shard_map/forward/pallas_call | solution.py:267
  34.3 1.1 %gram.1 = (f32[8,1024]{1,0:T(8,128)S(1)}, f32[2,8,8]{2,1,0:T(8,128)S(1)}) custom-call(f32[8,1024]{1,0:T(8,128)S(1)} %get-tuple-element.15.refs_0_, f32[8,1024]{1,0:T(8,128)S(1)} %collective-permute-done.2.refs_1_, f32[8,1024]{1,0:T(8,128)S(1)} %collective-permute-done.3.refs_2_, f32[8,1024]{1,0:T(8,128)S(1)} %collective-permute-done.4.refs_3_, ...), custom_call_target="tpu_custom_call" | custom-call | tf_op jit(solution)/shard_map/gram/pallas_call | solution.py:284
  35.4 1.2 %collective-permute-done.12 = f32[2,8,8]{2,1,0:T(8,128)S(1)} collective-permute-done((f32[2,8,8]{2,1,0:T(8,128)S(1)}, f32[2,8,8]{2,1,0:T(8,128)S(1)}, u32[]{:S(2)}, u32[]{:S(2)}) %collective-permute-start.12) | collective-permute-done | bytes 544 | tf_op jit(solution)/shard_map/ppermute | solution.py:303
  36.6 2.4 %collective-permute-start.14 = (f32[2,8,8]{2,1,0:T(8,128)S(1)}, f32[2,8,8]{2,1,0:T(8,128)S(1)}, u32[]{:S(2)}, u32[]{:S(2)}) collective-permute-start(f32[2,8,8]{2,1,0:T(8,128)S(1)} %add.26), channel_id=1, source_target_pairs={{0,10},{2,8},{4,20},{6,22},{8,2},{10,0},{12,28},{14,30},{16,26},{1... | collective-permute-start | bytes 1544 | tf_op jit(solution)/shard_map/ppermute | solution.py:314
  39.0 2.3 %collective-permute-start.15 = (f32[2,8,8]{2,1,0:T(8,128)S(1)}, f32[2,8,8]{2,1,0:T(8,128)S(1)}, u32[]{:S(2)}, u32[]{:S(2)}) collective-permute-start(f32[2,8,8]{2,1,0:T(8,128)S(1)} %add.26), channel_id=1, source_target_pairs={{0,18},{2,16},{4,28},{6,30},{8,26},{10,24},{12,20},{14,22},{16,2},... | collective-permute-start | bytes 1544 | tf_op jit(solution)/shard_map/ppermute | solution.py:314
  41.3 2.0 %collective-permute-start.16 = (f32[2,8,8]{2,1,0:T(8,128)S(1)}, f32[2,8,8]{2,1,0:T(8,128)S(1)}, u32[]{:S(2)}, u32[]{:S(2)}) collective-permute-start(f32[2,8,8]{2,1,0:T(8,128)S(1)} %add.26), channel_id=1, source_target_pairs={{0,26},{2,24},{4,30},{6,28},{8,18},{10,16},{12,22},{14,20},{16,10}... | collective-permute-start | bytes 1544 | tf_op jit(solution)/shard_map/ppermute | solution.py:314
  43.3 0.5 collective-permute-start.11
  43.8 0.6 %collective-permute-done.15 = f32[2,8,8]{2,1,0:T(8,128)S(1)} collective-permute-done((f32[2,8,8]{2,1,0:T(8,128)S(1)}, f32[2,8,8]{2,1,0:T(8,128)S(1)}, u32[]{:S(2)}, u32[]{:S(2)}) %collective-permute-start.15) | collective-permute-done | bytes 544 | tf_op jit(solution)/shard_map/ppermute | solution.py:314
  44.4 3.2 %collective-permute-done.16 = f32[2,8,8]{2,1,0:T(8,128)S(1)} collective-permute-done((f32[2,8,8]{2,1,0:T(8,128)S(1)}, f32[2,8,8]{2,1,0:T(8,128)S(1)}, u32[]{:S(2)}, u32[]{:S(2)}) %collective-permute-start.16) | collective-permute-done | bytes 544 | tf_op jit(solution)/shard_map/ppermute | solution.py:314
  47.7 0.6 %add_convert_fusion = bf16[8,1024]{1,0:T(8,128)(2,1)} fusion(f32[8,1024]{1,0:T(8,128)S(1)} %get-tuple-element.22, f32[8,1024]{1,0:T(8,128)S(1)} %collective-permute-done.11), kind=kLoop, calls=%fused_computation | loop fusion | flops 16384 | bytes 81920 | tf_op jit(solution)/shard_map/convert_element_type | solution.py:296
  48.3 0.5 %collective-permute-done.17 = f32[2,8,8]{2,1,0:T(8,128)S(1)} collective-permute-done((f32[2,8,8]{2,1,0:T(8,128)S(1)}, f32[2,8,8]{2,1,0:T(8,128)S(1)}, u32[]{:S(2)}, u32[]{:S(2)}) %collective-permute-start.17) | collective-permute-done | bytes 544 | tf_op jit(solution)/shard_map/ppermute | solution.py:320
  48.9 0.7 %copy.8 = f32[16,8]{0,1:T(8,128)} copy(f32[16,8]{1,0:T(8,128)S(1)} %add_bitcast_fusion) | data formatting | bytes 1024 | tf_op jit(solution)/shard_map/reshape | solution.py:295
  (31 shorter events, 0.1 us)
Async XLA Ops:
  0.6 28.8 %copy-start.4 = (s32[1,1,256]{2,1,0:T(1,128)S(1)}, s32[1,1,256]{2,1,0:T(1,128)}, u32[]{:S(2)}) copy-start(s32[1,1,256]{2,1,0:T(1,128)} %param.7) | copy-start | bytes 3076
  0.6 28.8 %copy-start.6 = (s32[1,1,256]{2,1,0:T(1,128)S(1)}, s32[1,1,256]{2,1,0:T(1,128)}, u32[]{:S(2)}) copy-start(s32[1,1,256]{2,1,0:T(1,128)} %param.8) | copy-start | bytes 3076
  0.7 9.9 %collective-permute-start = (bf16[8,1024]{1,0:T(8,128)(2,1)}, bf16[8,1024]{1,0:T(8,128)(2,1)S(1)}, u32[]{:S(2)}, u32[]{:S(2)}) collective-permute-start(bf16[8,1024]{1,0:T(8,128)(2,1)} %refs_6_.1), channel_id=1, source_target_pairs={{0,2},{2,0},{1,3},{3,1},{4,6},{6,4},{5,7},{7,5},{8,10},{10,8},{9,1... | collective-permute-start | bytes 49160 | tf_op jit(solution)/shard_map/ppermute | solution.py:221
  3.7 17.0 %collective-permute-start.5 = (bf16[8,1024]{1,0:T(8,128)(2,1)}, bf16[8,1024]{1,0:T(8,128)(2,1)S(1)}, u32[]{:S(2)}, u32[]{:S(2)}) collective-permute-start(bf16[8,1024]{1,0:T(8,128)(2,1)} %refs_6_.1), channel_id=1, source_target_pairs={{0,8},{4,12},{8,16},{12,20},{16,24},{20,28},{24,0},{28,4},{1,9},{5... | collective-permute-start | bytes 49160 | tf_op jit(solution)/shard_map/ppermute | solution.py:218
  5.2 15.4 %collective-permute-start.6 = (bf16[8,1024]{1,0:T(8,128)(2,1)}, bf16[8,1024]{1,0:T(8,128)(2,1)S(1)}, u32[]{:S(2)}, u32[]{:S(2)}) collective-permute-start(bf16[8,1024]{1,0:T(8,128)(2,1)} %refs_6_.1), channel_id=1, source_target_pairs={{0,16},{4,20},{8,24},{12,28},{16,0},{20,4},{24,8},{28,12},{1,17},{... | collective-permute-start | bytes 49160 | tf_op jit(solution)/shard_map/ppermute | solution.py:218
  7.8 12.8 %collective-permute-start.7 = (bf16[8,1024]{1,0:T(8,128)(2,1)}, bf16[8,1024]{1,0:T(8,128)(2,1)S(1)}, u32[]{:S(2)}, u32[]{:S(2)}) collective-permute-start(bf16[8,1024]{1,0:T(8,128)(2,1)} %refs_6_.1), channel_id=1, source_target_pairs={{0,24},{4,28},{8,0},{12,4},{16,8},{20,12},{24,16},{28,20},{1,25},{... | collective-permute-start | bytes 49160 | tf_op jit(solution)/shard_map/ppermute | solution.py:218
  10.6 3.4 %copy-start = (bf16[1,1,256,128,128]{4,3,2,1,0:T(8,128)(2,1)S(1)}, bf16[1,1,256,128,128]{4,3,2,1,0:T(8,128)(2,1)}, u32[]{:S(2)}) copy-start(bf16[1,1,256,128,128]{4,3,2,1,0:T(8,128)(2,1)} %param.6) | copy-start | bytes 25165828
  14.0 0.7 %copy-start.3 = (s32[1,1,256]{2,1,0:T(1,128)S(1)}, s32[1,1,256]{2,1,0:T(1,128)}, u32[]{:S(2)}) copy-start(s32[1,1,256]{2,1,0:T(1,128)} %param.7) | copy-start | bytes 3076
  14.7 0.7 %copy-start.5 = (s32[1,1,256]{2,1,0:T(1,128)S(1)}, s32[1,1,256]{2,1,0:T(1,128)}, u32[]{:S(2)}) copy-start(s32[1,1,256]{2,1,0:T(1,128)} %param.8) | copy-start | bytes 3076
  17.3 3.3 %copy-start.1 = (bf16[256,128,128]{2,1,0:T(8,128)(2,1)}, bf16[256,128,128]{2,1,0:T(8,128)(2,1)S(1)}, u32[]{:S(2)}) copy-start(bf16[256,128,128]{2,1,0:T(8,128)(2,1)S(1)} %get-tuple-element.19.tiles) | copy-start | bytes 25165828
  20.6 1.3 %collective-permute-start.1 = (f32[8,4096]{1,0:T(8,128)S(1)}, f32[8,4096]{1,0:T(8,128)S(1)}, u32[]{:S(2)}, u32[]{:S(2)}) collective-permute-start(f32[8,4096]{1,0:T(8,128)S(1)} %get-tuple-element.14), channel_id=1, source_target_pairs={{0,4},{4,0},{8,12},{12,8},{16,20},{20,16},{24,28},{28,24},{1,5},{5... | collective-permute-start | bytes 393224 | tf_op jit(solution)/shard_map/ppermute | solution.py:215
  20.7 8.3 %collective-permute-start.8 = (bf16[8,4096]{1,0:T(8,128)(2,1)S(1)}, bf16[8,4096]{1,0:T(8,128)(2,1)S(1)}, u32[]{:S(2)}, u32[]{:S(2)}) collective-permute-start(bf16[8,4096]{1,0:T(8,128)(2,1)S(1)} %constant_dynamic-update-slice_fusion.near), channel_id=1, source_target_pairs={{0,4},{4,0},{8,12},{12,8},{16,20},{20,16},{24,28},{28,24},{1,5},{5... | collective-permute-start | bytes 196616 | tf_op jit(solution)/shard_map/ppermute | solution.py:215
  22.0 12.3 %collective-permute-start.2 = (f32[8,1024]{1,0:T(8,128)S(1)}, f32[8,1024]{1,0:T(8,128)S(1)}, u32[]{:S(2)}, u32[]{:S(2)}) collective-permute-start(f32[8,1024]{1,0:T(8,128)S(1)} %get-tuple-element.16), channel_id=1, source_target_pairs={{0,8},{4,12},{8,16},{12,20},{16,24},{20,28},{24,0},{28,4},{1,9},{5... | collective-permute-start | bytes 98312 | tf_op jit(solution)/shard_map/ppermute | solution.py:218
  23.8 10.5 %collective-permute-start.3 = (f32[8,1024]{1,0:T(8,128)S(1)}, f32[8,1024]{1,0:T(8,128)S(1)}, u32[]{:S(2)}, u32[]{:S(2)}) collective-permute-start(f32[8,1024]{1,0:T(8,128)S(1)} %get-tuple-element.17), channel_id=1, source_target_pairs={{0,16},{4,20},{8,24},{12,28},{16,0},{20,4},{24,8},{28,12},{1,17},{... | collective-permute-start | bytes 98312 | tf_op jit(solution)/shard_map/ppermute | solution.py:218
  25.2 9.1 %collective-permute-start.4 = (f32[8,1024]{1,0:T(8,128)S(1)}, f32[8,1024]{1,0:T(8,128)S(1)}, u32[]{:S(2)}, u32[]{:S(2)}) collective-permute-start(f32[8,1024]{1,0:T(8,128)S(1)} %get-tuple-element.18), channel_id=1, source_target_pairs={{0,24},{4,28},{8,0},{12,4},{16,8},{20,12},{24,16},{28,20},{1,25},{... | collective-permute-start | bytes 98312 | tf_op jit(solution)/shard_map/ppermute | solution.py:218
  27.4 6.8 %collective-permute-start.9 = (bf16[8,1024]{1,0:T(8,128)(2,1)}, bf16[8,1024]{1,0:T(8,128)(2,1)S(1)}, u32[]{:S(2)}, u32[]{:S(2)}) collective-permute-start(bf16[8,1024]{1,0:T(8,128)(2,1)} %refs_6_.1), channel_id=1, source_target_pairs={{0,1},{1,0},{2,3},{3,2},{4,5},{5,4},{6,7},{7,6},{8,9},{9,8},{10,11... | collective-permute-start | bytes 49160 | tf_op jit(solution)/shard_map/ppermute | solution.py:224
  28.9 5.3 %collective-permute-start.10 = (bf16[8,1024]{1,0:T(8,128)(2,1)S(1)}, bf16[8,1024]{1,0:T(8,128)(2,1)S(1)}, u32[]{:S(2)}, u32[]{:S(2)}) collective-permute-start(bf16[8,1024]{1,0:T(8,128)(2,1)S(1)} %collective-permute-done.refs_1_.refs_7_), channel_id=1, source_target_pairs={{0,1},{1,0},{2,3},{3,2},{4,5},{5,4},{6,7},{7,6},{8,9},{9,8},{10,11... | collective-permute-start | bytes 49160 | tf_op jit(solution)/shard_map/ppermute | solution.py:224
  29.4 3.4 %copy-start.2 = (bf16[256,128,128]{2,1,0:T(8,128)(2,1)S(1)}, bf16[256,128,128]{2,1,0:T(8,128)(2,1)}, u32[]{:S(2)}) copy-start(bf16[256,128,128]{2,1,0:T(8,128)(2,1)} %copy-done.1) | copy-start | bytes 25165828
  35.4 1.2 %collective-permute-start.12 = (f32[2,8,8]{2,1,0:T(8,128)S(1)}, f32[2,8,8]{2,1,0:T(8,128)S(1)}, u32[]{:S(2)}, u32[]{:S(2)}) collective-permute-start(f32[2,8,8]{2,1,0:T(8,128)S(1)} %get-tuple-element.23), channel_id=1, source_target_pairs={{0,4},{4,0},{8,12},{12,8},{16,20},{20,16},{24,28},{28,24},{1,5},{5... | collective-permute-start | bytes 1544 | tf_op jit(solution)/shard_map/ppermute | solution.py:303
  36.6 7.2 %collective-permute-start.13 = (f32[2,8,8]{2,1,0:T(8,128)S(1)}, f32[2,8,8]{2,1,0:T(8,128)S(1)}, u32[]{:S(2)}, u32[]{:S(2)}) collective-permute-start(f32[2,8,8]{2,1,0:T(8,128)S(1)} %add.26), channel_id=1, source_target_pairs={{0,2},{2,0},{4,12},{6,14},{8,10},{10,8},{12,4},{14,6},{16,18},{18,... | collective-permute-start | bytes 1544 | tf_op jit(solution)/shard_map/ppermute | solution.py:314
  36.6 7.2 %collective-permute-start.14 = (f32[2,8,8]{2,1,0:T(8,128)S(1)}, f32[2,8,8]{2,1,0:T(8,128)S(1)}, u32[]{:S(2)}, u32[]{:S(2)}) collective-permute-start(f32[2,8,8]{2,1,0:T(8,128)S(1)} %add.26), channel_id=1, source_target_pairs={{0,10},{2,8},{4,20},{6,22},{8,2},{10,0},{12,28},{14,30},{16,26},{1... | collective-permute-start | bytes 1544 | tf_op jit(solution)/shard_map/ppermute | solution.py:314
  39.0 5.4 %collective-permute-start.15 = (f32[2,8,8]{2,1,0:T(8,128)S(1)}, f32[2,8,8]{2,1,0:T(8,128)S(1)}, u32[]{:S(2)}, u32[]{:S(2)}) collective-permute-start(f32[2,8,8]{2,1,0:T(8,128)S(1)} %add.26), channel_id=1, source_target_pairs={{0,18},{2,16},{4,28},{6,30},{8,26},{10,24},{12,20},{14,22},{16,2},... | collective-permute-start | bytes 1544 | tf_op jit(solution)/shard_map/ppermute | solution.py:314
  41.3 6.3 %collective-permute-start.16 = (f32[2,8,8]{2,1,0:T(8,128)S(1)}, f32[2,8,8]{2,1,0:T(8,128)S(1)}, u32[]{:S(2)}, u32[]{:S(2)}) collective-permute-start(f32[2,8,8]{2,1,0:T(8,128)S(1)} %add.26), channel_id=1, source_target_pairs={{0,26},{2,24},{4,30},{6,28},{8,18},{10,16},{12,22},{14,20},{16,10}... | collective-permute-start | bytes 1544 | tf_op jit(solution)/shard_map/ppermute | solution.py:314
  43.3 4.4 %collective-permute-start.11 = (f32[8,1024]{1,0:T(8,128)S(1)}, f32[8,1024]{1,0:T(8,128)S(1)}, u32[]{:S(2)}, u32[]{:S(2)}) collective-permute-start(f32[8,1024]{1,0:T(8,128)S(1)} %get-tuple-element.21.refs_5_), channel_id=1, source_target_pairs={{0,2},{2,0},{1,3},{3,1},{4,6},{6,4},{5,7},{7,5},{8,10},{10,8},{9,1... | collective-permute-start | bytes 98312 | tf_op jit(solution)/shard_map/ppermute | solution.py:221
  47.7 1.2 %collective-permute-start.17 = (f32[2,8,8]{2,1,0:T(8,128)S(1)}, f32[2,8,8]{2,1,0:T(8,128)S(1)}, u32[]{:S(2)}, u32[]{:S(2)}) collective-permute-start(f32[2,8,8]{2,1,0:T(8,128)S(1)} %select_add_fusion), channel_id=1, source_target_pairs={{0,4},{4,0},{8,12},{12,8},{16,20},{20,16},{24,28},{28,24},{1,5},{5... | collective-permute-start | bytes 1544 | tf_op jit(solution)/shard_map/ppermute | solution.py:320

commit v3 on v2

--- a/solution.py
+++ b/solution.py
@@ -68,7 +68,7 @@
 
 def places(rows, cols, span, stretch):
     def get(s):
-        r, c = rows[s], cols[s]
+        r, c = rows[0, s], cols[0, s]
         return r, c, lax.rem(r, span), lax.div(c, span) * stretch + lax.rem(c, stretch)
 
     return get
@@ -79,39 +79,41 @@
     return lax.div(i, 2), lax.rem(i, 2), lax.axis_index("col")
 
 
-def start_lists(lists, held, sems):
-    copies = [pltpu.make_async_copy(a, b, sems.at[n]) for n, (a, b) in enumerate(zip(lists, held))]
+def start_copies(sems, *pairs):
+    copies = [pltpu.make_async_copy(a, b, sems.at[n]) for n, (a, b) in enumerate(pairs)]
     for copy in copies:
         copy.start()
     return copies
 
 
-def mirror_kernel(sizes, counts, rows_hbm, cols_hbm, tiles_hbm, *refs):
+def mirror_kernel(sizes, counts, rows_hbm, cols_hbm, tiles_hbm, x_hbm, *refs):
     nz, ncol, stretch = sizes
     span = ncol * stretch
-    blocks, (mine, other, tiles), refs = refs[:ncol], refs[ncol : ncol + 3], refs[ncol + 3 :]
-    rows, cols, list_sems, tile_sems, low, high, *sums = refs
-    slots = tiles.shape[0]
+    blocks, (mine, other, tiles, x), refs = refs[: ncol - 1], refs[ncol - 1 : ncol + 3], refs[ncol + 3 :]
+    rows, cols, small, sems, low, high, *sums = refs
     tile = tiles.shape[-1]
     width = stretch * tile
-    copies = start_lists((rows_hbm, cols_hbm), (rows, cols), list_sems)
-    count = counts[0]
+    count = counts[0, 0]
     chunks = pl.cdiv(count, CHUNK)
 
     def load(step):
         at = pl.ds(step * CHUNK, CHUNK)
-        return pltpu.make_async_copy(tiles_hbm.at[at], tiles.at[at], tile_sems.at[step])
+        return pltpu.make_async_copy(tiles_hbm.at[at], tiles.at[at], sems.at[step])
 
     def start(step):
         @pl.when(step < chunks)
         def _():
             load(step).start()
 
+    copies = start_copies(small, (x_hbm, x), (rows_hbm, rows), (cols_hbm, cols))
     for step in range(AHEAD):
         start(step)
     z, core, j = position()
-    for t in range(ncol):
-        place_block(low, high, blocks[t], lax.rem(j + ncol - t, ncol) * stretch, stretch, tile)
+    for t in range(1, ncol):
+        place_block(low, high, blocks[t - 1], lax.rem(j + ncol - t, ncol) * stretch, stretch, tile)
+    for copy in copies:
+        copy.wait()
+    place_block(low, high, x, j * stretch, stretch, tile)
     low[span] = jnp.zeros(low.shape[1:], low.dtype)
     high[span] = jnp.zeros(high.shape[1:], high.dtype)
     get = places(rows, cols, span, stretch)
@@ -124,8 +126,6 @@
         load(step).wait()
         start(step + AHEAD)
 
-    for copy in copies:
-        copy.wait()
     multiply_tiles(pick, False, count, tiles, low, high, sums, arrive)
     for s in range(nz):
         target = 2 * lax.rem(z + s, nz)
@@ -141,17 +141,19 @@
 def forward_kernel(sizes, counts, rows_hbm, cols_hbm, tiles, near, far, *refs):
     nz, ncol, stretch = sizes
     span = ncol * stretch
-    outs, (rows, cols, list_sems, low, high, *sums) = refs[:ncol], refs[ncol:]
+    outs, (rows, cols, small, low, high, *sums) = refs[:ncol], refs[ncol:]
+    copies = start_copies(small, (rows_hbm, rows), (cols_hbm, cols))
     tile = tiles.shape[-1]
     width = stretch * tile
-    copies = start_lists((rows_hbm, cols_hbm), (rows, cols), list_sems)
-    count = counts[0]
+    count = counts[0, 0]
     z, core, j = position()
     for s in range(nz):
         source = 2 * lax.rem(z + nz - s, nz)
         for ref, c in ((near, core), (far, 1 - core)):
             place_block(low, high, ref[:, s * width : (s + 1) * width], (source + c) * stretch, stretch, tile)
     dead = 2 * nz * stretch
+    for copy in copies:
+        copy.wait()
     low[dead] = jnp.zeros(low.shape[1:], low.dtype)
     high[dead] = jnp.zeros(high.shape[1:], high.dtype)
     get = places(rows, cols, span, stretch)
@@ -160,8 +162,6 @@
         _, _, row_place, col_place = get(s)
         return jnp.where(s < count, col_place, dead), row_place
 
-    for copy in copies:
-        copy.wait()
     multiply_tiles(pick, True, count, tiles, low, high, sums)
     for t in range(ncol):
         first = lax.rem(j + t, ncol) * stretch
@@ -188,18 +188,25 @@
         total += ref[...]
     image[...] = total
     terms = [total] + [ref[...] for ref in parts[1:]]
+    products = []
     for k in range(nvec):
         product = None
         for t in range(ncol):
             one = lax.dot_general(
+                terms[t],
                 xs[k * ncol + t][...].astype(F32),
-                terms[t],
                 (((1,), (1,)), ((), ())),
                 precision=HIGHEST,
                 preferred_element_type=F32,
             )
             product = one if product is None else product + one
-        share[lax.rem(lax.axis_index("vec") + nvec - k, nvec)] = product * scale
+        products.append(product * scale)
+    me = lax.axis_index("vec")
+    for a in range(nvec):
+        picked = products[0]
+        for k in range(1, nvec):
+            picked = jnp.where(lax.rem(me + nvec - a, nvec) == k, products[k], picked)
+        share[:, a * picked.shape[1] : (a + 1) * picked.shape[1]] = picked
 
 
 def shards(sizes, vectors, tile_vals, tile_rows, tile_cols, tile_counts):
@@ -209,7 +216,10 @@
     slots, tile = tile_vals.shape[2], tile_vals.shape[-1]
     stretch = width // tile
     span = ncol * stretch
-    tiles, rows, cols, counts = tile_vals[0, 0], tile_rows[0, 0], tile_cols[0, 0], tile_counts[0]
+    x_hbm, tiles, rows, cols = (
+        pltpu.with_memory_space_constraint(a, pltpu.HBM)
+        for a in (vectors, tile_vals[0, 0], tile_rows[0], tile_cols[0])
+    )
 
     def core_swap(x):
         return lax.ppermute(x, "row", [(a, a ^ 1) for a in range(nrow)])
@@ -224,8 +234,7 @@
         return lax.ppermute(x, "vec", [(a, (a + t) % nvec) for a in range(nvec)])
 
     row_x = [vectors] + [col_shift(vectors, t) for t in range(1, ncol)]
-    near = jnp.concatenate([vectors] + [z_shift(vectors, s) for s in range(1, nz)], axis=1)
-    far = core_swap(near)
+    ring_x = [z_shift(vectors, s) for s in range(1, nz)]
 
     def tables(count):
         shape = pltpu.VMEM((count + 1, 2 * vlocal, tile), vectors.dtype)
@@ -240,27 +249,29 @@
     cost = pl.CostEstimate(
         flops=2 * slots * tile * tile * 2 * vlocal, bytes_accessed=slots * tile * tile * 2, transcendentals=0
     )
-    lists = [pltpu.SMEM((slots,), jnp.int32)] * 2 + [pltpu.SemaphoreType.DMA((2,))]
-    mine, other, held = pl.pallas_call(
+    lists = [pltpu.SMEM((1, slots), jnp.int32)] * 2
+    mine, other, held, x = pl.pallas_call(
         functools.partial(mirror_kernel, step),
-        out_shape=[ring, ring, jax.ShapeDtypeStruct(tiles.shape, tiles.dtype)],
-        in_specs=[SMEM] + [HBM] * 3 + [VMEM] * ncol,
-        out_specs=[VMEM] * 3,
+        out_shape=[ring, ring, jax.ShapeDtypeStruct(tiles.shape, tiles.dtype), jax.ShapeDtypeStruct(vectors.shape, vectors.dtype)],
+        in_specs=[SMEM] + [HBM] * 4 + [VMEM] * (ncol - 1),
+        out_specs=[VMEM] * 4,
         scratch_shapes=lists
-        + [pltpu.SemaphoreType.DMA((slots // CHUNK,))]
+        + [pltpu.SemaphoreType.DMA((3,)), pltpu.SemaphoreType.DMA((slots // CHUNK,))]
         + tables(span)
         + sums(nrow * stretch),
-        compiler_params=params(24),
+        compiler_params=params(6),
         cost_estimate=cost,
         name="mirror",
-    )(counts, rows, cols, tiles, *row_x)
+    )(tile_counts, rows, cols, tiles, x_hbm, *row_x[1:])
+    near = jnp.concatenate([x] + ring_x, axis=1)
+    far = core_swap(near)
     theirs = core_swap(other)
     pieces = pl.pallas_call(
         functools.partial(pair_kernel, nz),
         out_shape=[block] * nz,
         in_specs=[VMEM] * 2,
         out_specs=[VMEM] * nz,
-        compiler_params=params(8),
+        compiler_params=params(6),
         name="pair",
     )(mine, theirs)
     col_parts = [pieces[0]] + [z_shift(pieces[s], s) for s in range(1, nz)]
@@ -269,30 +280,30 @@
         out_shape=[block] * ncol,
         in_specs=[SMEM] + [HBM] * 2 + [VMEM] * 3,
         out_specs=[VMEM] * ncol,
-        scratch_shapes=lists + tables(nrow * stretch) + sums(span),
-        compiler_params=params(24),
+        scratch_shapes=lists + [pltpu.SemaphoreType.DMA((2,))] + tables(nrow * stretch) + sums(span),
+        compiler_params=params(6),
         cost_estimate=cost,
         name="forward",
-    )(counts, rows, cols, held, near, far)
+    )(tile_counts, rows, cols, held, near, far)
     others = [vec_shift(x, t) for t in range(1, nvec) for x in [row_x[0]] + row_x[1:]]
     def by_target(xs):
         return [xs[(ncol - t) % ncol] for t in range(ncol)]
 
-    xs = by_target(row_x)
+    xs = by_target([x] + row_x[1:])
     for t in range(1, nvec):
         xs += by_target(others[(t - 1) * ncol : t * ncol])
     image, share = pl.pallas_call(
         functools.partial(gram_kernel, nz, ncol, nvec, 1.0 / math.sqrt(width * nrow * ncol)),
-        out_shape=[block, jax.ShapeDtypeStruct((nvec, vlocal, vlocal), F32)],
+        out_shape=[block, jax.ShapeDtypeStruct((vlocal, nvec * vlocal), F32)],
         in_specs=[VMEM] * (nz + ncol + nvec * ncol),
         out_specs=[VMEM] * 2,
-        compiler_params=params(8),
+        compiler_params=params(6),
         name="gram",
     )(*col_parts, *row_parts, *xs)
     for t in range(1, ncol):
         image = image + col_shift(row_parts[t], t)
     share = all_sum(share, nz, ncol)
-    gram = share.reshape(nvec * vlocal, vlocal)
+    gram = share.T
     return (image.astype(jnp.bfloat16), gram)
 
 
@@ -303,7 +314,6 @@
     share = share + lax.ppermute(share, "row", [(a, a ^ 1) for a in range(nrow)])
     shifts = sorted(((s, t) for s in range(nz) for t in range(ncol)), key=sum)[1:]
     got = None
-    core = lax.axis_index("row") % 2
     for n in range(0, len(shifts), 2):
         pair = shifts[n : n + 2]
         perm = []
@@ -313,7 +323,7 @@
                 perm.append((a * ncol + b, (a ^ (2 * s)) * ncol + (b + t) % ncol))
         part = lax.ppermute(share, ("row", "col"), perm)
         if len(pair) == 1:
-            part = jnp.where(core == 0, part, 0.0)
+            part = part * 0.5
         got = part if got is None else got + part
     if got is None:
         return share

time: 50 us -> 39.4 us (0.79)
  local copies, waits for them, and re-layouts: 12.8 us -> 0.02 us
  starting transfers between devices: 23.8 us -> 25.3 us
  waiting for transfers between devices: 6.35 us -> 7.26 us
  other arithmetic: 0.62 us -> 1.22 us
  Pallas kernels: 4.5 us -> 3.93 us
    unnamed x17 -> x5, local copies, waits for them, and re-layouts: 12.2 us -> 0.01 us
    ppermute x4, waiting for transfers between devices: 3.87 us -> 1.34 us  [all_sum(): part = lax.ppermute(share, ('row', 'col'), perm)]
    ppermute x2, waiting for transfers between devices: 0.01 us -> 2.32 us  [col_shift(): return lax.ppermute(x, 'col', [(a, (a + t) % ncol) for a in range(ncol)])]
    ppermute x6, starting transfers between devices: 10.9 us -> 12.7 us  [z_shift(): lax.ppermute(x, 'row', [(a, (a + 2 * s) % nrow) for a in range(nrow)])]
    ppermute x2, waiting for transfers between devices: 0.01 us -> 1.69 us  [vec_shift(): return lax.ppermute(x, 'vec', [(a, (a + t) % nvec) for a in range(nvec)])]
    pallas_call x1, Pallas kernels: 1.09 us -> 0.4 us  [shards(): pl.pallas_call(functools.partial(gram_kernel, nz, ncol, nvec, 1.0 / math....]
    reshape x1 -> x0, local copies, waits for them, and re-layouts: 0.66 us -> none  [shards(): gram = share.reshape(nvec * vlocal, vlocal)]
    transpose x0 -> x1, other arithmetic: none -> 0.6 us  [shards(): gram = share.T]
  transfers between devices with their start and end apart: 18 -> 18, of which waited for: 5 -> 6; matrix products, arithmetic and copies ran while one was open for 3% -> 2% of each run, Pallas kernels for 7% -> 9%
where the time goes in v3:
time: 39.4 us; the launch traced here: 39.2 us
  starting transfers between devices  25.3 us (64%)
  waiting for transfers between devices  7.26 us (18%)
  Pallas kernels  3.93 us (10%)
  between operations  1.41 us (4%)
  other arithmetic  1.22 us (3%)
    ppermute x6, starting transfers between devices, z_shift(): lax.ppermute(x, 'row', [(a, (a + 2 * s) % nrow) for a in range(nrow)])  12.7 us
    ppermute x4, starting transfers between devices, all_sum(): part = lax.ppermute(share, ('row', 'col'), perm)  6.75 us
    ppermute x2, starting transfers between devices, col_shift(): return lax.ppermute(x, 'col', [(a, (a + t) % ncol) for a in range(ncol)])  3.24 us
    ppermute x2, waiting for transfers between devices, col_shift(): return lax.ppermute(x, 'col', [(a, (a + t) % ncol) for a in range(ncol)])  2.32 us
    ppermute x2, starting transfers between devices, vec_shift(): return lax.ppermute(x, 'vec', [(a, (a + t) % nvec) for a in range(nvec)])  2.03 us
    pallas_call x1, Pallas kernels, shards(): pl.pallas_call(functools.partial(mirror_kernel, step), out_shape=[ring, r...  1.98 us
    ppermute x2, waiting for transfers between devices, vec_shift(): return lax.ppermute(x, 'vec', [(a, (a + t) % nvec) for a in range(nvec)])  1.69 us
    pallas_call x1, Pallas kernels, shards(): pl.pallas_call(functools.partial(forward_kernel, step), out_shape=[block]...  1.54 us
  transfers between devices with their start and end apart: 18, of which 6 were waited for; matrix products, arithmetic and copies ran while one was open for 2% of the time, Pallas kernels for 9%

profile of v3, /device:TPU:0, one launch (start us, length us, event | category | flops | bytes accessed | tf_op | source)
XLA Modules:
  0.0 39.2 jit_solution(5492383072536423660)
XLA Ops:
  0.6 3.0 %collective-permute-start = (bf16[8,1024]{1,0:T(8,128)(2,1)}, bf16[8,1024]{1,0:T(8,128)(2,1)S(1)}, u32[]{:S(2)}, u32[]{:S(2)}) collective-permute-start(bf16[8,1024]{1,0:T(8,128)(2,1)} %x_hbm.1), channel_id=1, source_target_pairs={{0,2},{2,0},{1,3},{3,1},{4,6},{6,4},{5,7},{7,5},{8,10},{10,8},{9,1... | collective-permute-start | bytes 49160 | tf_op jit(solution)/shard_map/ppermute | solution.py:231
  3.6 1.6 %collective-permute-start.5 = (bf16[8,1024]{1,0:T(8,128)(2,1)}, bf16[8,1024]{1,0:T(8,128)(2,1)S(1)}, u32[]{:S(2)}, u32[]{:S(2)}) collective-permute-start(bf16[8,1024]{1,0:T(8,128)(2,1)} %x_hbm.1), channel_id=1, source_target_pairs={{0,8},{4,12},{8,16},{12,20},{16,24},{20,28},{24,0},{28,4},{1,9},{5... | collective-permute-start | bytes 49160 | tf_op jit(solution)/shard_map/ppermute | solution.py:228
  5.2 2.6 %collective-permute-start.6 = (bf16[8,1024]{1,0:T(8,128)(2,1)}, bf16[8,1024]{1,0:T(8,128)(2,1)S(1)}, u32[]{:S(2)}, u32[]{:S(2)}) collective-permute-start(bf16[8,1024]{1,0:T(8,128)(2,1)} %x_hbm.1), channel_id=1, source_target_pairs={{0,16},{4,20},{8,24},{12,28},{16,0},{20,4},{24,8},{28,12},{1,17},{... | collective-permute-start | bytes 49160 | tf_op jit(solution)/shard_map/ppermute | solution.py:228
  7.8 1.3 %collective-permute-start.7 = (bf16[8,1024]{1,0:T(8,128)(2,1)}, bf16[8,1024]{1,0:T(8,128)(2,1)S(1)}, u32[]{:S(2)}, u32[]{:S(2)}) collective-permute-start(bf16[8,1024]{1,0:T(8,128)(2,1)} %x_hbm.1), channel_id=1, source_target_pairs={{0,24},{4,28},{8,0},{12,4},{16,8},{20,12},{24,16},{28,20},{1,25},{... | collective-permute-start | bytes 49160 | tf_op jit(solution)/shard_map/ppermute | solution.py:228
  9.8 2.0 %mirror.1 = (f32[8,4096]{1,0:T(8,128)S(1)}, f32[8,4096]{1,0:T(8,128)S(1)}, bf16[256,128,128]{2,1,0:T(8,128)(2,1)S(1)}, bf16[8,1024]{1,0:T(8,128)(2,1)S(1)}) custom-call(s32[1,1]{1,0:T(1,128)S(6)} %copy.10.counts, s32[1,256]{1,0:T(1,128)} %bitcast.6, s32[1,256]{1,0:T(1,128)} %bitcast.8, bf16[256,128,128]{2,1,0:T(8,128)(2,1)} %bitcast.5, ...), custom_call_target="tpu_custom_call" | custom-call | flops 134217728 | bytes 8388608 | tf_op jit(solution)/shard_map/mirror/pallas_call | solution.py:253
  11.8 0.1 collective-permute-start.1
  11.9 0.0 collective-permute-done.7
  12.0 0.5 %collective-permute-start.8 = (bf16[8,4096]{1,0:T(8,128)(2,1)S(1)}, bf16[8,4096]{1,0:T(8,128)(2,1)S(1)}, u32[]{:S(2)}, u32[]{:S(2)}) collective-permute-start(bf16[8,4096]{1,0:T(8,128)(2,1)S(1)} %constant_dynamic-update-slice_fusion.near), channel_id=1, source_target_pairs={{0,4},{4,0},{8,12},{12,8},{16,20},{20,16},{24,28},{28,24},{1,5},{5... | collective-permute-start | bytes 196616 | tf_op jit(solution)/shard_map/ppermute | solution.py:225
  12.5 0.7 %collective-permute-done.1.theirs = f32[8,4096]{1,0:T(8,128)S(1)} collective-permute-done((f32[8,4096]{1,0:T(8,128)S(1)}, f32[8,4096]{1,0:T(8,128)S(1)}, u32[]{:S(2)}, u32[]{:S(2)}) %collective-permute-start.1) | collective-permute-done | bytes 131104 | tf_op jit(solution)/shard_map/ppermute | solution.py:225
  13.2 3.0 %collective-permute-start.2 = (f32[8,1024]{1,0:T(8,128)S(1)}, f32[8,1024]{1,0:T(8,128)S(1)}, u32[]{:S(2)}, u32[]{:S(2)}) collective-permute-start(f32[8,1024]{1,0:T(8,128)S(1)} %get-tuple-element.17), channel_id=1, source_target_pairs={{0,8},{4,12},{8,16},{12,20},{16,24},{20,28},{24,0},{28,4},{1,9},{5... | collective-permute-start | bytes 98312 | tf_op jit(solution)/shard_map/ppermute | solution.py:228
  16.3 1.9 %collective-permute-start.3 = (f32[8,1024]{1,0:T(8,128)S(1)}, f32[8,1024]{1,0:T(8,128)S(1)}, u32[]{:S(2)}, u32[]{:S(2)}) collective-permute-start(f32[8,1024]{1,0:T(8,128)S(1)} %get-tuple-element.18), channel_id=1, source_target_pairs={{0,16},{4,20},{8,24},{12,28},{16,0},{20,4},{24,8},{28,12},{1,17},{... | collective-permute-start | bytes 98312 | tf_op jit(solution)/shard_map/ppermute | solution.py:228
  18.2 2.2 %collective-permute-start.4 = (f32[8,1024]{1,0:T(8,128)S(1)}, f32[8,1024]{1,0:T(8,128)S(1)}, u32[]{:S(2)}, u32[]{:S(2)}) collective-permute-start(f32[8,1024]{1,0:T(8,128)S(1)} %get-tuple-element.19), channel_id=1, source_target_pairs={{0,24},{4,28},{8,0},{12,4},{16,8},{20,12},{24,16},{28,20},{1,25},{... | collective-permute-start | bytes 98312 | tf_op jit(solution)/shard_map/ppermute | solution.py:228
  20.4 1.5 %collective-permute-start.9 = (bf16[8,1024]{1,0:T(8,128)(2,1)S(1)}, bf16[8,1024]{1,0:T(8,128)(2,1)S(1)}, u32[]{:S(2)}, u32[]{:S(2)}) collective-permute-start(bf16[8,1024]{1,0:T(8,128)(2,1)S(1)} %copy-done), channel_id=1, source_target_pairs={{0,1},{1,0},{2,3},{3,2},{4,5},{5,4},{6,7},{7,6},{8,9},{9,8},{10,11... | collective-permute-start | bytes 49160 | tf_op jit(solution)/shard_map/ppermute | solution.py:234
  22.0 0.5 %collective-permute-start.10 = (bf16[8,1024]{1,0:T(8,128)(2,1)S(1)}, bf16[8,1024]{1,0:T(8,128)(2,1)S(1)}, u32[]{:S(2)}, u32[]{:S(2)}) collective-permute-start(bf16[8,1024]{1,0:T(8,128)(2,1)S(1)} %collective-permute-done.refs_0_.refs_7_), channel_id=1, source_target_pairs={{0,1},{1,0},{2,3},{3,2},{4,5},{5,4},{6,7},{7,6},{8,9},{9,8},{10,11... | collective-permute-start | bytes 49160 | tf_op jit(solution)/shard_map/ppermute | solution.py:234
  22.5 1.5 %forward.1 = (f32[8,1024]{1,0:T(8,128)S(1)}, f32[8,1024]{1,0:T(8,128)S(1)}) custom-call(s32[1,1]{1,0:T(1,128)S(6)} %copy.10.counts, s32[1,256]{1,0:T(1,128)} %bitcast.7, s32[1,256]{1,0:T(1,128)} %bitcast.9, bf16[256,128,128]{2,1,0:T(8,128)(2,1)S(1)} %get-tuple-element.20.tiles, bf16[8,4096]{1,0:T(8,128)(2,1)S(1)} %constant_dynamic-update-slice_fusion.near, ...), custom_call_target="tpu_custom_call" | custom-call | flops 134217728 | bytes 8388608 | tf_op jit(solution)/shard_map/forward/pallas_call | solution.py:278
  24.0 0.2 collective-permute-done.9.refs_8_
  24.2 1.5 %collective-permute-done.10.refs_9_ = bf16[8,1024]{1,0:T(8,128)(2,1)S(1)} collective-permute-done((bf16[8,1024]{1,0:T(8,128)(2,1)S(1)}, bf16[8,1024]{1,0:T(8,128)(2,1)S(1)}, u32[]{:S(2)}, u32[]{:S(2)}) %collective-permute-start.10) | collective-permute-done | bytes 16416 | tf_op jit(solution)/shard_map/ppermute | solution.py:234
  25.7 0.0 collective-permute-done.2.refs_1_
  25.7 0.0 collective-permute-done.3.refs_2_
  25.7 0.0 collective-permute-done.4.refs_3_
  25.7 0.4 %gram.1 = (f32[8,1024]{1,0:T(8,128)S(1)}, f32[8,16]{1,0:T(8,128)S(1)}) custom-call(f32[8,1024]{1,0:T(8,128)S(1)} %get-tuple-element.16.refs_0_, f32[8,1024]{1,0:T(8,128)S(1)} %collective-permute-done.2.refs_1_, f32[8,1024]{1,0:T(8,128)S(1)} %collective-permute-done.3.refs_2_, f32[8,1024]{1,0:T(8,128)S(1)} %collective-permute-done.4.refs_3_, ...), custom_call_target="tpu_custom_call" | custom-call | tf_op jit(solution)/shard_map/gram/pallas_call | solution.py:295
  26.1 1.2 %collective-permute-done.12 = f32[8,16]{1,0:T(8,128)S(1)} collective-permute-done((f32[8,16]{1,0:T(8,128)S(1)}, f32[8,16]{1,0:T(8,128)S(1)}, u32[]{:S(2)}, u32[]{:S(2)}) %collective-permute-start.12) | collective-permute-done | bytes 544 | tf_op jit(solution)/shard_map/ppermute | solution.py:314
  27.3 0.3 collective-permute-start.16
  27.6 1.9 %collective-permute-start.15 = (f32[8,16]{1,0:T(8,128)S(1)}, f32[8,16]{1,0:T(8,128)S(1)}, u32[]{:S(2)}, u32[]{:S(2)}) collective-permute-start(f32[8,16]{1,0:T(8,128)S(1)} %add.22), channel_id=1, source_target_pairs={{0,18},{2,16},{4,28},{6,30},{8,26},{10,24},{12,20},{14,22},{16,2},... | collective-permute-start | bytes 1544 | tf_op jit(solution)/shard_map/ppermute | solution.py:324
  29.4 0.9 %collective-permute-start.13 = (f32[8,16]{1,0:T(8,128)S(1)}, f32[8,16]{1,0:T(8,128)S(1)}, u32[]{:S(2)}, u32[]{:S(2)}) collective-permute-start(f32[8,16]{1,0:T(8,128)S(1)} %add.22), channel_id=1, source_target_pairs={{0,2},{2,0},{4,12},{6,14},{8,10},{10,8},{12,4},{14,6},{16,18},{18,... | collective-permute-start | bytes 1544 | tf_op jit(solution)/shard_map/ppermute | solution.py:324
  30.4 3.7 %collective-permute-start.14 = (f32[8,16]{1,0:T(8,128)S(1)}, f32[8,16]{1,0:T(8,128)S(1)}, u32[]{:S(2)}, u32[]{:S(2)}) collective-permute-start(f32[8,16]{1,0:T(8,128)S(1)} %add.22), channel_id=1, source_target_pairs={{0,10},{2,8},{4,20},{6,22},{8,2},{10,0},{12,28},{14,30},{16,26},{1... | collective-permute-start | bytes 1544 | tf_op jit(solution)/shard_map/ppermute | solution.py:324
  34.0 0.2 collective-permute-start.11
  34.3 0.0 collective-permute-done.16
  34.3 1.3 %collective-permute-done.14 = f32[8,16]{1,0:T(8,128)S(1)} collective-permute-done((f32[8,16]{1,0:T(8,128)S(1)}, f32[8,16]{1,0:T(8,128)S(1)}, u32[]{:S(2)}, u32[]{:S(2)}) %collective-permute-start.14) | collective-permute-done | bytes 544 | tf_op jit(solution)/shard_map/ppermute | solution.py:324
  35.6 2.3 %collective-permute-done.11 = f32[8,1024]{1,0:T(8,128)S(1)} collective-permute-done((f32[8,1024]{1,0:T(8,128)S(1)}, f32[8,1024]{1,0:T(8,128)S(1)}, u32[]{:S(2)}, u32[]{:S(2)}) %collective-permute-start.11) | collective-permute-done | bytes 32800 | tf_op jit(solution)/shard_map/ppermute | solution.py:231
  38.0 0.6 %add_convert_fusion = bf16[8,1024]{1,0:T(8,128)(2,1)} fusion(f32[8,1024]{1,0:T(8,128)S(1)} %get-tuple-element.24, f32[8,1024]{1,0:T(8,128)S(1)} %collective-permute-done.11), kind=kLoop, calls=%fused_computation | loop fusion | flops 16384 | bytes 81920 | tf_op jit(solution)/shard_map/convert_element_type | solution.py:307
  38.6 0.6 %add_bitcast_fusion = f32[16,8]{0,1:T(8,128)} fusion(f32[8,16]{1,0:T(8,128)S(1)} %collective-permute-done.17, f32[8,16]{1,0:T(8,128)S(1)} %add.22, f32[8,16]{1,0:T(8,128)S(1)} %multiply_add_fusion), kind=kLoop, calls=%fused_computation.5 | loop fusion | flops 256 | bytes 2048 | tf_op jit(solution)/shard_map/transpose | solution.py:306
  (18 shorter events, 0.1 us)
Async XLA Ops:
  0.6 19.8 %copy-start = (bf16[8,1024]{1,0:T(8,128)(2,1)S(1)}, bf16[8,1024]{1,0:T(8,128)(2,1)}, u32[]{:S(2)}) copy-start(bf16[8,1024]{1,0:T(8,128)(2,1)} %x_hbm.1) | copy-start | bytes 49156
  0.6 9.2 %collective-permute-start = (bf16[8,1024]{1,0:T(8,128)(2,1)}, bf16[8,1024]{1,0:T(8,128)(2,1)S(1)}, u32[]{:S(2)}, u32[]{:S(2)}) collective-permute-start(bf16[8,1024]{1,0:T(8,128)(2,1)} %x_hbm.1), channel_id=1, source_target_pairs={{0,2},{2,0},{1,3},{3,1},{4,6},{6,4},{5,7},{7,5},{8,10},{10,8},{9,1... | collective-permute-start | bytes 49160 | tf_op jit(solution)/shard_map/ppermute | solution.py:231
  3.6 8.3 %collective-permute-start.5 = (bf16[8,1024]{1,0:T(8,128)(2,1)}, bf16[8,1024]{1,0:T(8,128)(2,1)S(1)}, u32[]{:S(2)}, u32[]{:S(2)}) collective-permute-start(bf16[8,1024]{1,0:T(8,128)(2,1)} %x_hbm.1), channel_id=1, source_target_pairs={{0,8},{4,12},{8,16},{12,20},{16,24},{20,28},{24,0},{28,4},{1,9},{5... | collective-permute-start | bytes 49160 | tf_op jit(solution)/shard_map/ppermute | solution.py:228
  5.2 6.7 %collective-permute-start.6 = (bf16[8,1024]{1,0:T(8,128)(2,1)}, bf16[8,1024]{1,0:T(8,128)(2,1)S(1)}, u32[]{:S(2)}, u32[]{:S(2)}) collective-permute-start(bf16[8,1024]{1,0:T(8,128)(2,1)} %x_hbm.1), channel_id=1, source_target_pairs={{0,16},{4,20},{8,24},{12,28},{16,0},{20,4},{24,8},{28,12},{1,17},{... | collective-permute-start | bytes 49160 | tf_op jit(solution)/shard_map/ppermute | solution.py:228
  7.8 4.1 %collective-permute-start.7 = (bf16[8,1024]{1,0:T(8,128)(2,1)}, bf16[8,1024]{1,0:T(8,128)(2,1)S(1)}, u32[]{:S(2)}, u32[]{:S(2)}) collective-permute-start(bf16[8,1024]{1,0:T(8,128)(2,1)} %x_hbm.1), channel_id=1, source_target_pairs={{0,24},{4,28},{8,0},{12,4},{16,8},{20,12},{24,16},{28,20},{1,25},{... | collective-permute-start | bytes 49160 | tf_op jit(solution)/shard_map/ppermute | solution.py:228
  11.8 1.4 %collective-permute-start.1 = (f32[8,4096]{1,0:T(8,128)S(1)}, f32[8,4096]{1,0:T(8,128)S(1)}, u32[]{:S(2)}, u32[]{:S(2)}) collective-permute-start(f32[8,4096]{1,0:T(8,128)S(1)} %get-tuple-element.15), channel_id=1, source_target_pairs={{0,4},{4,0},{8,12},{12,8},{16,20},{20,16},{24,28},{28,24},{1,5},{5... | collective-permute-start | bytes 393224 | tf_op jit(solution)/shard_map/ppermute | solution.py:225
  12.0 10.0 %collective-permute-start.8 = (bf16[8,4096]{1,0:T(8,128)(2,1)S(1)}, bf16[8,4096]{1,0:T(8,128)(2,1)S(1)}, u32[]{:S(2)}, u32[]{:S(2)}) collective-permute-start(bf16[8,4096]{1,0:T(8,128)(2,1)S(1)} %constant_dynamic-update-slice_fusion.near), channel_id=1, source_target_pairs={{0,4},{4,0},{8,12},{12,8},{16,20},{20,16},{24,28},{28,24},{1,5},{5... | collective-permute-start | bytes 196616 | tf_op jit(solution)/shard_map/ppermute | solution.py:225
  13.2 12.5 %collective-permute-start.2 = (f32[8,1024]{1,0:T(8,128)S(1)}, f32[8,1024]{1,0:T(8,128)S(1)}, u32[]{:S(2)}, u32[]{:S(2)}) collective-permute-start(f32[8,1024]{1,0:T(8,128)S(1)} %get-tuple-element.17), channel_id=1, source_target_pairs={{0,8},{4,12},{8,16},{12,20},{16,24},{20,28},{24,0},{28,4},{1,9},{5... | collective-permute-start | bytes 98312 | tf_op jit(solution)/shard_map/ppermute | solution.py:228
  16.3 9.4 %collective-permute-start.3 = (f32[8,1024]{1,0:T(8,128)S(1)}, f32[8,1024]{1,0:T(8,128)S(1)}, u32[]{:S(2)}, u32[]{:S(2)}) collective-permute-start(f32[8,1024]{1,0:T(8,128)S(1)} %get-tuple-element.18), channel_id=1, source_target_pairs={{0,16},{4,20},{8,24},{12,28},{16,0},{20,4},{24,8},{28,12},{1,17},{... | collective-permute-start | bytes 98312 | tf_op jit(solution)/shard_map/ppermute | solution.py:228
  18.2 7.5 %collective-permute-start.4 = (f32[8,1024]{1,0:T(8,128)S(1)}, f32[8,1024]{1,0:T(8,128)S(1)}, u32[]{:S(2)}, u32[]{:S(2)}) collective-permute-start(f32[8,1024]{1,0:T(8,128)S(1)} %get-tuple-element.19), channel_id=1, source_target_pairs={{0,24},{4,28},{8,0},{12,4},{16,8},{20,12},{24,16},{28,20},{1,25},{... | collective-permute-start | bytes 98312 | tf_op jit(solution)/shard_map/ppermute | solution.py:228
  20.4 3.7 %collective-permute-start.9 = (bf16[8,1024]{1,0:T(8,128)(2,1)S(1)}, bf16[8,1024]{1,0:T(8,128)(2,1)S(1)}, u32[]{:S(2)}, u32[]{:S(2)}) collective-permute-start(bf16[8,1024]{1,0:T(8,128)(2,1)S(1)} %copy-done), channel_id=1, source_target_pairs={{0,1},{1,0},{2,3},{3,2},{4,5},{5,4},{6,7},{7,6},{8,9},{9,8},{10,11... | collective-permute-start | bytes 49160 | tf_op jit(solution)/shard_map/ppermute | solution.py:234
  22.0 3.7 %collective-permute-start.10 = (bf16[8,1024]{1,0:T(8,128)(2,1)S(1)}, bf16[8,1024]{1,0:T(8,128)(2,1)S(1)}, u32[]{:S(2)}, u32[]{:S(2)}) collective-permute-start(bf16[8,1024]{1,0:T(8,128)(2,1)S(1)} %collective-permute-done.refs_0_.refs_7_), channel_id=1, source_target_pairs={{0,1},{1,0},{2,3},{3,2},{4,5},{5,4},{6,7},{7,6},{8,9},{9,8},{10,11... | collective-permute-start | bytes 49160 | tf_op jit(solution)/shard_map/ppermute | solution.py:234
  26.1 1.2 %collective-permute-start.12 = (f32[8,16]{1,0:T(8,128)S(1)}, f32[8,16]{1,0:T(8,128)S(1)}, u32[]{:S(2)}, u32[]{:S(2)}) collective-permute-start(f32[8,16]{1,0:T(8,128)S(1)} %get-tuple-element.25), channel_id=1, source_target_pairs={{0,4},{4,0},{8,12},{12,8},{16,20},{20,16},{24,28},{28,24},{1,5},{5... | collective-permute-start | bytes 1544 | tf_op jit(solution)/shard_map/ppermute | solution.py:314
  27.3 7.0 %collective-permute-start.16 = (f32[8,16]{1,0:T(8,128)S(1)}, f32[8,16]{1,0:T(8,128)S(1)}, u32[]{:S(2)}, u32[]{:S(2)}) collective-permute-start(f32[8,16]{1,0:T(8,128)S(1)} %add.22), channel_id=1, source_target_pairs={{0,26},{2,24},{4,30},{6,28},{8,18},{10,16},{12,22},{14,20},{16,10}... | collective-permute-start | bytes 1544 | tf_op jit(solution)/shard_map/ppermute | solution.py:324
  27.6 6.7 %collective-permute-start.15 = (f32[8,16]{1,0:T(8,128)S(1)}, f32[8,16]{1,0:T(8,128)S(1)}, u32[]{:S(2)}, u32[]{:S(2)}) collective-permute-start(f32[8,16]{1,0:T(8,128)S(1)} %add.22), channel_id=1, source_target_pairs={{0,18},{2,16},{4,28},{6,30},{8,26},{10,24},{12,20},{14,22},{16,2},... | collective-permute-start | bytes 1544 | tf_op jit(solution)/shard_map/ppermute | solution.py:324
  29.4 4.9 %collective-permute-start.13 = (f32[8,16]{1,0:T(8,128)S(1)}, f32[8,16]{1,0:T(8,128)S(1)}, u32[]{:S(2)}, u32[]{:S(2)}) collective-permute-start(f32[8,16]{1,0:T(8,128)S(1)} %add.22), channel_id=1, source_target_pairs={{0,2},{2,0},{4,12},{6,14},{8,10},{10,8},{12,4},{14,6},{16,18},{18,... | collective-permute-start | bytes 1544 | tf_op jit(solution)/shard_map/ppermute | solution.py:324
  30.4 5.3 %collective-permute-start.14 = (f32[8,16]{1,0:T(8,128)S(1)}, f32[8,16]{1,0:T(8,128)S(1)}, u32[]{:S(2)}, u32[]{:S(2)}) collective-permute-start(f32[8,16]{1,0:T(8,128)S(1)} %add.22), channel_id=1, source_target_pairs={{0,10},{2,8},{4,20},{6,22},{8,2},{10,0},{12,28},{14,30},{16,26},{1... | collective-permute-start | bytes 1544 | tf_op jit(solution)/shard_map/ppermute | solution.py:324
  34.0 3.9 %collective-permute-start.11 = (f32[8,1024]{1,0:T(8,128)S(1)}, f32[8,1024]{1,0:T(8,128)S(1)}, u32[]{:S(2)}, u32[]{:S(2)}) collective-permute-start(f32[8,1024]{1,0:T(8,128)S(1)} %get-tuple-element.23.refs_5_), channel_id=1, source_target_pairs={{0,2},{2,0},{1,3},{3,1},{4,6},{6,4},{5,7},{7,5},{8,10},{10,8},{9,1... | collective-permute-start | bytes 98312 | tf_op jit(solution)/shard_map/ppermute | solution.py:231
  35.6 2.9 %collective-permute-start.17 = (f32[8,16]{1,0:T(8,128)S(1)}, f32[8,16]{1,0:T(8,128)S(1)}, u32[]{:S(2)}, u32[]{:S(2)}) collective-permute-start(f32[8,16]{1,0:T(8,128)S(1)} %multiply_add_fusion), channel_id=1, source_target_pairs={{0,4},{4,0},{8,12},{12,8},{16,20},{20,16},{24,28},{28,24},{1,5},{5... | collective-permute-start | bytes 1544 | tf_op jit(solution)/shard_map/ppermute | solution.py:330

commit v4 on v3

--- a/solution.py
+++ b/solution.py
@@ -9,10 +9,11 @@
 from jax.sharding import PartitionSpec as P
 
 CHUNK = 32
-AHEAD = 2
+AHEAD = 4
+UNROLL = 128
 GROUP = 8
+VMEM = pl.BlockSpec(memory_space=pltpu.VMEM)
 SMEM = pl.BlockSpec(memory_space=pltpu.SMEM)
-VMEM = pl.BlockSpec(memory_space=pltpu.VMEM)
 HBM = pl.BlockSpec(memory_space=pltpu.HBM)
 F32 = jnp.float32
 HIGHEST = lax.Precision.HIGHEST
@@ -31,7 +32,7 @@
         high[first + q] = jnp.concatenate([zero, part], axis=0)
 
 
-def multiply_tiles(pick, forward, count, tiles, low, high, sums, arrive=None):
+def multiply_tiles(pick, forward, many, count, tiles, low, high, sums, arrive=None):
     slots = tiles.shape[0]
     tile = tiles.shape[-1]
     vlocal = sums[0].shape[1]
@@ -41,10 +42,10 @@
     def chunk(step, carry):
         if arrive is not None:
             arrive(step)
-        for g in range(CHUNK // (2 * GROUP)):
+        for g in range(many // (2 * GROUP)):
             results = []
             for u in range(GROUP):
-                s = step * CHUNK + g * 2 * GROUP + 2 * u
+                s = step * many + g * 2 * GROUP + 2 * u
                 in0, out0 = pick(s)
                 in1, out1 = pick(s + 1)
                 left = jnp.concatenate([low[in0], high[in1]], axis=1)
@@ -62,8 +63,8 @@
                 b[out1] += both[vlocal:]
         return carry
 
-    assert slots % CHUNK == 0
-    lax.fori_loop(0, pl.cdiv(count, CHUNK), chunk, 0)
+    assert slots % many == 0
+    lax.fori_loop(0, pl.cdiv(count, many), chunk, 0)
 
 
 def places(rows, cols, span, stretch):
@@ -93,26 +94,22 @@
     rows, cols, small, sems, low, high, *sums = refs
     tile = tiles.shape[-1]
     width = stretch * tile
-    count = counts[0, 0]
-    chunks = pl.cdiv(count, CHUNK)
 
     def load(step):
         at = pl.ds(step * CHUNK, CHUNK)
         return pltpu.make_async_copy(tiles_hbm.at[at], tiles.at[at], sems.at[step])
 
-    def start(step):
-        @pl.when(step < chunks)
-        def _():
-            load(step).start()
-
     copies = start_copies(small, (x_hbm, x), (rows_hbm, rows), (cols_hbm, cols))
-    for step in range(AHEAD):
-        start(step)
+    ahead = min(AHEAD, tiles.shape[0] // CHUNK)
+    for step in range(ahead):
+        load(step).start()
     z, core, j = position()
     for t in range(1, ncol):
         place_block(low, high, blocks[t - 1], lax.rem(j + ncol - t, ncol) * stretch, stretch, tile)
     for copy in copies:
         copy.wait()
+    count = counts[0, 0]
+    chunks = pl.cdiv(count, CHUNK)
     place_block(low, high, x, j * stretch, stretch, tile)
     low[span] = jnp.zeros(low.shape[1:], low.dtype)
     high[span] = jnp.zeros(high.shape[1:], high.dtype)
@@ -124,9 +121,18 @@
 
     def arrive(step):
         load(step).wait()
-        start(step + AHEAD)
-
-    multiply_tiles(pick, False, count, tiles, low, high, sums, arrive)
+
+        @pl.when(step + ahead < chunks)
+        def _():
+            load(step + ahead).start()
+
+    multiply_tiles(pick, False, CHUNK, count, tiles, low, high, sums, arrive)
+    for step in range(1, ahead):
+
+        @pl.when(step >= chunks)
+        def _():
+            load(step).wait()
+
     for s in range(nz):
         target = 2 * lax.rem(z + s, nz)
         for out, c in ((mine, core), (other, 1 - core)):
@@ -145,7 +151,6 @@
     copies = start_copies(small, (rows_hbm, rows), (cols_hbm, cols))
     tile = tiles.shape[-1]
     width = stretch * tile
-    count = counts[0, 0]
     z, core, j = position()
     for s in range(nz):
         source = 2 * lax.rem(z + nz - s, nz)
@@ -154,6 +159,7 @@
     dead = 2 * nz * stretch
     for copy in copies:
         copy.wait()
+    count = counts[0, 0]
     low[dead] = jnp.zeros(low.shape[1:], low.dtype)
     high[dead] = jnp.zeros(high.shape[1:], high.dtype)
     get = places(rows, cols, span, stretch)
@@ -162,7 +168,7 @@
         _, _, row_place, col_place = get(s)
         return jnp.where(s < count, col_place, dead), row_place
 
-    multiply_tiles(pick, True, count, tiles, low, high, sums)
+    multiply_tiles(pick, True, UNROLL, count, tiles, low, high, sums)
     for t in range(ncol):
         first = lax.rem(j + t, ncol) * stretch
         for q in range(stretch):
@@ -308,26 +314,29 @@
 
 
 def all_sum(share, nz, ncol):
-    if nz * ncol > 8 or nz & (nz - 1):
+    if nz * ncol > 8 or nz & (nz - 1) or nz == 1:
         return lax.psum(share, ("row", "col"))
     nrow = 2 * nz
-    share = share + lax.ppermute(share, "row", [(a, a ^ 1) for a in range(nrow)])
-    shifts = sorted(((s, t) for s in range(nz) for t in range(ncol)), key=sum)[1:]
-    got = None
-    for n in range(0, len(shifts), 2):
-        pair = shifts[n : n + 2]
+
+    def send(x, pair):
         perm = []
         for a in range(nrow):
             for b in range(ncol):
-                s, t = pair[(a % 2) % len(pair)]
+                s, t = pair[a % 2]
                 perm.append((a * ncol + b, (a ^ (2 * s)) * ncol + (b + t) % ncol))
-        part = lax.ppermute(share, ("row", "col"), perm)
-        if len(pair) == 1:
-            part = part * 0.5
-        got = part if got is None else got + part
-    if got is None:
-        return share
-    return share + got + lax.ppermute(got, "row", [(a, a ^ 1) for a in range(nrow)])
+        return lax.ppermute(x, ("row", "col"), perm)
+
+    def swap(x):
+        return lax.ppermute(x, "row", [(a, a ^ 1) for a in range(nrow)])
+
+    got = send(share, ((1, 0), (1, 0)))
+    share = share + swap(share)
+    shifts = [(s, t) for s in range(nz) for t in range(ncol) if (s, t) not in ((0, 0), (1, 0))]
+    for n in range(0, len(shifts) - 1, 2):
+        got = got + send(share, shifts[n : n + 2])
+    if len(shifts) % 2:
+        got = got + 0.5 * send(share, shifts[-1:] * 2)
+    return share + got + swap(got)
 
 
 def solution(mesh):

time: 39.4 us -> 33.5 us (0.85)
  starting transfers between devices: 25.3 us -> 21 us
  waiting for transfers between devices: 7.26 us -> 4.95 us
  Pallas kernels: 3.93 us -> 4.7 us
    ppermute x6, starting transfers between devices: 6.75 us -> 2.95 us  [the longest x4 2.55 us: send(): return lax.ppermute(x, ('row', 'col'), perm)]
    ppermute x2, waiting for transfers between devices: 2.32 us -> 0.14 us  [col_shift(): return lax.ppermute(x, 'col', [(a, (a + t) % ncol) for a in range(ncol)])]
    ppermute x6, starting transfers between devices: 12.7 us -> 10.6 us  [z_shift(): lax.ppermute(x, 'row', [(a, (a + 2 * s) % nrow) for a in range(nrow)])]
    ppermute x2, starting transfers between devices: 3.24 us -> 4.81 us  [col_shift(): return lax.ppermute(x, 'col', [(a, (a + t) % ncol) for a in range(ncol)])]
    ppermute x2, waiting for transfers between devices: 1.69 us -> 1.24 us  [vec_shift(): return lax.ppermute(x, 'vec', [(a, (a + t) % nvec) for a in range(nvec)])]
    pallas_call x1, Pallas kernels: 1.54 us -> 1.97 us  [shards(): pl.pallas_call(functools.partial(forward_kernel, step), out_shape=[block]...]
  transfers between devices with their start and end apart: 18 -> 18, of which waited for: 6 -> 8; matrix products, arithmetic and copies ran while one was open for 2% -> 2% of each run, Pallas kernels for 9% -> 13%
where the time goes in v4:
time: 33.5 us; the launch traced here: 33.2 us
  starting transfers between devices  21 us (63%)
  waiting for transfers between devices  4.95 us (15%)
  Pallas kernels  4.7 us (14%)
  between operations  1.41 us (4%)
  other arithmetic  1.22 us (4%)
    ppermute x6, starting transfers between devices, z_shift(): lax.ppermute(x, 'row', [(a, (a + 2 * s) % nrow) for a in range(nrow)])  10.6 us
    ppermute x2, starting transfers between devices, col_shift(): return lax.ppermute(x, 'col', [(a, (a + t) % ncol) for a in range(ncol)])  4.81 us
    ppermute x4, starting transfers between devices, send(): return lax.ppermute(x, ('row', 'col'), perm)  2.55 us
    pallas_call x1, Pallas kernels, shards(): pl.pallas_call(functools.partial(mirror_kernel, step), out_shape=[ring, r...  2.32 us
    ppermute x2, starting transfers between devices, vec_shift(): return lax.ppermute(x, 'vec', [(a, (a + t) % nvec) for a in range(nvec)])  2.03 us
    pallas_call x1, Pallas kernels, shards(): pl.pallas_call(functools.partial(forward_kernel, step), out_shape=[block]...  1.97 us
    ppermute x4, waiting for transfers between devices, send(): return lax.ppermute(x, ('row', 'col'), perm)  1.58 us
    ppermute x2, waiting for transfers between devices, swap(): return lax.ppermute(x, 'row', [(a, a ^ 1) for a in range(nrow)])  1.25 us
  transfers between devices with their start and end apart: 18, of which 8 were waited for; matrix products, arithmetic and copies ran while one was open for 2% of the time, Pallas kernels for 13%

profile of v4, /device:TPU:0, one launch (start us, length us, event | category | flops | bytes accessed | tf_op | source)
XLA Modules:
  0.0 33.2 jit_solution(5046419855262865624)
XLA Ops:
  0.6 3.0 %collective-permute-start = (bf16[8,1024]{1,0:T(8,128)(2,1)}, bf16[8,1024]{1,0:T(8,128)(2,1)S(1)}, u32[]{:S(2)}, u32[]{:S(2)}) collective-permute-start(bf16[8,1024]{1,0:T(8,128)(2,1)} %x_hbm.1), channel_id=1, source_target_pairs={{0,2},{2,0},{1,3},{3,1},{4,6},{6,4},{5,7},{7,5},{8,10},{10,8},{9,1... | collective-permute-start | bytes 49160 | tf_op jit(solution)/shard_map/ppermute | solution.py:237
  3.6 1.6 %collective-permute-start.5 = (bf16[8,1024]{1,0:T(8,128)(2,1)}, bf16[8,1024]{1,0:T(8,128)(2,1)S(1)}, u32[]{:S(2)}, u32[]{:S(2)}) collective-permute-start(bf16[8,1024]{1,0:T(8,128)(2,1)} %x_hbm.1), channel_id=1, source_target_pairs={{0,8},{4,12},{8,16},{12,20},{16,24},{20,28},{24,0},{28,4},{1,9},{5... | collective-permute-start | bytes 49160 | tf_op jit(solution)/shard_map/ppermute | solution.py:234
  5.2 2.6 %collective-permute-start.6 = (bf16[8,1024]{1,0:T(8,128)(2,1)}, bf16[8,1024]{1,0:T(8,128)(2,1)S(1)}, u32[]{:S(2)}, u32[]{:S(2)}) collective-permute-start(bf16[8,1024]{1,0:T(8,128)(2,1)} %x_hbm.1), channel_id=1, source_target_pairs={{0,16},{4,20},{8,24},{12,28},{16,0},{20,4},{24,8},{28,12},{1,17},{... | collective-permute-start | bytes 49160 | tf_op jit(solution)/shard_map/ppermute | solution.py:234
  7.8 1.3 %collective-permute-start.7 = (bf16[8,1024]{1,0:T(8,128)(2,1)}, bf16[8,1024]{1,0:T(8,128)(2,1)S(1)}, u32[]{:S(2)}, u32[]{:S(2)}) collective-permute-start(bf16[8,1024]{1,0:T(8,128)(2,1)} %x_hbm.1), channel_id=1, source_target_pairs={{0,24},{4,28},{8,0},{12,4},{16,8},{20,12},{24,16},{28,20},{1,25},{... | collective-permute-start | bytes 49160 | tf_op jit(solution)/shard_map/ppermute | solution.py:234
  9.8 0.0 collective-permute-done.refs_0_.refs_7_
  9.8 2.3 %mirror.1 = (f32[8,4096]{1,0:T(8,128)S(1)}, f32[8,4096]{1,0:T(8,128)S(1)}, bf16[256,128,128]{2,1,0:T(8,128)(2,1)S(1)}, bf16[8,1024]{1,0:T(8,128)(2,1)S(1)}) custom-call(s32[1,1]{1,0:T(1,128)S(6)} %copy.10.counts, s32[1,256]{1,0:T(1,128)} %bitcast.6, s32[1,256]{1,0:T(1,128)} %bitcast.8, bf16[256,128,128]{2,1,0:T(8,128)(2,1)} %bitcast.5, ...), custom_call_target="tpu_custom_call" | custom-call | flops 134217728 | bytes 8388608 | tf_op jit(solution)/shard_map/mirror/pallas_call | solution.py:259
  12.1 0.1 collective-permute-start.1
  12.3 0.0 collective-permute-done.6
  12.3 0.0 collective-permute-done.7
  12.3 0.5 %collective-permute-start.8 = (bf16[8,4096]{1,0:T(8,128)(2,1)S(1)}, bf16[8,4096]{1,0:T(8,128)(2,1)S(1)}, u32[]{:S(2)}, u32[]{:S(2)}) collective-permute-start(bf16[8,4096]{1,0:T(8,128)(2,1)S(1)} %constant_dynamic-update-slice_fusion.near), channel_id=1, source_target_pairs={{0,4},{4,0},{8,12},{12,8},{16,20},{20,16},{24,28},{28,24},{1,5},{5... | collective-permute-start | bytes 196616 | tf_op jit(solution)/shard_map/ppermute | solution.py:231
  12.8 0.7 %collective-permute-done.1.theirs = f32[8,4096]{1,0:T(8,128)S(1)} collective-permute-done((f32[8,4096]{1,0:T(8,128)S(1)}, f32[8,4096]{1,0:T(8,128)S(1)}, u32[]{:S(2)}, u32[]{:S(2)}) %collective-permute-start.1) | collective-permute-done | bytes 131104 | tf_op jit(solution)/shard_map/ppermute | solution.py:231
  13.6 1.6 %collective-permute-start.2 = (f32[8,1024]{1,0:T(8,128)S(1)}, f32[8,1024]{1,0:T(8,128)S(1)}, u32[]{:S(2)}, u32[]{:S(2)}) collective-permute-start(f32[8,1024]{1,0:T(8,128)S(1)} %get-tuple-element.17), channel_id=1, source_target_pairs={{0,8},{4,12},{8,16},{12,20},{16,24},{20,28},{24,0},{28,4},{1,9},{5... | collective-permute-start | bytes 98312 | tf_op jit(solution)/shard_map/ppermute | solution.py:234
  15.1 1.2 %collective-permute-start.3 = (f32[8,1024]{1,0:T(8,128)S(1)}, f32[8,1024]{1,0:T(8,128)S(1)}, u32[]{:S(2)}, u32[]{:S(2)}) collective-permute-start(f32[8,1024]{1,0:T(8,128)S(1)} %get-tuple-element.18), channel_id=1, source_target_pairs={{0,16},{4,20},{8,24},{12,28},{16,0},{20,4},{24,8},{28,12},{1,17},{... | collective-permute-start | bytes 98312 | tf_op jit(solution)/shard_map/ppermute | solution.py:234
  16.4 2.2 %collective-permute-start.4 = (f32[8,1024]{1,0:T(8,128)S(1)}, f32[8,1024]{1,0:T(8,128)S(1)}, u32[]{:S(2)}, u32[]{:S(2)}) collective-permute-start(f32[8,1024]{1,0:T(8,128)S(1)} %get-tuple-element.19), channel_id=1, source_target_pairs={{0,24},{4,28},{8,0},{12,4},{16,8},{20,12},{24,16},{28,20},{1,25},{... | collective-permute-start | bytes 98312 | tf_op jit(solution)/shard_map/ppermute | solution.py:234
  18.6 1.5 %collective-permute-start.9 = (bf16[8,1024]{1,0:T(8,128)(2,1)S(1)}, bf16[8,1024]{1,0:T(8,128)(2,1)S(1)}, u32[]{:S(2)}, u32[]{:S(2)}) collective-permute-start(bf16[8,1024]{1,0:T(8,128)(2,1)S(1)} %copy-done), channel_id=1, source_target_pairs={{0,1},{1,0},{2,3},{3,2},{4,5},{5,4},{6,7},{7,6},{8,9},{9,8},{10,11... | collective-permute-start | bytes 49160 | tf_op jit(solution)/shard_map/ppermute | solution.py:240
  20.1 0.5 %collective-permute-start.10 = (bf16[8,1024]{1,0:T(8,128)(2,1)S(1)}, bf16[8,1024]{1,0:T(8,128)(2,1)S(1)}, u32[]{:S(2)}, u32[]{:S(2)}) collective-permute-start(bf16[8,1024]{1,0:T(8,128)(2,1)S(1)} %collective-permute-done.refs_0_.refs_7_), channel_id=1, source_target_pairs={{0,1},{1,0},{2,3},{3,2},{4,5},{5,4},{6,7},{7,6},{8,9},{9,8},{10,11... | collective-permute-start | bytes 49160 | tf_op jit(solution)/shard_map/ppermute | solution.py:240
  20.7 2.0 %forward.1 = (f32[8,1024]{1,0:T(8,128)S(1)}, f32[8,1024]{1,0:T(8,128)S(1)}) custom-call(s32[1,1]{1,0:T(1,128)S(6)} %copy.10.counts, s32[1,256]{1,0:T(1,128)} %bitcast.7, s32[1,256]{1,0:T(1,128)} %bitcast.9, bf16[256,128,128]{2,1,0:T(8,128)(2,1)S(1)} %get-tuple-element.20.tiles, bf16[8,4096]{1,0:T(8,128)(2,1)S(1)} %constant_dynamic-update-slice_fusion.near, ...), custom_call_target="tpu_custom_call" | custom-call | flops 134217728 | bytes 8388608 | tf_op jit(solution)/shard_map/forward/pallas_call | solution.py:284
  22.6 1.2 %collective-permute-done.10.refs_9_ = bf16[8,1024]{1,0:T(8,128)(2,1)S(1)} collective-permute-done((bf16[8,1024]{1,0:T(8,128)(2,1)S(1)}, bf16[8,1024]{1,0:T(8,128)(2,1)S(1)}, u32[]{:S(2)}, u32[]{:S(2)}) %collective-permute-start.10) | collective-permute-done | bytes 16416 | tf_op jit(solution)/shard_map/ppermute | solution.py:240
  23.9 0.4 %gram.1 = (f32[8,1024]{1,0:T(8,128)S(1)}, f32[8,16]{1,0:T(8,128)S(1)}) custom-call(f32[8,1024]{1,0:T(8,128)S(1)} %get-tuple-element.16.refs_0_, f32[8,1024]{1,0:T(8,128)S(1)} %collective-permute-done.2.refs_1_, f32[8,1024]{1,0:T(8,128)S(1)} %collective-permute-done.3.refs_2_, f32[8,1024]{1,0:T(8,128)S(1)} %collective-permute-done.4.refs_3_, ...), custom_call_target="tpu_custom_call" | custom-call | tf_op jit(solution)/shard_map/gram/pallas_call | solution.py:301
  24.3 1.2 %collective-permute-done.12 = f32[8,16]{1,0:T(8,128)S(1)} collective-permute-done((f32[8,16]{1,0:T(8,128)S(1)}, f32[8,16]{1,0:T(8,128)S(1)}, u32[]{:S(2)}, u32[]{:S(2)}) %collective-permute-start.12) | collective-permute-done | bytes 544 | tf_op jit(solution)/shard_map/ppermute | solution.py:330
  25.5 1.2 %collective-permute-start.16 = (f32[8,16]{1,0:T(8,128)S(1)}, f32[8,16]{1,0:T(8,128)S(1)}, u32[]{:S(2)}, u32[]{:S(2)}) collective-permute-start(f32[8,16]{1,0:T(8,128)S(1)} %add.22), channel_id=1, source_target_pairs={{0,24},{2,26},{4,30},{6,28},{8,16},{10,18},{12,22},{14,20},{16,8},... | collective-permute-start | bytes 1544 | tf_op jit(solution)/shard_map/ppermute | solution.py:327
  26.7 1.2 %collective-permute-start.15 = (f32[8,16]{1,0:T(8,128)S(1)}, f32[8,16]{1,0:T(8,128)S(1)}, u32[]{:S(2)}, u32[]{:S(2)}) collective-permute-start(f32[8,16]{1,0:T(8,128)S(1)} %add.22), channel_id=1, source_target_pairs={{0,16},{2,18},{4,22},{6,20},{8,24},{10,26},{12,30},{14,28},{16,0},... | collective-permute-start | bytes 1544 | tf_op jit(solution)/shard_map/ppermute | solution.py:327
  27.8 0.2 collective-permute-start.14
  28.0 1.8 %collective-permute-start.11 = (f32[8,1024]{1,0:T(8,128)S(1)}, f32[8,1024]{1,0:T(8,128)S(1)}, u32[]{:S(2)}, u32[]{:S(2)}) collective-permute-start(f32[8,1024]{1,0:T(8,128)S(1)} %get-tuple-element.23.refs_5_), channel_id=1, source_target_pairs={{0,2},{2,0},{1,3},{3,1},{4,6},{6,4},{5,7},{7,5},{8,10},{10,8},{9,1... | collective-permute-start | bytes 98312 | tf_op jit(solution)/shard_map/ppermute | solution.py:237
  29.8 1.0 %collective-permute-done.16 = f32[8,16]{1,0:T(8,128)S(1)} collective-permute-done((f32[8,16]{1,0:T(8,128)S(1)}, f32[8,16]{1,0:T(8,128)S(1)}, u32[]{:S(2)}, u32[]{:S(2)}) %collective-permute-start.16) | collective-permute-done | bytes 544 | tf_op jit(solution)/shard_map/ppermute | solution.py:327
  30.9 0.3 collective-permute-done.15
  31.2 0.3 collective-permute-done.14
  31.4 0.4 %collective-permute-start.17 = (f32[8,16]{1,0:T(8,128)S(1)}, f32[8,16]{1,0:T(8,128)S(1)}, u32[]{:S(2)}, u32[]{:S(2)}) collective-permute-start(f32[8,16]{1,0:T(8,128)S(1)} %add_add_fusion), channel_id=1, source_target_pairs={{0,4},{4,0},{8,12},{12,8},{16,20},{20,16},{24,28},{28,24},{1,5},{5... | collective-permute-start | bytes 1544 | tf_op jit(solution)/shard_map/ppermute | solution.py:330
  31.8 0.1 collective-permute-done.11
  32.0 0.6 %add_convert_fusion = bf16[8,1024]{1,0:T(8,128)(2,1)} fusion(f32[8,1024]{1,0:T(8,128)S(1)} %get-tuple-element.24, f32[8,1024]{1,0:T(8,128)S(1)} %collective-permute-done.11), kind=kLoop, calls=%fused_computation | loop fusion | flops 16384 | bytes 81920 | tf_op jit(solution)/shard_map/convert_element_type | solution.py:313
  32.6 0.1 collective-permute-done.17
  32.6 0.6 %add_bitcast_fusion = f32[16,8]{0,1:T(8,128)} fusion(f32[8,16]{1,0:T(8,128)S(1)} %collective-permute-done.17, f32[8,16]{1,0:T(8,128)S(1)} %add.22, f32[8,16]{1,0:T(8,128)S(1)} %add_add_fusion), kind=kLoop, calls=%fused_computation.5 | loop fusion | flops 256 | bytes 2048 | tf_op jit(solution)/shard_map/transpose | solution.py:312
  (18 shorter events, 0.1 us)
Async XLA Ops:
  0.6 18.0 %copy-start = (bf16[8,1024]{1,0:T(8,128)(2,1)S(1)}, bf16[8,1024]{1,0:T(8,128)(2,1)}, u32[]{:S(2)}) copy-start(bf16[8,1024]{1,0:T(8,128)(2,1)} %x_hbm.1) | copy-start | bytes 49156
  0.6 9.2 %collective-permute-start = (bf16[8,1024]{1,0:T(8,128)(2,1)}, bf16[8,1024]{1,0:T(8,128)(2,1)S(1)}, u32[]{:S(2)}, u32[]{:S(2)}) collective-permute-start(bf16[8,1024]{1,0:T(8,128)(2,1)} %x_hbm.1), channel_id=1, source_target_pairs={{0,2},{2,0},{1,3},{3,1},{4,6},{6,4},{5,7},{7,5},{8,10},{10,8},{9,1... | collective-permute-start | bytes 49160 | tf_op jit(solution)/shard_map/ppermute | solution.py:237
  3.6 8.6 %collective-permute-start.5 = (bf16[8,1024]{1,0:T(8,128)(2,1)}, bf16[8,1024]{1,0:T(8,128)(2,1)S(1)}, u32[]{:S(2)}, u32[]{:S(2)}) collective-permute-start(bf16[8,1024]{1,0:T(8,128)(2,1)} %x_hbm.1), channel_id=1, source_target_pairs={{0,8},{4,12},{8,16},{12,20},{16,24},{20,28},{24,0},{28,4},{1,9},{5... | collective-permute-start | bytes 49160 | tf_op jit(solution)/shard_map/ppermute | solution.py:234
  5.2 7.0 %collective-permute-start.6 = (bf16[8,1024]{1,0:T(8,128)(2,1)}, bf16[8,1024]{1,0:T(8,128)(2,1)S(1)}, u32[]{:S(2)}, u32[]{:S(2)}) collective-permute-start(bf16[8,1024]{1,0:T(8,128)(2,1)} %x_hbm.1), channel_id=1, source_target_pairs={{0,16},{4,20},{8,24},{12,28},{16,0},{20,4},{24,8},{28,12},{1,17},{... | collective-permute-start | bytes 49160 | tf_op jit(solution)/shard_map/ppermute | solution.py:234
  7.8 4.5 %collective-permute-start.7 = (bf16[8,1024]{1,0:T(8,128)(2,1)}, bf16[8,1024]{1,0:T(8,128)(2,1)S(1)}, u32[]{:S(2)}, u32[]{:S(2)}) collective-permute-start(bf16[8,1024]{1,0:T(8,128)(2,1)} %x_hbm.1), channel_id=1, source_target_pairs={{0,24},{4,28},{8,0},{12,4},{16,8},{20,12},{24,16},{28,20},{1,25},{... | collective-permute-start | bytes 49160 | tf_op jit(solution)/shard_map/ppermute | solution.py:234
  12.1 1.4 %collective-permute-start.1 = (f32[8,4096]{1,0:T(8,128)S(1)}, f32[8,4096]{1,0:T(8,128)S(1)}, u32[]{:S(2)}, u32[]{:S(2)}) collective-permute-start(f32[8,4096]{1,0:T(8,128)S(1)} %get-tuple-element.15), channel_id=1, source_target_pairs={{0,4},{4,0},{8,12},{12,8},{16,20},{20,16},{24,28},{28,24},{1,5},{5... | collective-permute-start | bytes 393224 | tf_op jit(solution)/shard_map/ppermute | solution.py:231
  12.3 7.8 %collective-permute-start.8 = (bf16[8,4096]{1,0:T(8,128)(2,1)S(1)}, bf16[8,4096]{1,0:T(8,128)(2,1)S(1)}, u32[]{:S(2)}, u32[]{:S(2)}) collective-permute-start(bf16[8,4096]{1,0:T(8,128)(2,1)S(1)} %constant_dynamic-update-slice_fusion.near), channel_id=1, source_target_pairs={{0,4},{4,0},{8,12},{12,8},{16,20},{20,16},{24,28},{28,24},{1,5},{5... | collective-permute-start | bytes 196616 | tf_op jit(solution)/shard_map/ppermute | solution.py:231
  13.6 10.3 %collective-permute-start.2 = (f32[8,1024]{1,0:T(8,128)S(1)}, f32[8,1024]{1,0:T(8,128)S(1)}, u32[]{:S(2)}, u32[]{:S(2)}) collective-permute-start(f32[8,1024]{1,0:T(8,128)S(1)} %get-tuple-element.17), channel_id=1, source_target_pairs={{0,8},{4,12},{8,16},{12,20},{16,24},{20,28},{24,0},{28,4},{1,9},{5... | collective-permute-start | bytes 98312 | tf_op jit(solution)/shard_map/ppermute | solution.py:234
  15.1 8.8 %collective-permute-start.3 = (f32[8,1024]{1,0:T(8,128)S(1)}, f32[8,1024]{1,0:T(8,128)S(1)}, u32[]{:S(2)}, u32[]{:S(2)}) collective-permute-start(f32[8,1024]{1,0:T(8,128)S(1)} %get-tuple-element.18), channel_id=1, source_target_pairs={{0,16},{4,20},{8,24},{12,28},{16,0},{20,4},{24,8},{28,12},{1,17},{... | collective-permute-start | bytes 98312 | tf_op jit(solution)/shard_map/ppermute | solution.py:234
  16.4 7.5 %collective-permute-start.4 = (f32[8,1024]{1,0:T(8,128)S(1)}, f32[8,1024]{1,0:T(8,128)S(1)}, u32[]{:S(2)}, u32[]{:S(2)}) collective-permute-start(f32[8,1024]{1,0:T(8,128)S(1)} %get-tuple-element.19), channel_id=1, source_target_pairs={{0,24},{4,28},{8,0},{12,4},{16,8},{20,12},{24,16},{28,20},{1,25},{... | collective-permute-start | bytes 98312 | tf_op jit(solution)/shard_map/ppermute | solution.py:234
  18.6 4.0 %collective-permute-start.9 = (bf16[8,1024]{1,0:T(8,128)(2,1)S(1)}, bf16[8,1024]{1,0:T(8,128)(2,1)S(1)}, u32[]{:S(2)}, u32[]{:S(2)}) collective-permute-start(bf16[8,1024]{1,0:T(8,128)(2,1)S(1)} %copy-done), channel_id=1, source_target_pairs={{0,1},{1,0},{2,3},{3,2},{4,5},{5,4},{6,7},{7,6},{8,9},{9,8},{10,11... | collective-permute-start | bytes 49160 | tf_op jit(solution)/shard_map/ppermute | solution.py:240
  20.1 3.7 %collective-permute-start.10 = (bf16[8,1024]{1,0:T(8,128)(2,1)S(1)}, bf16[8,1024]{1,0:T(8,128)(2,1)S(1)}, u32[]{:S(2)}, u32[]{:S(2)}) collective-permute-start(bf16[8,1024]{1,0:T(8,128)(2,1)S(1)} %collective-permute-done.refs_0_.refs_7_), channel_id=1, source_target_pairs={{0,1},{1,0},{2,3},{3,2},{4,5},{5,4},{6,7},{7,6},{8,9},{9,8},{10,11... | collective-permute-start | bytes 49160 | tf_op jit(solution)/shard_map/ppermute | solution.py:240
  24.3 1.2 %collective-permute-start.12 = (f32[8,16]{1,0:T(8,128)S(1)}, f32[8,16]{1,0:T(8,128)S(1)}, u32[]{:S(2)}, u32[]{:S(2)}) collective-permute-start(f32[8,16]{1,0:T(8,128)S(1)} %get-tuple-element.25), channel_id=1, source_target_pairs={{0,4},{4,0},{8,12},{12,8},{16,20},{20,16},{24,28},{28,24},{1,5},{5... | collective-permute-start | bytes 1544 | tf_op jit(solution)/shard_map/ppermute | solution.py:330
  24.3 5.5 %collective-permute-start.13 = (f32[8,16]{1,0:T(8,128)S(1)}, f32[8,16]{1,0:T(8,128)S(1)}, u32[]{:S(2)}, u32[]{:S(2)}) collective-permute-start(f32[8,16]{1,0:T(8,128)S(1)} %get-tuple-element.25), channel_id=1, source_target_pairs={{0,8},{2,10},{4,12},{6,14},{8,0},{10,2},{12,4},{14,6},{16,24},{18,... | collective-permute-start | bytes 1544 | tf_op jit(solution)/shard_map/ppermute | solution.py:327
  25.5 5.4 %collective-permute-start.16 = (f32[8,16]{1,0:T(8,128)S(1)}, f32[8,16]{1,0:T(8,128)S(1)}, u32[]{:S(2)}, u32[]{:S(2)}) collective-permute-start(f32[8,16]{1,0:T(8,128)S(1)} %add.22), channel_id=1, source_target_pairs={{0,24},{2,26},{4,30},{6,28},{8,16},{10,18},{12,22},{14,20},{16,8},... | collective-permute-start | bytes 1544 | tf_op jit(solution)/shard_map/ppermute | solution.py:327
  26.7 4.5 %collective-permute-start.15 = (f32[8,16]{1,0:T(8,128)S(1)}, f32[8,16]{1,0:T(8,128)S(1)}, u32[]{:S(2)}, u32[]{:S(2)}) collective-permute-start(f32[8,16]{1,0:T(8,128)S(1)} %add.22), channel_id=1, source_target_pairs={{0,16},{2,18},{4,22},{6,20},{8,24},{10,26},{12,30},{14,28},{16,0},... | collective-permute-start | bytes 1544 | tf_op jit(solution)/shard_map/ppermute | solution.py:327
  27.8 3.6 %collective-permute-start.14 = (f32[8,16]{1,0:T(8,128)S(1)}, f32[8,16]{1,0:T(8,128)S(1)}, u32[]{:S(2)}, u32[]{:S(2)}) collective-permute-start(f32[8,16]{1,0:T(8,128)S(1)} %add.22), channel_id=1, source_target_pairs={{0,2},{2,0},{4,14},{6,12},{8,10},{10,8},{12,6},{14,4},{16,18},{18,... | collective-permute-start | bytes 1544 | tf_op jit(solution)/shard_map/ppermute | solution.py:327
  28.0 3.9 %collective-permute-start.11 = (f32[8,1024]{1,0:T(8,128)S(1)}, f32[8,1024]{1,0:T(8,128)S(1)}, u32[]{:S(2)}, u32[]{:S(2)}) collective-permute-start(f32[8,1024]{1,0:T(8,128)S(1)} %get-tuple-element.23.refs_5_), channel_id=1, source_target_pairs={{0,2},{2,0},{1,3},{3,1},{4,6},{6,4},{5,7},{7,5},{8,10},{10,8},{9,1... | collective-permute-start | bytes 98312 | tf_op jit(solution)/shard_map/ppermute | solution.py:237
  31.4 1.2 %collective-permute-start.17 = (f32[8,16]{1,0:T(8,128)S(1)}, f32[8,16]{1,0:T(8,128)S(1)}, u32[]{:S(2)}, u32[]{:S(2)}) collective-permute-start(f32[8,16]{1,0:T(8,128)S(1)} %add_add_fusion), channel_id=1, source_target_pairs={{0,4},{4,0},{8,12},{12,8},{16,20},{20,16},{24,28},{28,24},{1,5},{5... | collective-permute-start | bytes 1544 | tf_op jit(solution)/shard_map/ppermute | solution.py:330

commit v5 on v4

--- a/solution.py
+++ b/solution.py
@@ -8,9 +8,8 @@
 from jax.experimental.pallas import tpu as pltpu
 from jax.sharding import PartitionSpec as P
 
-CHUNK = 32
-AHEAD = 4
 UNROLL = 128
+LONGER = 4
 GROUP = 8
 VMEM = pl.BlockSpec(memory_space=pltpu.VMEM)
 SMEM = pl.BlockSpec(memory_space=pltpu.SMEM)
@@ -32,7 +31,7 @@
         high[first + q] = jnp.concatenate([zero, part], axis=0)
 
 
-def multiply_tiles(pick, forward, many, count, tiles, low, high, sums, arrive=None):
+def multiply_tiles(pick, forward, many, count, tiles, low, high, sums):
     slots = tiles.shape[0]
     tile = tiles.shape[-1]
     vlocal = sums[0].shape[1]
@@ -40,8 +39,6 @@
         acc[...] = jnp.zeros_like(acc)
 
     def chunk(step, carry):
-        if arrive is not None:
-            arrive(step)
         for g in range(many // (2 * GROUP)):
             results = []
             for u in range(GROUP):
@@ -87,29 +84,28 @@
     return copies
 
 
-def mirror_kernel(sizes, counts, rows_hbm, cols_hbm, tiles_hbm, x_hbm, *refs):
+def stage_kernel(tiles, token):
+    token[...] = jnp.zeros_like(token)
+
+
+def mirror_kernel(sizes, counts, rows_hbm, cols_hbm, tiles, x_hbm, token, *refs):
     nz, ncol, stretch = sizes
     span = ncol * stretch
-    blocks, (mine, other, tiles, x), refs = refs[: ncol - 1], refs[ncol - 1 : ncol + 3], refs[ncol + 3 :]
-    rows, cols, small, sems, low, high, *sums = refs
+    blocks, (mine, other, x, wide), refs = refs[: ncol - 1], refs[ncol - 1 : ncol + 3], refs[ncol + 3 :]
+    rows, cols, small, low, high, *sums = refs
     tile = tiles.shape[-1]
     width = stretch * tile
 
-    def load(step):
-        at = pl.ds(step * CHUNK, CHUNK)
-        return pltpu.make_async_copy(tiles_hbm.at[at], tiles.at[at], sems.at[step])
-
     copies = start_copies(small, (x_hbm, x), (rows_hbm, rows), (cols_hbm, cols))
-    ahead = min(AHEAD, tiles.shape[0] // CHUNK)
-    for step in range(ahead):
-        load(step).start()
     z, core, j = position()
     for t in range(1, ncol):
+        wide[:, t * width : (t + 1) * width] = blocks[t - 1][...]
         place_block(low, high, blocks[t - 1], lax.rem(j + ncol - t, ncol) * stretch, stretch, tile)
     for copy in copies:
         copy.wait()
     count = counts[0, 0]
-    chunks = pl.cdiv(count, CHUNK)
+    wide[:, :width] = x[...]
+    wide[:, ncol * width :] = jnp.zeros_like(wide[:, ncol * width :])
     place_block(low, high, x, j * stretch, stretch, tile)
     low[span] = jnp.zeros(low.shape[1:], low.dtype)
     high[span] = jnp.zeros(high.shape[1:], high.dtype)
@@ -119,20 +115,7 @@
         r, c, row_place, col_place = get(s)
         return jnp.where((s < count) & (r != c), row_place, span), col_place
 
-    def arrive(step):
-        load(step).wait()
-
-        @pl.when(step + ahead < chunks)
-        def _():
-            load(step + ahead).start()
-
-    multiply_tiles(pick, False, CHUNK, count, tiles, low, high, sums, arrive)
-    for step in range(1, ahead):
-
-        @pl.when(step >= chunks)
-        def _():
-            load(step).wait()
-
+    multiply_tiles(pick, False, UNROLL, count, tiles, low, high, sums)
     for s in range(nz):
         target = 2 * lax.rem(z + s, nz)
         for out, c in ((mine, core), (other, 1 - core)):
@@ -188,31 +171,35 @@
 def gram_kernel(nz, ncol, nvec, scale, *refs):
     cols, refs = refs[:nz], refs[nz:]
     parts, refs = refs[:ncol], refs[ncol:]
-    xs, (image, share) = refs[: nvec * ncol], refs[nvec * ncol :]
+    xs, (image, share, *messages) = refs[:nvec], refs[nvec:]
+    width = image.shape[1]
     total = parts[0][...]
     for ref in cols:
         total += ref[...]
     image[...] = total
-    terms = [total] + [ref[...] for ref in parts[1:]]
-    products = []
-    for k in range(nvec):
-        product = None
-        for t in range(ncol):
-            one = lax.dot_general(
-                terms[t],
-                xs[k * ncol + t][...].astype(F32),
-                (((1,), (1,)), ((), ())),
-                precision=HIGHEST,
-                preferred_element_type=F32,
-            )
-            product = one if product is None else product + one
-        products.append(product * scale)
+    terms = jnp.concatenate([total] + [parts[ncol - t][...] for t in range(1, ncol)], axis=1)
+    products = [
+        scale
+        * lax.dot_general(
+            terms,
+            ref[:, : terms.shape[1]].astype(F32),
+            (((1,), (1,)), ((), ())),
+            precision=HIGHEST,
+            preferred_element_type=F32,
+        )
+        for ref in xs
+    ]
     me = lax.axis_index("vec")
     for a in range(nvec):
         picked = products[0]
         for k in range(1, nvec):
             picked = jnp.where(lax.rem(me + nvec - a, nvec) == k, products[k], picked)
         share[:, a * picked.shape[1] : (a + 1) * picked.shape[1]] = picked
+    for t in range(1, ncol):
+        message = messages[t - 1]
+        message[:, :width] = parts[t][...]
+        message[:, width:] = jnp.zeros_like(message[:, width:])
+        message[:, width : width + share.shape[1]] = share[...]
 
 
 def shards(sizes, vectors, tile_vals, tile_rows, tile_cols, tile_counts):
@@ -222,10 +209,21 @@
     slots, tile = tile_vals.shape[2], tile_vals.shape[-1]
     stretch = width // tile
     span = ncol * stretch
-    x_hbm, tiles, rows, cols = (
+    x_hbm, tiles_hbm = (
         pltpu.with_memory_space_constraint(a, pltpu.HBM)
-        for a in (vectors, tile_vals[0, 0], tile_rows[0], tile_cols[0])
+        for a in (vectors, tile_vals[0, 0])
     )
+    tiles, rows, cols = tile_vals[0, 0], tile_rows[0], tile_cols[0]
+    token = pl.pallas_call(
+        stage_kernel,
+        out_shape=jax.ShapeDtypeStruct((vlocal, tile), F32),
+        in_specs=[HBM],
+        out_specs=VMEM,
+        compiler_params=params(6),
+        cost_estimate=pl.CostEstimate(flops=0, bytes_accessed=2 * tile_vals.size * 2, transcendentals=0),
+        name="stage",
+    )(tiles_hbm)
+    vectors, token = lax.optimization_barrier((vectors, token))
 
     def core_swap(x):
         return lax.ppermute(x, "row", [(a, a ^ 1) for a in range(nrow)])
@@ -256,19 +254,19 @@
         flops=2 * slots * tile * tile * 2 * vlocal, bytes_accessed=slots * tile * tile * 2, transcendentals=0
     )
     lists = [pltpu.SMEM((1, slots), jnp.int32)] * 2
-    mine, other, held, x = pl.pallas_call(
+    mine, other, x, wide = pl.pallas_call(
         functools.partial(mirror_kernel, step),
-        out_shape=[ring, ring, jax.ShapeDtypeStruct(tiles.shape, tiles.dtype), jax.ShapeDtypeStruct(vectors.shape, vectors.dtype)],
-        in_specs=[SMEM] + [HBM] * 4 + [VMEM] * (ncol - 1),
+        out_shape=[ring, ring, jax.ShapeDtypeStruct(vectors.shape, vectors.dtype), jax.ShapeDtypeStruct((vlocal, LONGER * ncol * width), vectors.dtype)],
+        in_specs=[SMEM] + [VMEM] * 3 + [HBM] + [VMEM] * ncol,
         out_specs=[VMEM] * 4,
         scratch_shapes=lists
-        + [pltpu.SemaphoreType.DMA((3,)), pltpu.SemaphoreType.DMA((slots // CHUNK,))]
+        + [pltpu.SemaphoreType.DMA((3,))]
         + tables(span)
         + sums(nrow * stretch),
         compiler_params=params(6),
         cost_estimate=cost,
         name="mirror",
-    )(tile_counts, rows, cols, tiles, x_hbm, *row_x[1:])
+    )(tile_counts, rows, cols, tiles, x_hbm, token, *row_x[1:])
     near = jnp.concatenate([x] + ring_x, axis=1)
     far = core_swap(near)
     theirs = core_swap(other)
@@ -284,58 +282,53 @@
     row_parts = pl.pallas_call(
         functools.partial(forward_kernel, step),
         out_shape=[block] * ncol,
-        in_specs=[SMEM] + [HBM] * 2 + [VMEM] * 3,
+        in_specs=[SMEM] + [VMEM] * 5,
         out_specs=[VMEM] * ncol,
         scratch_shapes=lists + [pltpu.SemaphoreType.DMA((2,))] + tables(nrow * stretch) + sums(span),
         compiler_params=params(6),
         cost_estimate=cost,
         name="forward",
-    )(tile_counts, rows, cols, held, near, far)
-    others = [vec_shift(x, t) for t in range(1, nvec) for x in [row_x[0]] + row_x[1:]]
-    def by_target(xs):
-        return [xs[(ncol - t) % ncol] for t in range(ncol)]
-
-    xs = by_target([x] + row_x[1:])
-    for t in range(1, nvec):
-        xs += by_target(others[(t - 1) * ncol : t * ncol])
-    image, share = pl.pallas_call(
+    )(tile_counts, rows, cols, tiles, near, far)
+    every_x = [wide] + [vec_shift(wide, t) for t in range(1, nvec)]
+    pad = -(-nvec * vlocal // tile) * tile
+    message = jax.ShapeDtypeStruct((vlocal, width + pad), F32)
+    image, share, *messages = pl.pallas_call(
         functools.partial(gram_kernel, nz, ncol, nvec, 1.0 / math.sqrt(width * nrow * ncol)),
-        out_shape=[block, jax.ShapeDtypeStruct((vlocal, nvec * vlocal), F32)],
-        in_specs=[VMEM] * (nz + ncol + nvec * ncol),
-        out_specs=[VMEM] * 2,
+        out_shape=[block, jax.ShapeDtypeStruct((vlocal, nvec * vlocal), F32)] + [message] * (ncol - 1),
+        in_specs=[VMEM] * (nz + ncol + nvec),
+        out_specs=[VMEM] * (ncol + 1),
         compiler_params=params(6),
         name="gram",
-    )(*col_parts, *row_parts, *xs)
+    )(*col_parts, *row_parts, *every_x)
+    got = jnp.zeros_like(share)
     for t in range(1, ncol):
-        image = image + col_shift(row_parts[t], t)
-    share = all_sum(share, nz, ncol)
+        message = col_shift(messages[t - 1], t)
+        image = image + message[:, :width]
+        got = got + message[:, width : width + share.shape[1]]
+    share = all_sum(share, got, nz, ncol, messages[0])
     gram = share.T
     return (image.astype(jnp.bfloat16), gram)
 
 
-def all_sum(share, nz, ncol):
-    if nz * ncol > 8 or nz & (nz - 1) or nz == 1:
+def all_sum(share, got, nz, ncol, message):
+    if nz * ncol > 8 or nz & (nz - 1) or ncol % 2:
         return lax.psum(share, ("row", "col"))
     nrow = 2 * nz
 
-    def send(x, pair):
+    def send(x, s, t):
         perm = []
         for a in range(nrow):
             for b in range(ncol):
-                s, t = pair[a % 2]
-                perm.append((a * ncol + b, (a ^ (2 * s)) * ncol + (b + t) % ncol))
+                perm.append((a * ncol + b, (a ^ (2 * s)) * ncol + (b + t + a % 2) % ncol))
         return lax.ppermute(x, ("row", "col"), perm)
 
     def swap(x):
         return lax.ppermute(x, "row", [(a, a ^ 1) for a in range(nrow)])
 
-    got = send(share, ((1, 0), (1, 0)))
-    share = share + swap(share)
-    shifts = [(s, t) for s in range(nz) for t in range(ncol) if (s, t) not in ((0, 0), (1, 0))]
-    for n in range(0, len(shifts) - 1, 2):
-        got = got + send(share, shifts[n : n + 2])
-    if len(shifts) % 2:
-        got = got + 0.5 * send(share, shifts[-1:] * 2)
+    share = share + swap(message)[:, -(-share.shape[1] // 128) * 128 * -1 :][:, : share.shape[1]]
+    for s in range(1, nz):
+        for t in range(0, ncol, 2):
+            got = got + send(share, s, t)
     return share + got + swap(got)
 
 

time: 33.5 us -> 32.1 us (0.958)
  starting transfers between devices: 21 us -> 19.4 us
  waiting for transfers between devices: 4.95 us -> 5.62 us
  Pallas kernels: 4.7 us -> 4.2 us
    ppermute x4 -> x3, starting transfers between devices: 2.55 us -> 4.39 us  [send(): return lax.ppermute(x, ('row', 'col'), perm)]
    ppermute x2, starting transfers between devices: 4.81 us -> 3.13 us  [col_shift(): return lax.ppermute(x, 'col', [(a, (a + t) % ncol) for a in range(ncol)])]
    ppermute x4 -> x3, waiting for transfers between devices: 1.58 us -> 3.2 us  [send(): return lax.ppermute(x, ('row', 'col'), perm)]
    ppermute x2 -> x1, waiting for transfers between devices: 1.24 us -> 0.01 us  [vec_shift(): return lax.ppermute(x, 'vec', [(a, (a + t) % nvec) for a in range(nvec)])]
    ppermute x6, waiting for transfers between devices: 0.02 us -> 0.76 us  [z_shift(): lax.ppermute(x, 'row', [(a, (a + 2 * s) % nrow) for a in range(nrow)])]
    ppermute x2, waiting for transfers between devices: 0.72 us -> 0.01 us  [core_swap(): return lax.ppermute(x, 'row', [(a, a ^ 1) for a in range(nrow)])]
    ppermute x6, starting transfers between devices: 10.6 us -> 9.9 us  [z_shift(): lax.ppermute(x, 'row', [(a, (a + 2 * s) % nrow) for a in range(nrow)])]
    ppermute x2 -> x1, starting transfers between devices: 2.03 us -> 1.58 us  [vec_shift(): return lax.ppermute(x, 'vec', [(a, (a + t) % nvec) for a in range(nvec)])]
  transfers between devices with their start and end apart: 18 -> 16, of which waited for: 8 -> 5; matrix products, arithmetic and copies ran while one was open for 2% -> 2% of each run, Pallas kernels for 13% -> 12%
where the time goes in v5:
time: 32.1 us; the launch traced here: 31.9 us
  starting transfers between devices  19.4 us (60%)
  waiting for transfers between devices  5.62 us (18%)
  Pallas kernels  4.2 us (13%)
  between operations  1.45 us (5%)
  other arithmetic  1.22 us (4%)
    ppermute x6, starting transfers between devices, z_shift(): lax.ppermute(x, 'row', [(a, (a + 2 * s) % nrow) for a in range(nrow)])  9.9 us
    ppermute x3, starting transfers between devices, send(): return lax.ppermute(x, ('row', 'col'), perm)  4.39 us
    ppermute x3, waiting for transfers between devices, send(): return lax.ppermute(x, ('row', 'col'), perm)  3.2 us
    ppermute x2, starting transfers between devices, col_shift(): return lax.ppermute(x, 'col', [(a, (a + t) % ncol) for a in range(ncol)])  3.13 us
    pallas_call x1, Pallas kernels, shards(): pl.pallas_call(functools.partial(mirror_kernel, step), out_shape=[ring, r...  1.93 us
    pallas_call x1, Pallas kernels, shards(): pl.pallas_call(functools.partial(forward_kernel, step), out_shape=[block]...  1.84 us
    ppermute x2, waiting for transfers between devices, swap(): return lax.ppermute(x, 'row', [(a, a ^ 1) for a in range(nrow)])  1.64 us
    ppermute x1, starting transfers between devices, vec_shift(): return lax.ppermute(x, 'vec', [(a, (a + t) % nvec) for a in range(nvec)])  1.58 us
  transfers between devices with their start and end apart: 16, of which 5 were waited for; matrix products, arithmetic and copies ran while one was open for 2% of the time, Pallas kernels for 12%

profile of v5, /device:TPU:0, one launch (start us, length us, event | category | flops | bytes accessed | tf_op | source)
XLA Modules:
  0.0 31.9 jit_solution(11333403007598185311)
XLA Ops:
  0.7 3.0 %collective-permute-start = (bf16[8,1024]{1,0:T(8,128)(2,1)}, bf16[8,1024]{1,0:T(8,128)(2,1)S(1)}, u32[]{:S(2)}, u32[]{:S(2)}) collective-permute-start(bf16[8,1024]{1,0:T(8,128)(2,1)} %x_hbm.1), channel_id=1, source_target_pairs={{0,2},{2,0},{1,3},{3,1},{4,6},{6,4},{5,7},{7,5},{8,10},{10,8},{9,1... | collective-permute-start | bytes 49160 | tf_op jit(solution)/shard_map/ppermute | solution.py:235
  3.7 1.6 %collective-permute-start.5 = (bf16[8,1024]{1,0:T(8,128)(2,1)}, bf16[8,1024]{1,0:T(8,128)(2,1)S(1)}, u32[]{:S(2)}, u32[]{:S(2)}) collective-permute-start(bf16[8,1024]{1,0:T(8,128)(2,1)} %x_hbm.1), channel_id=1, source_target_pairs={{0,8},{4,12},{8,16},{12,20},{16,24},{20,28},{24,0},{28,4},{1,9},{5... | collective-permute-start | bytes 49160 | tf_op jit(solution)/shard_map/ppermute | solution.py:232
  5.3 2.6 %collective-permute-start.6 = (bf16[8,1024]{1,0:T(8,128)(2,1)}, bf16[8,1024]{1,0:T(8,128)(2,1)S(1)}, u32[]{:S(2)}, u32[]{:S(2)}) collective-permute-start(bf16[8,1024]{1,0:T(8,128)(2,1)} %x_hbm.1), channel_id=1, source_target_pairs={{0,16},{4,20},{8,24},{12,28},{16,0},{20,4},{24,8},{28,12},{1,17},{... | collective-permute-start | bytes 49160 | tf_op jit(solution)/shard_map/ppermute | solution.py:232
  7.8 1.3 %collective-permute-start.7 = (bf16[8,1024]{1,0:T(8,128)(2,1)}, bf16[8,1024]{1,0:T(8,128)(2,1)S(1)}, u32[]{:S(2)}, u32[]{:S(2)}) collective-permute-start(bf16[8,1024]{1,0:T(8,128)(2,1)} %x_hbm.1), channel_id=1, source_target_pairs={{0,24},{4,28},{8,0},{12,4},{16,8},{20,12},{24,16},{28,20},{1,25},{... | collective-permute-start | bytes 49160 | tf_op jit(solution)/shard_map/ppermute | solution.py:232
  9.8 0.0 collective-permute-done.refs_0_
  9.9 1.9 %mirror.1 = (f32[8,4096]{1,0:T(8,128)S(1)}, f32[8,4096]{1,0:T(8,128)S(1)}, bf16[8,1024]{1,0:T(8,128)(2,1)S(1)}, bf16[8,8192]{1,0:T(8,128)(2,1)S(1)}) custom-call(s32[1,1]{1,0:T(1,128)S(6)} %copy.10.counts, s32[1,256]{1,0:T(1,128)S(1)} %bitcast.8, s32[1,256]{1,0:T(1,128)S(1)} %bitcast.10, bf16[256,128,128]{2,1,0:T(8,128)(2,1)S(1)} %bitcast.6, ...), custom_call_target="tpu_custom_call" | custom-call | flops 134217728 | bytes 8388608 | tf_op jit(solution)/shard_map/mirror/pallas_call | solution.py:257
  11.8 0.1 collective-permute-start.1
  11.9 1.6 %collective-permute-start.9 = (bf16[8,8192]{1,0:T(8,128)(2,1)S(1)}, bf16[8,8192]{1,0:T(8,128)(2,1)S(1)}, u32[]{:S(2)}, u32[]{:S(2)}) collective-permute-start(bf16[8,8192]{1,0:T(8,128)(2,1)S(1)} %get-tuple-element.28.refs_6_), channel_id=1, source_target_pairs={{0,1},{1,0},{2,3},{3,2},{4,5},{5,4},{6,7},{7,6},{8,9},{9,8},{10,11... | collective-permute-start | bytes 393224 | tf_op jit(solution)/shard_map/ppermute | solution.py:238
  13.5 0.0 collective-permute-done.5
  13.5 0.0 collective-permute-done.6
  13.5 0.2 collective-permute-start.8
  13.8 0.0 collective-permute-done.1.theirs
  13.8 1.8 %collective-permute-start.2 = (f32[8,1024]{1,0:T(8,128)S(1)}, f32[8,1024]{1,0:T(8,128)S(1)}, u32[]{:S(2)}, u32[]{:S(2)}) collective-permute-start(f32[8,1024]{1,0:T(8,128)S(1)} %get-tuple-element.22), channel_id=1, source_target_pairs={{0,8},{4,12},{8,16},{12,20},{16,24},{20,28},{24,0},{28,4},{1,9},{5... | collective-permute-start | bytes 98312 | tf_op jit(solution)/shard_map/ppermute | solution.py:232
  15.6 0.3 %collective-permute-start.3 = (f32[8,1024]{1,0:T(8,128)S(1)}, f32[8,1024]{1,0:T(8,128)S(1)}, u32[]{:S(2)}, u32[]{:S(2)}) collective-permute-start(f32[8,1024]{1,0:T(8,128)S(1)} %get-tuple-element.23), channel_id=1, source_target_pairs={{0,16},{4,20},{8,24},{12,28},{16,0},{20,4},{24,8},{28,12},{1,17},{... | collective-permute-start | bytes 98312 | tf_op jit(solution)/shard_map/ppermute | solution.py:232
  15.9 2.2 %collective-permute-start.4 = (f32[8,1024]{1,0:T(8,128)S(1)}, f32[8,1024]{1,0:T(8,128)S(1)}, u32[]{:S(2)}, u32[]{:S(2)}) collective-permute-start(f32[8,1024]{1,0:T(8,128)S(1)} %get-tuple-element.24), channel_id=1, source_target_pairs={{0,24},{4,28},{8,0},{12,4},{16,8},{20,12},{24,16},{28,20},{1,25},{... | collective-permute-start | bytes 98312 | tf_op jit(solution)/shard_map/ppermute | solution.py:232
  18.2 0.0 collective-permute-done.8.far
  18.2 1.8 %forward.1 = (f32[8,1024]{1,0:T(8,128)S(1)}, f32[8,1024]{1,0:T(8,128)S(1)}) custom-call(s32[1,1]{1,0:T(1,128)S(6)} %copy.10.counts, s32[1,256]{1,0:T(1,128)S(1)} %bitcast.9, s32[1,256]{1,0:T(1,128)S(1)} %bitcast.11, bf16[256,128,128]{2,1,0:T(8,128)(2,1)S(1)} %bitcast.7, bf16[8,4096]{1,0:T(8,128)(2,1)S(1)} %constant_dynamic-update-slice_fusion.near, ...), custom_call_target="tpu_custom_call" | custom-call | flops 134217728 | bytes 8388608 | tf_op jit(solution)/shard_map/forward/pallas_call | solution.py:282
  20.0 0.0 collective-permute-done.9.refs_7_
  20.0 0.0 collective-permute-done.2.refs_1_
  20.1 0.7 %collective-permute-done.3.refs_2_ = f32[8,1024]{1,0:T(8,128)S(1)} collective-permute-done((f32[8,1024]{1,0:T(8,128)S(1)}, f32[8,1024]{1,0:T(8,128)S(1)}, u32[]{:S(2)}, u32[]{:S(2)}) %collective-permute-start.3) | collective-permute-done | bytes 32800 | tf_op jit(solution)/shard_map/ppermute | solution.py:232
  20.8 0.0 collective-permute-done.4.refs_3_
  20.8 0.4 %gram.1 = (f32[8,1024]{1,0:T(8,128)S(1)}, f32[8,16]{1,0:T(8,128)S(1)}, f32[8,1152]{1,0:T(8,128)S(1)}) custom-call(f32[8,1024]{1,0:T(8,128)S(1)} %get-tuple-element.21.refs_0_, f32[8,1024]{1,0:T(8,128)S(1)} %collective-permute-done.2.refs_1_, f32[8,1024]{1,0:T(8,128)S(1)} %collective-permute-done.3.refs_2_, f32[8,1024]{1,0:T(8,128)S(1)} %collective-permute-done.4.refs_3_, ...), custom_call_target="tpu_custom_call" | custom-call | tf_op jit(solution)/shard_map/gram/pallas_call | solution.py:295
  21.2 0.1 collective-permute-start.10
  21.3 1.1 %collective-permute-done.11 = f32[8,1152]{1,0:T(8,128)S(1)} collective-permute-done((f32[8,1152]{1,0:T(8,128)S(1)}, f32[8,1152]{1,0:T(8,128)S(1)}, u32[]{:S(2)}, u32[]{:S(2)}) %collective-permute-start.11) | collective-permute-done | bytes 36896 | tf_op jit(solution)/shard_map/ppermute | solution.py:326
  22.5 3.1 %collective-permute-start.14 = (f32[8,16]{1,0:T(8,128)S(1)}, f32[8,16]{1,0:T(8,128)S(1)}, u32[]{:S(2)}, u32[]{:S(2)}) collective-permute-start(f32[8,16]{1,0:T(8,128)S(1)} %slice_add_fusion.2), channel_id=1, source_target_pairs={{0,24},{2,26},{4,30},{6,28},{8,16},{10,18},{12,22},{14,20},{16,8},... | collective-permute-start | bytes 1544 | tf_op jit(solution)/shard_map/ppermute | solution.py:323
  25.5 1.3 %collective-permute-start.12 = (f32[8,16]{1,0:T(8,128)S(1)}, f32[8,16]{1,0:T(8,128)S(1)}, u32[]{:S(2)}, u32[]{:S(2)}) collective-permute-start(f32[8,16]{1,0:T(8,128)S(1)} %slice_add_fusion.2), channel_id=1, source_target_pairs={{0,8},{2,10},{4,14},{6,12},{8,0},{10,2},{12,6},{14,4},{16,24},{18,... | collective-permute-start | bytes 1544 | tf_op jit(solution)/shard_map/ppermute | solution.py:323
  26.8 1.0 %collective-permute-done.14 = f32[8,16]{1,0:T(8,128)S(1)} collective-permute-done((f32[8,16]{1,0:T(8,128)S(1)}, f32[8,16]{1,0:T(8,128)S(1)}, u32[]{:S(2)}, u32[]{:S(2)}) %collective-permute-start.14) | collective-permute-done | bytes 544 | tf_op jit(solution)/shard_map/ppermute | solution.py:323
  27.9 2.2 %collective-permute-done.13 = f32[8,16]{1,0:T(8,128)S(1)} collective-permute-done((f32[8,16]{1,0:T(8,128)S(1)}, f32[8,16]{1,0:T(8,128)S(1)}, u32[]{:S(2)}, u32[]{:S(2)}) %collective-permute-start.13) | collective-permute-done | bytes 544 | tf_op jit(solution)/shard_map/ppermute | solution.py:323
  30.1 0.1 collective-permute-start.15
  30.1 0.6 %fusion = bf16[8,1024]{1,0:T(8,128)(2,1)} fusion(f32[8,1024]{1,0:T(8,128)S(1)} %get-tuple-element.29, f32[8,1152]{1,0:T(8,128)S(1)} %collective-permute-done.10), kind=kLoop, calls=%fused_computation.1 | loop fusion | flops 16384 | bytes 81920 | tf_op jit(solution)/shard_map/convert_element_type | solution.py:310
  30.7 0.5 %collective-permute-done.15 = f32[8,16]{1,0:T(8,128)S(1)} collective-permute-done((f32[8,16]{1,0:T(8,128)S(1)}, f32[8,16]{1,0:T(8,128)S(1)}, u32[]{:S(2)}, u32[]{:S(2)}) %collective-permute-start.15) | collective-permute-done | bytes 544 | tf_op jit(solution)/shard_map/ppermute | solution.py:326
  31.3 0.6 %add_bitcast_fusion = f32[16,8]{0,1:T(8,128)} fusion(f32[8,16]{1,0:T(8,128)S(1)} %collective-permute-done.15, f32[8,16]{1,0:T(8,128)S(1)} %slice_add_fusion.2, f32[8,16]{1,0:T(8,128)S(1)} %fusion.2), kind=kLoop, calls=%fused_computation.10 | loop fusion | flops 256 | bytes 2048 | tf_op jit(solution)/shard_map/transpose | solution.py:309
  (19 shorter events, 0.1 us)
Async XLA Ops:
  0.6 9.2 %copy-start = (bf16[1,1,256,128,128]{4,3,2,1,0:T(8,128)(2,1)S(1)}, bf16[1,1,256,128,128]{4,3,2,1,0:T(8,128)(2,1)}, u32[]{:S(2)}) copy-start(bf16[1,1,256,128,128]{4,3,2,1,0:T(8,128)(2,1)} %param.6) | copy-start | bytes 25165828
  0.6 9.2 %copy-start.1 = (s32[1,1,256]{2,1,0:T(1,128)S(1)}, s32[1,1,256]{2,1,0:T(1,128)}, u32[]{:S(2)}) copy-start(s32[1,1,256]{2,1,0:T(1,128)} %param.7) | copy-start | bytes 3076
  0.7 9.2 %copy-start.2 = (s32[1,1,256]{2,1,0:T(1,128)S(1)}, s32[1,1,256]{2,1,0:T(1,128)}, u32[]{:S(2)}) copy-start(s32[1,1,256]{2,1,0:T(1,128)} %param.8) | copy-start | bytes 3076
  0.7 9.2 %collective-permute-start = (bf16[8,1024]{1,0:T(8,128)(2,1)}, bf16[8,1024]{1,0:T(8,128)(2,1)S(1)}, u32[]{:S(2)}, u32[]{:S(2)}) collective-permute-start(bf16[8,1024]{1,0:T(8,128)(2,1)} %x_hbm.1), channel_id=1, source_target_pairs={{0,2},{2,0},{1,3},{3,1},{4,6},{6,4},{5,7},{7,5},{8,10},{10,8},{9,1... | collective-permute-start | bytes 49160 | tf_op jit(solution)/shard_map/ppermute | solution.py:235
  3.7 9.8 %collective-permute-start.5 = (bf16[8,1024]{1,0:T(8,128)(2,1)}, bf16[8,1024]{1,0:T(8,128)(2,1)S(1)}, u32[]{:S(2)}, u32[]{:S(2)}) collective-permute-start(bf16[8,1024]{1,0:T(8,128)(2,1)} %x_hbm.1), channel_id=1, source_target_pairs={{0,8},{4,12},{8,16},{12,20},{16,24},{20,28},{24,0},{28,4},{1,9},{5... | collective-permute-start | bytes 49160 | tf_op jit(solution)/shard_map/ppermute | solution.py:232
  5.3 8.3 %collective-permute-start.6 = (bf16[8,1024]{1,0:T(8,128)(2,1)}, bf16[8,1024]{1,0:T(8,128)(2,1)S(1)}, u32[]{:S(2)}, u32[]{:S(2)}) collective-permute-start(bf16[8,1024]{1,0:T(8,128)(2,1)} %x_hbm.1), channel_id=1, source_target_pairs={{0,16},{4,20},{8,24},{12,28},{16,0},{20,4},{24,8},{28,12},{1,17},{... | collective-permute-start | bytes 49160 | tf_op jit(solution)/shard_map/ppermute | solution.py:232
  7.8 5.7 %collective-permute-start.7 = (bf16[8,1024]{1,0:T(8,128)(2,1)}, bf16[8,1024]{1,0:T(8,128)(2,1)S(1)}, u32[]{:S(2)}, u32[]{:S(2)}) collective-permute-start(bf16[8,1024]{1,0:T(8,128)(2,1)} %x_hbm.1), channel_id=1, source_target_pairs={{0,24},{4,28},{8,0},{12,4},{16,8},{20,12},{24,16},{28,20},{1,25},{... | collective-permute-start | bytes 49160 | tf_op jit(solution)/shard_map/ppermute | solution.py:232
  11.8 1.9 %collective-permute-start.1 = (f32[8,4096]{1,0:T(8,128)S(1)}, f32[8,4096]{1,0:T(8,128)S(1)}, u32[]{:S(2)}, u32[]{:S(2)}) collective-permute-start(f32[8,4096]{1,0:T(8,128)S(1)} %get-tuple-element.20), channel_id=1, source_target_pairs={{0,4},{4,0},{8,12},{12,8},{16,20},{20,16},{24,28},{28,24},{1,5},{5... | collective-permute-start | bytes 393224 | tf_op jit(solution)/shard_map/ppermute | solution.py:229
  11.9 8.1 %collective-permute-start.9 = (bf16[8,8192]{1,0:T(8,128)(2,1)S(1)}, bf16[8,8192]{1,0:T(8,128)(2,1)S(1)}, u32[]{:S(2)}, u32[]{:S(2)}) collective-permute-start(bf16[8,8192]{1,0:T(8,128)(2,1)S(1)} %get-tuple-element.28.refs_6_), channel_id=1, source_target_pairs={{0,1},{1,0},{2,3},{3,2},{4,5},{5,4},{6,7},{7,6},{8,9},{9,8},{10,11... | collective-permute-start | bytes 393224 | tf_op jit(solution)/shard_map/ppermute | solution.py:238
  13.5 4.6 %collective-permute-start.8 = (bf16[8,4096]{1,0:T(8,128)(2,1)S(1)}, bf16[8,4096]{1,0:T(8,128)(2,1)S(1)}, u32[]{:S(2)}, u32[]{:S(2)}) collective-permute-start(bf16[8,4096]{1,0:T(8,128)(2,1)S(1)} %constant_dynamic-update-slice_fusion.near), channel_id=1, source_target_pairs={{0,4},{4,0},{8,12},{12,8},{16,20},{20,16},{24,28},{28,24},{1,5},{5... | collective-permute-start | bytes 196616 | tf_op jit(solution)/shard_map/ppermute | solution.py:229
  13.8 6.3 %collective-permute-start.2 = (f32[8,1024]{1,0:T(8,128)S(1)}, f32[8,1024]{1,0:T(8,128)S(1)}, u32[]{:S(2)}, u32[]{:S(2)}) collective-permute-start(f32[8,1024]{1,0:T(8,128)S(1)} %get-tuple-element.22), channel_id=1, source_target_pairs={{0,8},{4,12},{8,16},{12,20},{16,24},{20,28},{24,0},{28,4},{1,9},{5... | collective-permute-start | bytes 98312 | tf_op jit(solution)/shard_map/ppermute | solution.py:232
  15.6 5.2 %collective-permute-start.3 = (f32[8,1024]{1,0:T(8,128)S(1)}, f32[8,1024]{1,0:T(8,128)S(1)}, u32[]{:S(2)}, u32[]{:S(2)}) collective-permute-start(f32[8,1024]{1,0:T(8,128)S(1)} %get-tuple-element.23), channel_id=1, source_target_pairs={{0,16},{4,20},{8,24},{12,28},{16,0},{20,4},{24,8},{28,12},{1,17},{... | collective-permute-start | bytes 98312 | tf_op jit(solution)/shard_map/ppermute | solution.py:232
  15.9 4.9 %collective-permute-start.4 = (f32[8,1024]{1,0:T(8,128)S(1)}, f32[8,1024]{1,0:T(8,128)S(1)}, u32[]{:S(2)}, u32[]{:S(2)}) collective-permute-start(f32[8,1024]{1,0:T(8,128)S(1)} %get-tuple-element.24), channel_id=1, source_target_pairs={{0,24},{4,28},{8,0},{12,4},{16,8},{20,12},{24,16},{28,20},{1,25},{... | collective-permute-start | bytes 98312 | tf_op jit(solution)/shard_map/ppermute | solution.py:232
  21.2 1.2 %collective-permute-start.11 = (f32[8,1152]{1,0:T(8,128)S(1)}, f32[8,1152]{1,0:T(8,128)S(1)}, u32[]{:S(2)}, u32[]{:S(2)}) collective-permute-start(f32[8,1152]{1,0:T(8,128)S(1)} %get-tuple-element.30), channel_id=1, source_target_pairs={{0,4},{4,0},{8,12},{12,8},{16,20},{20,16},{24,28},{28,24},{1,5},{5... | collective-permute-start | bytes 110600 | tf_op jit(solution)/shard_map/ppermute | solution.py:326
  21.2 5.6 %collective-permute-start.10 = (f32[8,1152]{1,0:T(8,128)S(1)}, f32[8,1152]{1,0:T(8,128)S(1)}, u32[]{:S(2)}, u32[]{:S(2)}) collective-permute-start(f32[8,1152]{1,0:T(8,128)S(1)} %get-tuple-element.30), channel_id=1, source_target_pairs={{0,2},{2,0},{1,3},{3,1},{4,6},{6,4},{5,7},{7,5},{8,10},{10,8},{9,1... | collective-permute-start | bytes 110600 | tf_op jit(solution)/shard_map/ppermute | solution.py:235
  22.5 5.4 %collective-permute-start.14 = (f32[8,16]{1,0:T(8,128)S(1)}, f32[8,16]{1,0:T(8,128)S(1)}, u32[]{:S(2)}, u32[]{:S(2)}) collective-permute-start(f32[8,16]{1,0:T(8,128)S(1)} %slice_add_fusion.2), channel_id=1, source_target_pairs={{0,24},{2,26},{4,30},{6,28},{8,16},{10,18},{12,22},{14,20},{16,8},... | collective-permute-start | bytes 1544 | tf_op jit(solution)/shard_map/ppermute | solution.py:323
  25.5 4.5 %collective-permute-start.13 = (f32[8,16]{1,0:T(8,128)S(1)}, f32[8,16]{1,0:T(8,128)S(1)}, u32[]{:S(2)}, u32[]{:S(2)}) collective-permute-start(f32[8,16]{1,0:T(8,128)S(1)} %slice_add_fusion.2), channel_id=1, source_target_pairs={{0,16},{2,18},{4,22},{6,20},{8,24},{10,26},{12,30},{14,28},{16,0},... | collective-permute-start | bytes 1544 | tf_op jit(solution)/shard_map/ppermute | solution.py:323
  25.5 4.5 %collective-permute-start.12 = (f32[8,16]{1,0:T(8,128)S(1)}, f32[8,16]{1,0:T(8,128)S(1)}, u32[]{:S(2)}, u32[]{:S(2)}) collective-permute-start(f32[8,16]{1,0:T(8,128)S(1)} %slice_add_fusion.2), channel_id=1, source_target_pairs={{0,8},{2,10},{4,14},{6,12},{8,0},{10,2},{12,6},{14,4},{16,24},{18,... | collective-permute-start | bytes 1544 | tf_op jit(solution)/shard_map/ppermute | solution.py:323
  30.1 1.2 %collective-permute-start.15 = (f32[8,16]{1,0:T(8,128)S(1)}, f32[8,16]{1,0:T(8,128)S(1)}, u32[]{:S(2)}, u32[]{:S(2)}) collective-permute-start(f32[8,16]{1,0:T(8,128)S(1)} %fusion.2), channel_id=1, source_target_pairs={{0,4},{4,0},{8,12},{12,8},{16,20},{20,16},{24,28},{28,24},{1,5},{5... | collective-permute-start | bytes 1544 | tf_op jit(solution)/shard_map/ppermute | solution.py:326

commit v6 on v5

--- a/solution.py
+++ b/solution.py
@@ -64,12 +64,24 @@
     lax.fori_loop(0, pl.cdiv(count, many), chunk, 0)
 
 
+def divide(x, n):
+    if n & (n - 1):
+        return lax.div(x, n), lax.rem(x, n)
+    return x >> (n.bit_length() - 1), x & (n - 1)
+
+
 def places(rows, cols, span, stretch):
-    def get(s):
-        r, c = rows[0, s], cols[0, s]
-        return r, c, lax.rem(r, span), lax.div(c, span) * stretch + lax.rem(c, stretch)
-
-    return get
+    group, inner = divide(cols[...], span)
+    return divide(rows[...], span)[1], group * stretch + divide(inner, stretch)[1]
+
+
+def hand_scalars(held, sem, *lists):
+    vector, scalar = held
+    for n, values in enumerate(lists):
+        vector[n : n + 1, :] = values
+    copy = pltpu.make_async_copy(vector, scalar, sem)
+    copy.start()
+    return copy
 
 
 def position():
@@ -77,43 +89,38 @@
     return lax.div(i, 2), lax.rem(i, 2), lax.axis_index("col")
 
 
-def start_copies(sems, *pairs):
-    copies = [pltpu.make_async_copy(a, b, sems.at[n]) for n, (a, b) in enumerate(pairs)]
-    for copy in copies:
-        copy.start()
-    return copies
-
-
 def stage_kernel(tiles, token):
     token[...] = jnp.zeros_like(token)
 
 
-def mirror_kernel(sizes, counts, rows_hbm, cols_hbm, tiles, x_hbm, token, *refs):
+def mirror_kernel(sizes, counts, rows, cols, tiles, x_hbm, token, *refs):
     nz, ncol, stretch = sizes
     span = ncol * stretch
     blocks, (mine, other, x, wide), refs = refs[: ncol - 1], refs[ncol - 1 : ncol + 3], refs[ncol + 3 :]
-    rows, cols, small, low, high, *sums = refs
+    vector, scalar, sems, low, high, *sums = refs
     tile = tiles.shape[-1]
     width = stretch * tile
-
-    copies = start_copies(small, (x_hbm, x), (rows_hbm, rows), (cols_hbm, cols))
+    count = counts[0, 0]
+    own = pltpu.make_async_copy(x_hbm, x, sems.at[0])
+    own.start()
+    slot = lax.broadcasted_iota(jnp.int32, rows.shape, 1)
+    row_place, col_place = places(rows, cols, span, stretch)
+    used = jnp.where((slot < count) & (rows[...] != cols[...]), row_place, span)
+    indices = hand_scalars((vector, scalar), sems.at[1], used, col_place)
     z, core, j = position()
     for t in range(1, ncol):
         wide[:, t * width : (t + 1) * width] = blocks[t - 1][...]
         place_block(low, high, blocks[t - 1], lax.rem(j + ncol - t, ncol) * stretch, stretch, tile)
-    for copy in copies:
-        copy.wait()
-    count = counts[0, 0]
+    own.wait()
     wide[:, :width] = x[...]
     wide[:, ncol * width :] = jnp.zeros_like(wide[:, ncol * width :])
     place_block(low, high, x, j * stretch, stretch, tile)
     low[span] = jnp.zeros(low.shape[1:], low.dtype)
     high[span] = jnp.zeros(high.shape[1:], high.dtype)
-    get = places(rows, cols, span, stretch)
+    indices.wait()
 
     def pick(s):
-        r, c, row_place, col_place = get(s)
-        return jnp.where((s < count) & (r != c), row_place, span), col_place
+        return scalar[0, s], scalar[1, s]
 
     multiply_tiles(pick, False, UNROLL, count, tiles, low, high, sums)
     for s in range(nz):
@@ -127,11 +134,14 @@
                 out[:, s * width + q * tile : s * width + (q + 1) * tile] = total
 
 
-def forward_kernel(sizes, counts, rows_hbm, cols_hbm, tiles, near, far, *refs):
+def forward_kernel(sizes, counts, rows, cols, tiles, near, far, *refs):
     nz, ncol, stretch = sizes
     span = ncol * stretch
-    outs, (rows, cols, small, low, high, *sums) = refs[:ncol], refs[ncol:]
-    copies = start_copies(small, (rows_hbm, rows), (cols_hbm, cols))
+    outs, (vector, scalar, sem, low, high, *sums) = refs[:ncol], refs[ncol:]
+    dead = 2 * nz * stretch
+    slot = lax.broadcasted_iota(jnp.int32, rows.shape, 1)
+    row_place, col_place = places(rows, cols, span, stretch)
+    indices = hand_scalars((vector, scalar), sem, jnp.where(slot < counts[0, 0], col_place, dead), row_place)
     tile = tiles.shape[-1]
     width = stretch * tile
     z, core, j = position()
@@ -139,19 +149,14 @@
         source = 2 * lax.rem(z + nz - s, nz)
         for ref, c in ((near, core), (far, 1 - core)):
             place_block(low, high, ref[:, s * width : (s + 1) * width], (source + c) * stretch, stretch, tile)
-    dead = 2 * nz * stretch
-    for copy in copies:
-        copy.wait()
-    count = counts[0, 0]
     low[dead] = jnp.zeros(low.shape[1:], low.dtype)
     high[dead] = jnp.zeros(high.shape[1:], high.dtype)
-    get = places(rows, cols, span, stretch)
+    indices.wait()
 
     def pick(s):
-        _, _, row_place, col_place = get(s)
-        return jnp.where(s < count, col_place, dead), row_place
-
-    multiply_tiles(pick, True, UNROLL, count, tiles, low, high, sums)
+        return scalar[0, s], scalar[1, s]
+
+    multiply_tiles(pick, True, UNROLL, counts[0, 0], tiles, low, high, sums)
     for t in range(ncol):
         first = lax.rem(j + t, ncol) * stretch
         for q in range(stretch):
@@ -178,17 +183,18 @@
         total += ref[...]
     image[...] = total
     terms = jnp.concatenate([total] + [parts[ncol - t][...] for t in range(1, ncol)], axis=1)
-    products = [
-        scale
-        * lax.dot_general(
-            terms,
-            ref[:, : terms.shape[1]].astype(F32),
-            (((1,), (1,)), ((), ())),
-            precision=HIGHEST,
-            preferred_element_type=F32,
-        )
-        for ref in xs
-    ]
+    split = []
+    rest = terms
+    for _ in range(3):
+        part = rest.astype(jnp.bfloat16)
+        split.append(part)
+        rest = rest - part.astype(F32)
+    split = jnp.concatenate(split, axis=0)
+    vlocal = terms.shape[0]
+    every = jnp.concatenate([ref[:, : terms.shape[1]] for ref in xs], axis=0)
+    thirds = lax.dot_general(split, every, (((1,), (1,)), ((), ())), preferred_element_type=F32)
+    whole = scale * (thirds[:vlocal] + thirds[vlocal : 2 * vlocal] + thirds[2 * vlocal :])
+    products = [whole[:, k * vlocal : (k + 1) * vlocal] for k in range(nvec)]
     me = lax.axis_index("vec")
     for a in range(nvec):
         picked = products[0]
@@ -253,14 +259,14 @@
     cost = pl.CostEstimate(
         flops=2 * slots * tile * tile * 2 * vlocal, bytes_accessed=slots * tile * tile * 2, transcendentals=0
     )
-    lists = [pltpu.SMEM((1, slots), jnp.int32)] * 2
+    lists = [pltpu.VMEM((2, slots), jnp.int32), pltpu.SMEM((2, slots), jnp.int32)]
     mine, other, x, wide = pl.pallas_call(
         functools.partial(mirror_kernel, step),
         out_shape=[ring, ring, jax.ShapeDtypeStruct(vectors.shape, vectors.dtype), jax.ShapeDtypeStruct((vlocal, LONGER * ncol * width), vectors.dtype)],
         in_specs=[SMEM] + [VMEM] * 3 + [HBM] + [VMEM] * ncol,
         out_specs=[VMEM] * 4,
         scratch_shapes=lists
-        + [pltpu.SemaphoreType.DMA((3,))]
+        + [pltpu.SemaphoreType.DMA((2,))]
         + tables(span)
         + sums(nrow * stretch),
         compiler_params=params(6),
@@ -284,7 +290,7 @@
         out_shape=[block] * ncol,
         in_specs=[SMEM] + [VMEM] * 5,
         out_specs=[VMEM] * ncol,
-        scratch_shapes=lists + [pltpu.SemaphoreType.DMA((2,))] + tables(nrow * stretch) + sums(span),
+        scratch_shapes=lists + [pltpu.SemaphoreType.DMA] + tables(nrow * stretch) + sums(span),
         compiler_params=params(6),
         cost_estimate=cost,
         name="forward",

time: 32.1 us -> 31.3 us (0.975)
  starting transfers between devices: 19.4 us -> 19 us
  Pallas kernels: 4.2 us -> 3.82 us
    pallas_call x1, Pallas kernels: 1.93 us -> 1.56 us  [shards(): pl.pallas_call(functools.partial(mirror_kernel, step), out_shape=[ring, r...]
    ppermute x6, starting transfers between devices: 9.9 us -> 9.55 us  [z_shift(): lax.ppermute(x, 'row', [(a, (a + 2 * s) % nrow) for a in range(nrow)])]
    ppermute x3, waiting for transfers between devices: 3.2 us -> 2.88 us  [send(): return lax.ppermute(x, ('row', 'col'), perm)]
  transfers between devices with their start and end apart: 16 -> 16, of which waited for: 5 -> 5; matrix products, arithmetic and copies ran while one was open for 2% -> 2% of each run, Pallas kernels for 12% -> 11%
where the time goes in v6:
time: 31.3 us; the launch traced here: 31 us
  starting transfers between devices  19 us (61%)
  waiting for transfers between devices  5.49 us (18%)
  Pallas kernels  3.82 us (12%)
  between operations  1.45 us (5%)
  other arithmetic  1.22 us (4%)
    ppermute x6, starting transfers between devices, z_shift(): lax.ppermute(x, 'row', [(a, (a + 2 * s) % nrow) for a in range(nrow)])  9.55 us
    ppermute x3, starting transfers between devices, send(): return lax.ppermute(x, ('row', 'col'), perm)  4.39 us
    ppermute x2, starting transfers between devices, col_shift(): return lax.ppermute(x, 'col', [(a, (a + t) % ncol) for a in range(ncol)])  3.16 us
    ppermute x3, waiting for transfers between devices, send(): return lax.ppermute(x, ('row', 'col'), perm)  2.88 us
    pallas_call x1, Pallas kernels, shards(): pl.pallas_call(functools.partial(forward_kernel, step), out_shape=[block]...  1.93 us
    ppermute x2, waiting for transfers between devices, swap(): return lax.ppermute(x, 'row', [(a, a ^ 1) for a in range(nrow)])  1.61 us
    ppermute x1, starting transfers between devices, vec_shift(): return lax.ppermute(x, 'vec', [(a, (a + t) % nvec) for a in range(nvec)])  1.58 us
    pallas_call x1, Pallas kernels, shards(): pl.pallas_call(functools.partial(mirror_kernel, step), out_shape=[ring, r...  1.56 us
  transfers between devices with their start and end apart: 16, of which 5 were waited for; matrix products, arithmetic and copies ran while one was open for 2% of the time, Pallas kernels for 11%

profile of v6, /device:TPU:0, one launch (start us, length us, event | category | flops | bytes accessed | tf_op | source)
XLA Modules:
  0.0 31.0 jit_solution(16770635021462112174)
XLA Ops:
  0.7 3.0 %collective-permute-start = (bf16[8,1024]{1,0:T(8,128)(2,1)}, bf16[8,1024]{1,0:T(8,128)(2,1)S(1)}, u32[]{:S(2)}, u32[]{:S(2)}) collective-permute-start(bf16[8,1024]{1,0:T(8,128)(2,1)} %x_hbm.1), channel_id=1, source_target_pairs={{0,2},{2,0},{1,3},{3,1},{4,6},{6,4},{5,7},{7,5},{8,10},{10,8},{9,1... | collective-permute-start | bytes 49160 | tf_op jit(solution)/shard_map/ppermute | solution.py:241
  3.7 1.6 %collective-permute-start.5 = (bf16[8,1024]{1,0:T(8,128)(2,1)}, bf16[8,1024]{1,0:T(8,128)(2,1)S(1)}, u32[]{:S(2)}, u32[]{:S(2)}) collective-permute-start(bf16[8,1024]{1,0:T(8,128)(2,1)} %x_hbm.1), channel_id=1, source_target_pairs={{0,8},{4,12},{8,16},{12,20},{16,24},{20,28},{24,0},{28,4},{1,9},{5... | collective-permute-start | bytes 49160 | tf_op jit(solution)/shard_map/ppermute | solution.py:238
  5.3 2.6 %collective-permute-start.6 = (bf16[8,1024]{1,0:T(8,128)(2,1)}, bf16[8,1024]{1,0:T(8,128)(2,1)S(1)}, u32[]{:S(2)}, u32[]{:S(2)}) collective-permute-start(bf16[8,1024]{1,0:T(8,128)(2,1)} %x_hbm.1), channel_id=1, source_target_pairs={{0,16},{4,20},{8,24},{12,28},{16,0},{20,4},{24,8},{28,12},{1,17},{... | collective-permute-start | bytes 49160 | tf_op jit(solution)/shard_map/ppermute | solution.py:238
  7.8 1.3 %collective-permute-start.7 = (bf16[8,1024]{1,0:T(8,128)(2,1)}, bf16[8,1024]{1,0:T(8,128)(2,1)S(1)}, u32[]{:S(2)}, u32[]{:S(2)}) collective-permute-start(bf16[8,1024]{1,0:T(8,128)(2,1)} %x_hbm.1), channel_id=1, source_target_pairs={{0,24},{4,28},{8,0},{12,4},{16,8},{20,12},{24,16},{28,20},{1,25},{... | collective-permute-start | bytes 49160 | tf_op jit(solution)/shard_map/ppermute | solution.py:238
  9.8 0.0 collective-permute-done.refs_0_
  9.9 1.6 %mirror.1 = (f32[8,4096]{1,0:T(8,128)S(1)}, f32[8,4096]{1,0:T(8,128)S(1)}, bf16[8,1024]{1,0:T(8,128)(2,1)S(1)}, bf16[8,8192]{1,0:T(8,128)(2,1)S(1)}) custom-call(s32[1,1]{1,0:T(1,128)S(6)} %copy.10.counts, s32[1,256]{1,0:T(1,128)S(1)} %bitcast.8, s32[1,256]{1,0:T(1,128)S(1)} %bitcast.10, bf16[256,128,128]{2,1,0:T(8,128)(2,1)S(1)} %bitcast.6, ...), custom_call_target="tpu_custom_call" | custom-call | flops 134217728 | bytes 8388608 | tf_op jit(solution)/shard_map/mirror/pallas_call | solution.py:263
  11.4 0.1 collective-permute-start.1
  11.5 1.6 %collective-permute-start.9 = (bf16[8,8192]{1,0:T(8,128)(2,1)S(1)}, bf16[8,8192]{1,0:T(8,128)(2,1)S(1)}, u32[]{:S(2)}, u32[]{:S(2)}) collective-permute-start(bf16[8,8192]{1,0:T(8,128)(2,1)S(1)} %get-tuple-element.28.refs_6_), channel_id=1, source_target_pairs={{0,1},{1,0},{2,3},{3,2},{4,5},{5,4},{6,7},{7,6},{8,9},{9,8},{10,11... | collective-permute-start | bytes 393224 | tf_op jit(solution)/shard_map/ppermute | solution.py:244
  13.1 0.0 collective-permute-done.5
  13.1 0.0 collective-permute-done.7
  13.2 0.2 collective-permute-start.8
  13.4 0.0 collective-permute-done.1.theirs
  13.4 1.5 %collective-permute-start.2 = (f32[8,1024]{1,0:T(8,128)S(1)}, f32[8,1024]{1,0:T(8,128)S(1)}, u32[]{:S(2)}, u32[]{:S(2)}) collective-permute-start(f32[8,1024]{1,0:T(8,128)S(1)} %get-tuple-element.22), channel_id=1, source_target_pairs={{0,8},{4,12},{8,16},{12,20},{16,24},{20,28},{24,0},{28,4},{1,9},{5... | collective-permute-start | bytes 98312 | tf_op jit(solution)/shard_map/ppermute | solution.py:238
  14.9 0.7 %collective-permute-start.3 = (f32[8,1024]{1,0:T(8,128)S(1)}, f32[8,1024]{1,0:T(8,128)S(1)}, u32[]{:S(2)}, u32[]{:S(2)}) collective-permute-start(f32[8,1024]{1,0:T(8,128)S(1)} %get-tuple-element.23), channel_id=1, source_target_pairs={{0,16},{4,20},{8,24},{12,28},{16,0},{20,4},{24,8},{28,12},{1,17},{... | collective-permute-start | bytes 98312 | tf_op jit(solution)/shard_map/ppermute | solution.py:238
  15.6 1.9 %collective-permute-start.4 = (f32[8,1024]{1,0:T(8,128)S(1)}, f32[8,1024]{1,0:T(8,128)S(1)}, u32[]{:S(2)}, u32[]{:S(2)}) collective-permute-start(f32[8,1024]{1,0:T(8,128)S(1)} %get-tuple-element.24), channel_id=1, source_target_pairs={{0,24},{4,28},{8,0},{12,4},{16,8},{20,12},{24,16},{28,20},{1,25},{... | collective-permute-start | bytes 98312 | tf_op jit(solution)/shard_map/ppermute | solution.py:238
  17.4 0.0 collective-permute-done.8.far
  17.5 1.9 %forward.1 = (f32[8,1024]{1,0:T(8,128)S(1)}, f32[8,1024]{1,0:T(8,128)S(1)}) custom-call(s32[1,1]{1,0:T(1,128)S(6)} %copy.10.counts, s32[1,256]{1,0:T(1,128)S(1)} %bitcast.9, s32[1,256]{1,0:T(1,128)S(1)} %bitcast.11, bf16[256,128,128]{2,1,0:T(8,128)(2,1)S(1)} %bitcast.7, bf16[8,4096]{1,0:T(8,128)(2,1)S(1)} %constant_dynamic-update-slice_fusion.near, ...), custom_call_target="tpu_custom_call" | custom-call | flops 134217728 | bytes 8388608 | tf_op jit(solution)/shard_map/forward/pallas_call | solution.py:288
  19.4 0.0 collective-permute-done.9.refs_7_
  19.4 0.0 collective-permute-done.2.refs_1_
  19.4 1.0 %collective-permute-done.3.refs_2_ = f32[8,1024]{1,0:T(8,128)S(1)} collective-permute-done((f32[8,1024]{1,0:T(8,128)S(1)}, f32[8,1024]{1,0:T(8,128)S(1)}, u32[]{:S(2)}, u32[]{:S(2)}) %collective-permute-start.3) | collective-permute-done | bytes 32800 | tf_op jit(solution)/shard_map/ppermute | solution.py:238
  20.4 0.3 %gram.1 = (f32[8,1024]{1,0:T(8,128)S(1)}, f32[8,16]{1,0:T(8,128)S(1)}, f32[8,1152]{1,0:T(8,128)S(1)}) custom-call(f32[8,1024]{1,0:T(8,128)S(1)} %get-tuple-element.21.refs_0_, f32[8,1024]{1,0:T(8,128)S(1)} %collective-permute-done.2.refs_1_, f32[8,1024]{1,0:T(8,128)S(1)} %collective-permute-done.3.refs_2_, f32[8,1024]{1,0:T(8,128)S(1)} %collective-permute-done.4.refs_3_, ...), custom_call_target="tpu_custom_call" | custom-call | tf_op jit(solution)/shard_map/gram/pallas_call | solution.py:301
  20.7 0.2 collective-permute-start.10
  20.9 1.1 %collective-permute-done.11 = f32[8,1152]{1,0:T(8,128)S(1)} collective-permute-done((f32[8,1152]{1,0:T(8,128)S(1)}, f32[8,1152]{1,0:T(8,128)S(1)}, u32[]{:S(2)}, u32[]{:S(2)}) %collective-permute-start.11) | collective-permute-done | bytes 36896 | tf_op jit(solution)/shard_map/ppermute | solution.py:332
  21.9 2.8 %collective-permute-start.14 = (f32[8,16]{1,0:T(8,128)S(1)}, f32[8,16]{1,0:T(8,128)S(1)}, u32[]{:S(2)}, u32[]{:S(2)}) collective-permute-start(f32[8,16]{1,0:T(8,128)S(1)} %slice_add_fusion.2), channel_id=1, source_target_pairs={{0,24},{2,26},{4,30},{6,28},{8,16},{10,18},{12,22},{14,20},{16,8},... | collective-permute-start | bytes 1544 | tf_op jit(solution)/shard_map/ppermute | solution.py:329
  24.7 0.1 collective-permute-start.13
  24.8 1.6 %collective-permute-start.12 = (f32[8,16]{1,0:T(8,128)S(1)}, f32[8,16]{1,0:T(8,128)S(1)}, u32[]{:S(2)}, u32[]{:S(2)}) collective-permute-start(f32[8,16]{1,0:T(8,128)S(1)} %slice_add_fusion.2), channel_id=1, source_target_pairs={{0,8},{2,10},{4,14},{6,12},{8,0},{10,2},{12,6},{14,4},{16,24},{18,... | collective-permute-start | bytes 1544 | tf_op jit(solution)/shard_map/ppermute | solution.py:329
  26.3 1.0 %collective-permute-done.14 = f32[8,16]{1,0:T(8,128)S(1)} collective-permute-done((f32[8,16]{1,0:T(8,128)S(1)}, f32[8,16]{1,0:T(8,128)S(1)}, u32[]{:S(2)}, u32[]{:S(2)}) %collective-permute-start.14) | collective-permute-done | bytes 544 | tf_op jit(solution)/shard_map/ppermute | solution.py:329
  27.3 1.9 %collective-permute-done.13 = f32[8,16]{1,0:T(8,128)S(1)} collective-permute-done((f32[8,16]{1,0:T(8,128)S(1)}, f32[8,16]{1,0:T(8,128)S(1)}, u32[]{:S(2)}, u32[]{:S(2)}) %collective-permute-start.13) | collective-permute-done | bytes 544 | tf_op jit(solution)/shard_map/ppermute | solution.py:329
  29.2 0.1 collective-permute-start.15
  29.3 0.6 %fusion = bf16[8,1024]{1,0:T(8,128)(2,1)} fusion(f32[8,1024]{1,0:T(8,128)S(1)} %get-tuple-element.29, f32[8,1152]{1,0:T(8,128)S(1)} %collective-permute-done.10), kind=kLoop, calls=%fused_computation.1 | loop fusion | flops 16384 | bytes 81920 | tf_op jit(solution)/shard_map/convert_element_type | solution.py:316
  29.9 0.5 %collective-permute-done.15 = f32[8,16]{1,0:T(8,128)S(1)} collective-permute-done((f32[8,16]{1,0:T(8,128)S(1)}, f32[8,16]{1,0:T(8,128)S(1)}, u32[]{:S(2)}, u32[]{:S(2)}) %collective-permute-start.15) | collective-permute-done | bytes 544 | tf_op jit(solution)/shard_map/ppermute | solution.py:332
  30.5 0.6 %add_bitcast_fusion = f32[16,8]{0,1:T(8,128)} fusion(f32[8,16]{1,0:T(8,128)S(1)} %collective-permute-done.15, f32[8,16]{1,0:T(8,128)S(1)} %slice_add_fusion.2, f32[8,16]{1,0:T(8,128)S(1)} %fusion.2), kind=kLoop, calls=%fused_computation.10 | loop fusion | flops 256 | bytes 2048 | tf_op jit(solution)/shard_map/transpose | solution.py:315
  (19 shorter events, 0.1 us)
Async XLA Ops:
  0.6 9.2 %copy-start = (bf16[1,1,256,128,128]{4,3,2,1,0:T(8,128)(2,1)S(1)}, bf16[1,1,256,128,128]{4,3,2,1,0:T(8,128)(2,1)}, u32[]{:S(2)}) copy-start(bf16[1,1,256,128,128]{4,3,2,1,0:T(8,128)(2,1)} %param.6) | copy-start | bytes 25165828
  0.6 9.2 %copy-start.1 = (s32[1,1,256]{2,1,0:T(1,128)S(1)}, s32[1,1,256]{2,1,0:T(1,128)}, u32[]{:S(2)}) copy-start(s32[1,1,256]{2,1,0:T(1,128)} %param.7) | copy-start | bytes 3076
  0.7 9.2 %copy-start.2 = (s32[1,1,256]{2,1,0:T(1,128)S(1)}, s32[1,1,256]{2,1,0:T(1,128)}, u32[]{:S(2)}) copy-start(s32[1,1,256]{2,1,0:T(1,128)} %param.8) | copy-start | bytes 3076
  0.7 9.2 %collective-permute-start = (bf16[8,1024]{1,0:T(8,128)(2,1)}, bf16[8,1024]{1,0:T(8,128)(2,1)S(1)}, u32[]{:S(2)}, u32[]{:S(2)}) collective-permute-start(bf16[8,1024]{1,0:T(8,128)(2,1)} %x_hbm.1), channel_id=1, source_target_pairs={{0,2},{2,0},{1,3},{3,1},{4,6},{6,4},{5,7},{7,5},{8,10},{10,8},{9,1... | collective-permute-start | bytes 49160 | tf_op jit(solution)/shard_map/ppermute | solution.py:241
  3.7 9.4 %collective-permute-start.5 = (bf16[8,1024]{1,0:T(8,128)(2,1)}, bf16[8,1024]{1,0:T(8,128)(2,1)S(1)}, u32[]{:S(2)}, u32[]{:S(2)}) collective-permute-start(bf16[8,1024]{1,0:T(8,128)(2,1)} %x_hbm.1), channel_id=1, source_target_pairs={{0,8},{4,12},{8,16},{12,20},{16,24},{20,28},{24,0},{28,4},{1,9},{5... | collective-permute-start | bytes 49160 | tf_op jit(solution)/shard_map/ppermute | solution.py:238
  5.3 7.9 %collective-permute-start.6 = (bf16[8,1024]{1,0:T(8,128)(2,1)}, bf16[8,1024]{1,0:T(8,128)(2,1)S(1)}, u32[]{:S(2)}, u32[]{:S(2)}) collective-permute-start(bf16[8,1024]{1,0:T(8,128)(2,1)} %x_hbm.1), channel_id=1, source_target_pairs={{0,16},{4,20},{8,24},{12,28},{16,0},{20,4},{24,8},{28,12},{1,17},{... | collective-permute-start | bytes 49160 | tf_op jit(solution)/shard_map/ppermute | solution.py:238
  7.8 5.3 %collective-permute-start.7 = (bf16[8,1024]{1,0:T(8,128)(2,1)}, bf16[8,1024]{1,0:T(8,128)(2,1)S(1)}, u32[]{:S(2)}, u32[]{:S(2)}) collective-permute-start(bf16[8,1024]{1,0:T(8,128)(2,1)} %x_hbm.1), channel_id=1, source_target_pairs={{0,24},{4,28},{8,0},{12,4},{16,8},{20,12},{24,16},{28,20},{1,25},{... | collective-permute-start | bytes 49160 | tf_op jit(solution)/shard_map/ppermute | solution.py:238
  11.4 1.9 %collective-permute-start.1 = (f32[8,4096]{1,0:T(8,128)S(1)}, f32[8,4096]{1,0:T(8,128)S(1)}, u32[]{:S(2)}, u32[]{:S(2)}) collective-permute-start(f32[8,4096]{1,0:T(8,128)S(1)} %get-tuple-element.20), channel_id=1, source_target_pairs={{0,4},{4,0},{8,12},{12,8},{16,20},{20,16},{24,28},{28,24},{1,5},{5... | collective-permute-start | bytes 393224 | tf_op jit(solution)/shard_map/ppermute | solution.py:235
  11.5 7.9 %collective-permute-start.9 = (bf16[8,8192]{1,0:T(8,128)(2,1)S(1)}, bf16[8,8192]{1,0:T(8,128)(2,1)S(1)}, u32[]{:S(2)}, u32[]{:S(2)}) collective-permute-start(bf16[8,8192]{1,0:T(8,128)(2,1)S(1)} %get-tuple-element.28.refs_6_), channel_id=1, source_target_pairs={{0,1},{1,0},{2,3},{3,2},{4,5},{5,4},{6,7},{7,6},{8,9},{9,8},{10,11... | collective-permute-start | bytes 393224 | tf_op jit(solution)/shard_map/ppermute | solution.py:244
  13.2 4.3 %collective-permute-start.8 = (bf16[8,4096]{1,0:T(8,128)(2,1)S(1)}, bf16[8,4096]{1,0:T(8,128)(2,1)S(1)}, u32[]{:S(2)}, u32[]{:S(2)}) collective-permute-start(bf16[8,4096]{1,0:T(8,128)(2,1)S(1)} %constant_dynamic-update-slice_fusion.near), channel_id=1, source_target_pairs={{0,4},{4,0},{8,12},{12,8},{16,20},{20,16},{24,28},{28,24},{1,5},{5... | collective-permute-start | bytes 196616 | tf_op jit(solution)/shard_map/ppermute | solution.py:235
  13.4 6.0 %collective-permute-start.2 = (f32[8,1024]{1,0:T(8,128)S(1)}, f32[8,1024]{1,0:T(8,128)S(1)}, u32[]{:S(2)}, u32[]{:S(2)}) collective-permute-start(f32[8,1024]{1,0:T(8,128)S(1)} %get-tuple-element.22), channel_id=1, source_target_pairs={{0,8},{4,12},{8,16},{12,20},{16,24},{20,28},{24,0},{28,4},{1,9},{5... | collective-permute-start | bytes 98312 | tf_op jit(solution)/shard_map/ppermute | solution.py:238
  14.9 5.5 %collective-permute-start.3 = (f32[8,1024]{1,0:T(8,128)S(1)}, f32[8,1024]{1,0:T(8,128)S(1)}, u32[]{:S(2)}, u32[]{:S(2)}) collective-permute-start(f32[8,1024]{1,0:T(8,128)S(1)} %get-tuple-element.23), channel_id=1, source_target_pairs={{0,16},{4,20},{8,24},{12,28},{16,0},{20,4},{24,8},{28,12},{1,17},{... | collective-permute-start | bytes 98312 | tf_op jit(solution)/shard_map/ppermute | solution.py:238
  15.6 4.8 %collective-permute-start.4 = (f32[8,1024]{1,0:T(8,128)S(1)}, f32[8,1024]{1,0:T(8,128)S(1)}, u32[]{:S(2)}, u32[]{:S(2)}) collective-permute-start(f32[8,1024]{1,0:T(8,128)S(1)} %get-tuple-element.24), channel_id=1, source_target_pairs={{0,24},{4,28},{8,0},{12,4},{16,8},{20,12},{24,16},{28,20},{1,25},{... | collective-permute-start | bytes 98312 | tf_op jit(solution)/shard_map/ppermute | solution.py:238
  20.7 1.2 %collective-permute-start.11 = (f32[8,1152]{1,0:T(8,128)S(1)}, f32[8,1152]{1,0:T(8,128)S(1)}, u32[]{:S(2)}, u32[]{:S(2)}) collective-permute-start(f32[8,1152]{1,0:T(8,128)S(1)} %get-tuple-element.30), channel_id=1, source_target_pairs={{0,4},{4,0},{8,12},{12,8},{16,20},{20,16},{24,28},{28,24},{1,5},{5... | collective-permute-start | bytes 110600 | tf_op jit(solution)/shard_map/ppermute | solution.py:332
  20.7 5.6 %collective-permute-start.10 = (f32[8,1152]{1,0:T(8,128)S(1)}, f32[8,1152]{1,0:T(8,128)S(1)}, u32[]{:S(2)}, u32[]{:S(2)}) collective-permute-start(f32[8,1152]{1,0:T(8,128)S(1)} %get-tuple-element.30), channel_id=1, source_target_pairs={{0,2},{2,0},{1,3},{3,1},{4,6},{6,4},{5,7},{7,5},{8,10},{10,8},{9,1... | collective-permute-start | bytes 110600 | tf_op jit(solution)/shard_map/ppermute | solution.py:241
  21.9 5.4 %collective-permute-start.14 = (f32[8,16]{1,0:T(8,128)S(1)}, f32[8,16]{1,0:T(8,128)S(1)}, u32[]{:S(2)}, u32[]{:S(2)}) collective-permute-start(f32[8,16]{1,0:T(8,128)S(1)} %slice_add_fusion.2), channel_id=1, source_target_pairs={{0,24},{2,26},{4,30},{6,28},{8,16},{10,18},{12,22},{14,20},{16,8},... | collective-permute-start | bytes 1544 | tf_op jit(solution)/shard_map/ppermute | solution.py:329
  24.7 4.5 %collective-permute-start.13 = (f32[8,16]{1,0:T(8,128)S(1)}, f32[8,16]{1,0:T(8,128)S(1)}, u32[]{:S(2)}, u32[]{:S(2)}) collective-permute-start(f32[8,16]{1,0:T(8,128)S(1)} %slice_add_fusion.2), channel_id=1, source_target_pairs={{0,16},{2,18},{4,22},{6,20},{8,24},{10,26},{12,30},{14,28},{16,0},... | collective-permute-start | bytes 1544 | tf_op jit(solution)/shard_map/ppermute | solution.py:329
  24.8 4.4 %collective-permute-start.12 = (f32[8,16]{1,0:T(8,128)S(1)}, f32[8,16]{1,0:T(8,128)S(1)}, u32[]{:S(2)}, u32[]{:S(2)}) collective-permute-start(f32[8,16]{1,0:T(8,128)S(1)} %slice_add_fusion.2), channel_id=1, source_target_pairs={{0,8},{2,10},{4,14},{6,12},{8,0},{10,2},{12,6},{14,4},{16,24},{18,... | collective-permute-start | bytes 1544 | tf_op jit(solution)/shard_map/ppermute | solution.py:329
  29.2 1.2 %collective-permute-start.15 = (f32[8,16]{1,0:T(8,128)S(1)}, f32[8,16]{1,0:T(8,128)S(1)}, u32[]{:S(2)}, u32[]{:S(2)}) collective-permute-start(f32[8,16]{1,0:T(8,128)S(1)} %fusion.2), channel_id=1, source_target_pairs={{0,4},{4,0},{8,12},{12,8},{16,20},{20,16},{24,28},{28,24},{1,5},{5... | collective-permute-start | bytes 1544 | tf_op jit(solution)/shard_map/ppermute | solution.py:332

commit v7 on v6

--- a/solution.py
+++ b/solution.py
@@ -93,7 +93,7 @@
     token[...] = jnp.zeros_like(token)
 
 
-def mirror_kernel(sizes, counts, rows, cols, tiles, x_hbm, token, *refs):
+def mirror_kernel(sizes, counts, rows, cols, tiles, x_hbm, token, sibling, *refs):
     nz, ncol, stretch = sizes
     span = ncol * stretch
     blocks, (mine, other, x, wide), refs = refs[: ncol - 1], refs[ncol - 1 : ncol + 3], refs[ncol + 3 :]
@@ -113,7 +113,8 @@
         place_block(low, high, blocks[t - 1], lax.rem(j + ncol - t, ncol) * stretch, stretch, tile)
     own.wait()
     wide[:, :width] = x[...]
-    wide[:, ncol * width :] = jnp.zeros_like(wide[:, ncol * width :])
+    wide[:, ncol * width : (ncol + 1) * width] = sibling[...]
+    wide[:, (ncol + 1) * width :] = jnp.zeros_like(wide[:, (ncol + 1) * width :])
     place_block(low, high, x, j * stretch, stretch, tile)
     low[span] = jnp.zeros(low.shape[1:], low.dtype)
     high[span] = jnp.zeros(high.shape[1:], high.dtype)
@@ -123,15 +124,18 @@
         return scalar[0, s], scalar[1, s]
 
     multiply_tiles(pick, False, UNROLL, count, tiles, low, high, sums)
-    for s in range(nz):
-        target = 2 * lax.rem(z + s, nz)
-        for out, c in ((mine, core), (other, 1 - core)):
+    for out, c in ((mine, core), (other, 1 - core)):
+        wanted = [(z, c)]
+        for p in range((nz - 2) // 2):
+            wanted += [(z + nz - (2 * p + 1 + c), 0), (z + nz - (2 * p + 1 + c), 1)]
+        wanted += [(z + 1, c)]
+        for n, (to, half) in enumerate(wanted):
             for q in range(stretch):
-                at = (target + c) * stretch + q
+                at = (2 * lax.rem(to, nz) + half) * stretch + q
                 total = sums[0][at]
                 for acc in sums[1:]:
                     total += acc[at]
-                out[:, s * width + q * tile : s * width + (q + 1) * tile] = total
+                out[:, n * width + q * tile : n * width + (q + 1) * tile] = total
 
 
 def forward_kernel(sizes, counts, rows, cols, tiles, near, far, *refs):
@@ -166,23 +170,32 @@
             outs[t][:, q * tile : (q + 1) * tile] = total
 
 
-def pair_kernel(nz, mine, theirs, *outs):
-    width = mine.shape[1] // nz
-    for s in range(nz):
-        at = slice(s * width, (s + 1) * width)
-        outs[s][...] = mine[:, at] + theirs[:, at]
+def pair_kernel(mine, theirs, *outs):
+    first = 0
+    for out in outs:
+        at = slice(first, first + out.shape[1])
+        out[...] = mine[:, at] + theirs[:, at]
+        first += out.shape[1]
 
 
 def gram_kernel(nz, ncol, nvec, scale, *refs):
-    cols, refs = refs[:nz], refs[nz:]
+    cols, doubles, refs = refs[:2], refs[2 : 2 + (nz - 2) // 2], refs[2 + (nz - 2) // 2 :]
     parts, refs = refs[:ncol], refs[ncol:]
-    xs, (image, share, *messages) = refs[:nvec], refs[nvec:]
+    xs, (image, give, share, *messages) = refs[:nvec], refs[nvec:]
     width = image.shape[1]
+    core = lax.rem(lax.axis_index("row"), 2)
+    kept = pl.ds(pl.multiple_of(core * width, width), width)
+    given = pl.ds(pl.multiple_of((1 - core) * width, width), width)
     total = parts[0][...]
     for ref in cols:
         total += ref[...]
+    away = jnp.zeros_like(total)
+    for ref in doubles:
+        total += ref[:, kept]
+        away += ref[:, given]
     image[...] = total
-    terms = jnp.concatenate([total] + [parts[ncol - t][...] for t in range(1, ncol)], axis=1)
+    give[...] = away
+    terms = jnp.concatenate([total] + [parts[ncol - t][...] for t in range(1, ncol)] + [away], axis=1)
     split = []
     rest = terms
     for _ in range(3):
@@ -244,6 +257,7 @@
         return lax.ppermute(x, "vec", [(a, (a + t) % nvec) for a in range(nvec)])
 
     row_x = [vectors] + [col_shift(vectors, t) for t in range(1, ncol)]
+    sibling = core_swap(vectors)
     ring_x = [z_shift(vectors, s) for s in range(1, nz)]
 
     def tables(count):
@@ -263,7 +277,7 @@
     mine, other, x, wide = pl.pallas_call(
         functools.partial(mirror_kernel, step),
         out_shape=[ring, ring, jax.ShapeDtypeStruct(vectors.shape, vectors.dtype), jax.ShapeDtypeStruct((vlocal, LONGER * ncol * width), vectors.dtype)],
-        in_specs=[SMEM] + [VMEM] * 3 + [HBM] + [VMEM] * ncol,
+        in_specs=[SMEM] + [VMEM] * 3 + [HBM] + [VMEM] * (1 + ncol),
         out_specs=[VMEM] * 4,
         scratch_shapes=lists
         + [pltpu.SemaphoreType.DMA((2,))]
@@ -272,19 +286,26 @@
         compiler_params=params(6),
         cost_estimate=cost,
         name="mirror",
-    )(tile_counts, rows, cols, tiles, x_hbm, token, *row_x[1:])
+    )(tile_counts, rows, cols, tiles, x_hbm, token, sibling, *row_x[1:])
     near = jnp.concatenate([x] + ring_x, axis=1)
     far = core_swap(near)
     theirs = core_swap(other)
+    pairs = (nz - 2) // 2
+    double = jax.ShapeDtypeStruct((vlocal, 2 * width), F32)
     pieces = pl.pallas_call(
-        functools.partial(pair_kernel, nz),
-        out_shape=[block] * nz,
+        pair_kernel,
+        out_shape=[block] + [double] * pairs + [block],
         in_specs=[VMEM] * 2,
-        out_specs=[VMEM] * nz,
+        out_specs=[VMEM] * (pairs + 2),
         compiler_params=params(6),
         name="pair",
     )(mine, theirs)
-    col_parts = [pieces[0]] + [z_shift(pieces[s], s) for s in range(1, nz)]
+    last = z_shift(pieces[-1], 1)
+    doubles = []
+    for p in range(pairs):
+        perm = [(a, (a - 2 * (2 * p + 1 + a % 2)) % nrow) for a in range(nrow)]
+        doubles.append(lax.ppermute(pieces[1 + p], "row", perm))
+    col_parts = [pieces[0], last] + doubles
     row_parts = pl.pallas_call(
         functools.partial(forward_kernel, step),
         out_shape=[block] * ncol,
@@ -298,14 +319,15 @@
     every_x = [wide] + [vec_shift(wide, t) for t in range(1, nvec)]
     pad = -(-nvec * vlocal // tile) * tile
     message = jax.ShapeDtypeStruct((vlocal, width + pad), F32)
-    image, share, *messages = pl.pallas_call(
+    image, give, share, *messages = pl.pallas_call(
         functools.partial(gram_kernel, nz, ncol, nvec, 1.0 / math.sqrt(width * nrow * ncol)),
-        out_shape=[block, jax.ShapeDtypeStruct((vlocal, nvec * vlocal), F32)] + [message] * (ncol - 1),
-        in_specs=[VMEM] * (nz + ncol + nvec),
-        out_specs=[VMEM] * (ncol + 1),
+        out_shape=[block, block, jax.ShapeDtypeStruct((vlocal, nvec * vlocal), F32)] + [message] * (ncol - 1),
+        in_specs=[VMEM] * (2 + pairs + ncol + nvec),
+        out_specs=[VMEM] * (ncol + 2),
         compiler_params=params(6),
         name="gram",
     )(*col_parts, *row_parts, *every_x)
+    image = image + core_swap(give)
     got = jnp.zeros_like(share)
     for t in range(1, ncol):
         message = col_shift(messages[t - 1], t)
@@ -339,7 +361,7 @@
 
 
 def solution(mesh):
-    assert mesh.shape["row"] % 2 == 0
+    assert mesh.shape["row"] % 4 == 0
     sizes = (mesh.shape["row"] // 2, mesh.shape["col"], mesh.shape["vec"])
     return jax.shard_map(
         functools.partial(shards, sizes),

time: 31.3 us -> 30.4 us (0.971)
  starting transfers between devices: 19 us -> 18 us
    ppermute x6 -> x4, starting transfers between devices: 9.55 us -> 6 us  [z_shift(): lax.ppermute(x, 'row', [(a, (a + 2 * s) % nrow) for a in range(nrow)])]
    ppermute x6 -> x4, waiting for transfers between devices: 1 us -> 3.28 us  [z_shift(): lax.ppermute(x, 'row', [(a, (a + 2 * s) % nrow) for a in range(nrow)])]
    ppermute x3, waiting for transfers between devices: 2.88 us -> 1.04 us  [send(): return lax.ppermute(x, ('row', 'col'), perm)]
    ppermute x0 -> x1, starting transfers between devices: none -> 1.59 us  [shards(): doubles.append(lax.ppermute(pieces[1 + p], 'row', perm))]
    ppermute x2 -> x4, starting transfers between devices: 0.29 us -> 1.35 us  [core_swap(): return lax.ppermute(x, 'row', [(a, a ^ 1) for a in range(nrow)])]
    ppermute x2, waiting for transfers between devices: 1.61 us -> 1.21 us  [swap(): return lax.ppermute(x, 'row', [(a, a ^ 1) for a in range(nrow)])]
  transfers between devices with their start and end apart: 16 -> 17, of which waited for: 5 -> 6; matrix products, arithmetic and copies ran while one was open for 2% -> 2% of each run, Pallas kernels for 11% -> 12%
where the time goes in v7:
time: 30.4 us; the launch traced here: 30.1 us
  starting transfers between devices  18 us (59%)
  waiting for transfers between devices  5.54 us (18%)
  Pallas kernels  3.86 us (13%)
  between operations  1.45 us (5%)
  other arithmetic  1.22 us (4%)
    ppermute x4, starting transfers between devices, z_shift(): lax.ppermute(x, 'row', [(a, (a + 2 * s) % nrow) for a in range(nrow)])  6 us
    ppermute x3, starting transfers between devices, send(): return lax.ppermute(x, ('row', 'col'), perm)  4.39 us
    ppermute x4, waiting for transfers between devices, z_shift(): lax.ppermute(x, 'row', [(a, (a + 2 * s) % nrow) for a in range(nrow)])  3.28 us
    ppermute x2, starting transfers between devices, col_shift(): return lax.ppermute(x, 'col', [(a, (a + t) % ncol) for a in range(ncol)])  3.11 us
    pallas_call x1, Pallas kernels, shards(): pl.pallas_call(functools.partial(forward_kernel, step), out_shape=[block]...  1.94 us
    ppermute x1, starting transfers between devices, shards(): doubles.append(lax.ppermute(pieces[1 + p], 'row', perm))  1.59 us
    ppermute x1, starting transfers between devices, vec_shift(): return lax.ppermute(x, 'vec', [(a, (a + t) % nvec) for a in range(nvec)])  1.58 us
    pallas_call x1, Pallas kernels, shards(): pl.pallas_call(functools.partial(mirror_kernel, step), out_shape=[ring, r...  1.57 us
  transfers between devices with their start and end apart: 17, of which 6 were waited for; matrix products, arithmetic and copies ran while one was open for 2% of the time, Pallas kernels for 12%

profile of v7, /device:TPU:0, one launch (start us, length us, event | category | flops | bytes accessed | tf_op | source)
XLA Modules:
  0.0 30.1 jit_solution(9672814259053842692)
XLA Ops:
  0.7 0.5 %collective-permute-start = (bf16[8,1024]{1,0:T(8,128)(2,1)}, bf16[8,1024]{1,0:T(8,128)(2,1)S(1)}, u32[]{:S(2)}, u32[]{:S(2)}) collective-permute-start(bf16[8,1024]{1,0:T(8,128)(2,1)} %x_hbm.1), channel_id=1, source_target_pairs={{0,4},{4,0},{8,12},{12,8},{16,20},{20,16},{24,28},{28,24},{1,5},{5... | collective-permute-start | bytes 49160 | tf_op jit(solution)/shard_map/ppermute | solution.py:248
  1.2 2.6 %collective-permute-start.1 = (bf16[8,1024]{1,0:T(8,128)(2,1)}, bf16[8,1024]{1,0:T(8,128)(2,1)S(1)}, u32[]{:S(2)}, u32[]{:S(2)}) collective-permute-start(bf16[8,1024]{1,0:T(8,128)(2,1)} %x_hbm.1), channel_id=1, source_target_pairs={{0,2},{2,0},{1,3},{3,1},{4,6},{6,4},{5,7},{7,5},{8,10},{10,8},{9,1... | collective-permute-start | bytes 49160 | tf_op jit(solution)/shard_map/ppermute | solution.py:254
  3.8 1.6 %collective-permute-start.5 = (bf16[8,1024]{1,0:T(8,128)(2,1)}, bf16[8,1024]{1,0:T(8,128)(2,1)S(1)}, u32[]{:S(2)}, u32[]{:S(2)}) collective-permute-start(bf16[8,1024]{1,0:T(8,128)(2,1)} %x_hbm.1), channel_id=1, source_target_pairs={{0,8},{4,12},{8,16},{12,20},{16,24},{20,28},{24,0},{28,4},{1,9},{5... | collective-permute-start | bytes 49160 | tf_op jit(solution)/shard_map/ppermute | solution.py:251
  5.3 2.6 %collective-permute-start.6 = (bf16[8,1024]{1,0:T(8,128)(2,1)}, bf16[8,1024]{1,0:T(8,128)(2,1)S(1)}, u32[]{:S(2)}, u32[]{:S(2)}) collective-permute-start(bf16[8,1024]{1,0:T(8,128)(2,1)} %x_hbm.1), channel_id=1, source_target_pairs={{0,16},{4,20},{8,24},{12,28},{16,0},{20,4},{24,8},{28,12},{1,17},{... | collective-permute-start | bytes 49160 | tf_op jit(solution)/shard_map/ppermute | solution.py:251
  7.9 1.3 %collective-permute-start.7 = (bf16[8,1024]{1,0:T(8,128)(2,1)}, bf16[8,1024]{1,0:T(8,128)(2,1)S(1)}, u32[]{:S(2)}, u32[]{:S(2)}) collective-permute-start(bf16[8,1024]{1,0:T(8,128)(2,1)} %x_hbm.1), channel_id=1, source_target_pairs={{0,24},{4,28},{8,0},{12,4},{16,8},{20,12},{24,16},{28,20},{1,25},{... | collective-permute-start | bytes 49160 | tf_op jit(solution)/shard_map/ppermute | solution.py:251
  9.9 0.0 collective-permute-done.sibling
  10.0 1.6 %mirror.1 = (f32[8,4096]{1,0:T(8,128)S(1)}, f32[8,4096]{1,0:T(8,128)S(1)}, bf16[8,1024]{1,0:T(8,128)(2,1)S(1)}, bf16[8,8192]{1,0:T(8,128)(2,1)S(1)}) custom-call(s32[1,1]{1,0:T(1,128)S(6)} %copy.10.counts, s32[1,256]{1,0:T(1,128)S(1)} %bitcast.8, s32[1,256]{1,0:T(1,128)S(1)} %bitcast.10, bf16[256,128,128]{2,1,0:T(8,128)(2,1)S(1)} %bitcast.6, ...), custom_call_target="tpu_custom_call" | custom-call | flops 134217728 | bytes 8388608 | tf_op jit(solution)/shard_map/mirror/pallas_call | solution.py:277
  11.5 0.1 collective-permute-start.2
  11.6 1.6 %collective-permute-start.9 = (bf16[8,8192]{1,0:T(8,128)(2,1)S(1)}, bf16[8,8192]{1,0:T(8,128)(2,1)S(1)}, u32[]{:S(2)}, u32[]{:S(2)}) collective-permute-start(bf16[8,8192]{1,0:T(8,128)(2,1)S(1)} %get-tuple-element.27.refs_5_), channel_id=1, source_target_pairs={{0,1},{1,0},{2,3},{3,2},{4,5},{5,4},{6,7},{7,6},{8,9},{9,8},{10,11... | collective-permute-start | bytes 393224 | tf_op jit(solution)/shard_map/ppermute | solution.py:257
  13.2 0.0 collective-permute-done.5
  13.2 0.0 collective-permute-done.7
  13.3 0.2 collective-permute-start.8
  13.5 0.0 collective-permute-done.2.theirs
  13.5 1.6 %collective-permute-start.4 = (f32[8,2048]{1,0:T(8,128)S(1)}, f32[8,2048]{1,0:T(8,128)S(1)}, u32[]{:S(2)}, u32[]{:S(2)}) collective-permute-start(f32[8,2048]{1,0:T(8,128)S(1)} %get-tuple-element.23), channel_id=1, source_target_pairs={{0,24},{4,20},{8,0},{12,28},{16,8},{20,4},{24,16},{28,12},{1,25},{... | collective-permute-start | bytes 196616 | tf_op jit(solution)/shard_map/ppermute | solution.py:307
  15.1 0.5 %collective-permute-start.3 = (f32[8,1024]{1,0:T(8,128)S(1)}, f32[8,1024]{1,0:T(8,128)S(1)}, u32[]{:S(2)}, u32[]{:S(2)}) collective-permute-start(f32[8,1024]{1,0:T(8,128)S(1)} %get-tuple-element.22), channel_id=1, source_target_pairs={{0,8},{4,12},{8,16},{12,20},{16,24},{20,28},{24,0},{28,4},{1,9},{5... | collective-permute-start | bytes 98312 | tf_op jit(solution)/shard_map/ppermute | solution.py:251
  15.6 0.0 collective-permute-done.8.far
  15.6 1.9 %forward.1 = (f32[8,1024]{1,0:T(8,128)S(1)}, f32[8,1024]{1,0:T(8,128)S(1)}) custom-call(s32[1,1]{1,0:T(1,128)S(6)} %copy.10.counts, s32[1,256]{1,0:T(1,128)S(1)} %bitcast.9, s32[1,256]{1,0:T(1,128)S(1)} %bitcast.11, bf16[256,128,128]{2,1,0:T(8,128)(2,1)S(1)} %bitcast.7, bf16[8,4096]{1,0:T(8,128)(2,1)S(1)} %constant_dynamic-update-slice_fusion.near, ...), custom_call_target="tpu_custom_call" | custom-call | flops 134217728 | bytes 8388608 | tf_op jit(solution)/shard_map/forward/pallas_call | solution.py:309
  17.5 0.0 collective-permute-done.9.refs_6_
  17.6 3.3 %collective-permute-done.3.refs_1_ = f32[8,1024]{1,0:T(8,128)S(1)} collective-permute-done((f32[8,1024]{1,0:T(8,128)S(1)}, f32[8,1024]{1,0:T(8,128)S(1)}, u32[]{:S(2)}, u32[]{:S(2)}) %collective-permute-start.3) | collective-permute-done | bytes 32800 | tf_op jit(solution)/shard_map/ppermute | solution.py:251
  20.8 0.3 %gram.1 = (f32[8,1024]{1,0:T(8,128)S(1)}, f32[8,1024]{1,0:T(8,128)S(1)}, f32[8,16]{1,0:T(8,128)S(1)}, f32[8,1152]{1,0:T(8,128)S(1)}) custom-call(f32[8,1024]{1,0:T(8,128)S(1)} %get-tuple-element.21.refs_0_, f32[8,1024]{1,0:T(8,128)S(1)} %collective-permute-done.3.refs_1_, f32[8,2048]{1,0:T(8,128)S(1)} %collective-permute-done.4.refs_2_, ...), custom_call_target="tpu_custom_call" | custom-call | tf_op jit(solution)/shard_map/gram/pallas_call | solution.py:322
  21.2 0.0 collective-permute-start.12
  21.2 0.5 %collective-permute-start.11 = (f32[8,1152]{1,0:T(8,128)S(1)}, f32[8,1152]{1,0:T(8,128)S(1)}, u32[]{:S(2)}, u32[]{:S(2)}) collective-permute-start(f32[8,1152]{1,0:T(8,128)S(1)} %get-tuple-element.30), channel_id=1, source_target_pairs={{0,2},{2,0},{1,3},{3,1},{4,6},{6,4},{5,7},{7,5},{8,10},{10,8},{9,1... | collective-permute-start | bytes 110600 | tf_op jit(solution)/shard_map/ppermute | solution.py:254
  21.7 0.7 %collective-permute-done.12 = f32[8,1152]{1,0:T(8,128)S(1)} collective-permute-done((f32[8,1152]{1,0:T(8,128)S(1)}, f32[8,1152]{1,0:T(8,128)S(1)}, u32[]{:S(2)}, u32[]{:S(2)}) %collective-permute-start.12) | collective-permute-done | bytes 36896 | tf_op jit(solution)/shard_map/ppermute | solution.py:354
  22.4 1.3 %collective-permute-start.15 = (f32[8,16]{1,0:T(8,128)S(1)}, f32[8,16]{1,0:T(8,128)S(1)}, u32[]{:S(2)}, u32[]{:S(2)}) collective-permute-start(f32[8,16]{1,0:T(8,128)S(1)} %slice_add_fusion.2), channel_id=1, source_target_pairs={{0,24},{2,26},{4,30},{6,28},{8,16},{10,18},{12,22},{14,20},{16,8},... | collective-permute-start | bytes 1544 | tf_op jit(solution)/shard_map/ppermute | solution.py:351
  23.7 3.1 %collective-permute-start.13 = (f32[8,16]{1,0:T(8,128)S(1)}, f32[8,16]{1,0:T(8,128)S(1)}, u32[]{:S(2)}, u32[]{:S(2)}) collective-permute-start(f32[8,16]{1,0:T(8,128)S(1)} %slice_add_fusion.2), channel_id=1, source_target_pairs={{0,8},{2,10},{4,14},{6,12},{8,0},{10,2},{12,6},{14,4},{16,24},{18,... | collective-permute-start | bytes 1544 | tf_op jit(solution)/shard_map/ppermute | solution.py:351
  26.8 0.5 %collective-permute-start.10 = (f32[8,1024]{1,0:T(8,128)S(1)}, f32[8,1024]{1,0:T(8,128)S(1)}, u32[]{:S(2)}, u32[]{:S(2)}) collective-permute-start(f32[8,1024]{1,0:T(8,128)S(1)} %get-tuple-element.29), channel_id=1, source_target_pairs={{0,4},{4,0},{8,12},{12,8},{16,20},{20,16},{24,28},{28,24},{1,5},{5... | collective-permute-start | bytes 98312 | tf_op jit(solution)/shard_map/ppermute | solution.py:248
  27.3 0.5 %collective-permute-done.15 = f32[8,16]{1,0:T(8,128)S(1)} collective-permute-done((f32[8,16]{1,0:T(8,128)S(1)}, f32[8,16]{1,0:T(8,128)S(1)}, u32[]{:S(2)}, u32[]{:S(2)}) %collective-permute-start.15) | collective-permute-done | bytes 544 | tf_op jit(solution)/shard_map/ppermute | solution.py:351
  27.8 0.4 %collective-permute-done.14 = f32[8,16]{1,0:T(8,128)S(1)} collective-permute-done((f32[8,16]{1,0:T(8,128)S(1)}, f32[8,16]{1,0:T(8,128)S(1)}, u32[]{:S(2)}, u32[]{:S(2)}) %collective-permute-start.14) | collective-permute-done | bytes 544 | tf_op jit(solution)/shard_map/ppermute | solution.py:351
  28.2 0.1 collective-permute-done.13
  28.4 0.6 %fusion = bf16[8,1024]{1,0:T(8,128)(2,1)} fusion(f32[8,1152]{1,0:T(8,128)S(1)} %collective-permute-done.11, f32[8,1024]{1,0:T(8,128)S(1)} %get-tuple-element.28, f32[8,1024]{1,0:T(8,128)S(1)} %collective-permute-done.10), kind=kLoop, calls=%fused_computation.1 | loop fusion | flops 24576 | bytes 114688 | tf_op jit(solution)/shard_map/convert_element_type | solution.py:338
  29.0 0.5 %collective-permute-done.16 = f32[8,16]{1,0:T(8,128)S(1)} collective-permute-done((f32[8,16]{1,0:T(8,128)S(1)}, f32[8,16]{1,0:T(8,128)S(1)}, u32[]{:S(2)}, u32[]{:S(2)}) %collective-permute-start.16) | collective-permute-done | bytes 544 | tf_op jit(solution)/shard_map/ppermute | solution.py:354
  29.5 0.6 %add_bitcast_fusion = f32[16,8]{0,1:T(8,128)} fusion(f32[8,16]{1,0:T(8,128)S(1)} %collective-permute-done.16, f32[8,16]{1,0:T(8,128)S(1)} %slice_add_fusion.2, f32[8,16]{1,0:T(8,128)S(1)} %fusion.2), kind=kLoop, calls=%fused_computation.10 | loop fusion | flops 256 | bytes 2048 | tf_op jit(solution)/shard_map/transpose | solution.py:337
  (21 shorter events, 0.1 us)
Async XLA Ops:
  0.6 9.3 %copy-start = (bf16[1,1,256,128,128]{4,3,2,1,0:T(8,128)(2,1)S(1)}, bf16[1,1,256,128,128]{4,3,2,1,0:T(8,128)(2,1)}, u32[]{:S(2)}) copy-start(bf16[1,1,256,128,128]{4,3,2,1,0:T(8,128)(2,1)} %param.6) | copy-start | bytes 25165828
  0.6 9.3 %copy-start.1 = (s32[1,1,256]{2,1,0:T(1,128)S(1)}, s32[1,1,256]{2,1,0:T(1,128)}, u32[]{:S(2)}) copy-start(s32[1,1,256]{2,1,0:T(1,128)} %param.7) | copy-start | bytes 3076
  0.7 9.3 %copy-start.2 = (s32[1,1,256]{2,1,0:T(1,128)S(1)}, s32[1,1,256]{2,1,0:T(1,128)}, u32[]{:S(2)}) copy-start(s32[1,1,256]{2,1,0:T(1,128)} %param.8) | copy-start | bytes 3076
  0.7 9.3 %collective-permute-start = (bf16[8,1024]{1,0:T(8,128)(2,1)}, bf16[8,1024]{1,0:T(8,128)(2,1)S(1)}, u32[]{:S(2)}, u32[]{:S(2)}) collective-permute-start(bf16[8,1024]{1,0:T(8,128)(2,1)} %x_hbm.1), channel_id=1, source_target_pairs={{0,4},{4,0},{8,12},{12,8},{16,20},{20,16},{24,28},{28,24},{1,5},{5... | collective-permute-start | bytes 49160 | tf_op jit(solution)/shard_map/ppermute | solution.py:248
  1.2 8.7 %collective-permute-start.1 = (bf16[8,1024]{1,0:T(8,128)(2,1)}, bf16[8,1024]{1,0:T(8,128)(2,1)S(1)}, u32[]{:S(2)}, u32[]{:S(2)}) collective-permute-start(bf16[8,1024]{1,0:T(8,128)(2,1)} %x_hbm.1), channel_id=1, source_target_pairs={{0,2},{2,0},{1,3},{3,1},{4,6},{6,4},{5,7},{7,5},{8,10},{10,8},{9,1... | collective-permute-start | bytes 49160 | tf_op jit(solution)/shard_map/ppermute | solution.py:254
  3.8 9.5 %collective-permute-start.5 = (bf16[8,1024]{1,0:T(8,128)(2,1)}, bf16[8,1024]{1,0:T(8,128)(2,1)S(1)}, u32[]{:S(2)}, u32[]{:S(2)}) collective-permute-start(bf16[8,1024]{1,0:T(8,128)(2,1)} %x_hbm.1), channel_id=1, source_target_pairs={{0,8},{4,12},{8,16},{12,20},{16,24},{20,28},{24,0},{28,4},{1,9},{5... | collective-permute-start | bytes 49160 | tf_op jit(solution)/shard_map/ppermute | solution.py:251
  5.3 7.9 %collective-permute-start.6 = (bf16[8,1024]{1,0:T(8,128)(2,1)}, bf16[8,1024]{1,0:T(8,128)(2,1)S(1)}, u32[]{:S(2)}, u32[]{:S(2)}) collective-permute-start(bf16[8,1024]{1,0:T(8,128)(2,1)} %x_hbm.1), channel_id=1, source_target_pairs={{0,16},{4,20},{8,24},{12,28},{16,0},{20,4},{24,8},{28,12},{1,17},{... | collective-permute-start | bytes 49160 | tf_op jit(solution)/shard_map/ppermute | solution.py:251
  7.9 5.3 %collective-permute-start.7 = (bf16[8,1024]{1,0:T(8,128)(2,1)}, bf16[8,1024]{1,0:T(8,128)(2,1)S(1)}, u32[]{:S(2)}, u32[]{:S(2)}) collective-permute-start(bf16[8,1024]{1,0:T(8,128)(2,1)} %x_hbm.1), channel_id=1, source_target_pairs={{0,24},{4,28},{8,0},{12,4},{16,8},{20,12},{24,16},{28,20},{1,25},{... | collective-permute-start | bytes 49160 | tf_op jit(solution)/shard_map/ppermute | solution.py:251
  11.5 1.9 %collective-permute-start.2 = (f32[8,4096]{1,0:T(8,128)S(1)}, f32[8,4096]{1,0:T(8,128)S(1)}, u32[]{:S(2)}, u32[]{:S(2)}) collective-permute-start(f32[8,4096]{1,0:T(8,128)S(1)} %get-tuple-element.20), channel_id=1, source_target_pairs={{0,4},{4,0},{8,12},{12,8},{16,20},{20,16},{24,28},{28,24},{1,5},{5... | collective-permute-start | bytes 393224 | tf_op jit(solution)/shard_map/ppermute | solution.py:248
  11.6 5.9 %collective-permute-start.9 = (bf16[8,8192]{1,0:T(8,128)(2,1)S(1)}, bf16[8,8192]{1,0:T(8,128)(2,1)S(1)}, u32[]{:S(2)}, u32[]{:S(2)}) collective-permute-start(bf16[8,8192]{1,0:T(8,128)(2,1)S(1)} %get-tuple-element.27.refs_5_), channel_id=1, source_target_pairs={{0,1},{1,0},{2,3},{3,2},{4,5},{5,4},{6,7},{7,6},{8,9},{9,8},{10,11... | collective-permute-start | bytes 393224 | tf_op jit(solution)/shard_map/ppermute | solution.py:257
  13.3 2.3 %collective-permute-start.8 = (bf16[8,4096]{1,0:T(8,128)(2,1)S(1)}, bf16[8,4096]{1,0:T(8,128)(2,1)S(1)}, u32[]{:S(2)}, u32[]{:S(2)}) collective-permute-start(bf16[8,4096]{1,0:T(8,128)(2,1)S(1)} %constant_dynamic-update-slice_fusion.near), channel_id=1, source_target_pairs={{0,4},{4,0},{8,12},{12,8},{16,20},{20,16},{24,28},{28,24},{1,5},{5... | collective-permute-start | bytes 196616 | tf_op jit(solution)/shard_map/ppermute | solution.py:248
  13.5 7.3 %collective-permute-start.4 = (f32[8,2048]{1,0:T(8,128)S(1)}, f32[8,2048]{1,0:T(8,128)S(1)}, u32[]{:S(2)}, u32[]{:S(2)}) collective-permute-start(f32[8,2048]{1,0:T(8,128)S(1)} %get-tuple-element.23), channel_id=1, source_target_pairs={{0,24},{4,20},{8,0},{12,28},{16,8},{20,4},{24,16},{28,12},{1,25},{... | collective-permute-start | bytes 196616 | tf_op jit(solution)/shard_map/ppermute | solution.py:307
  15.1 5.7 %collective-permute-start.3 = (f32[8,1024]{1,0:T(8,128)S(1)}, f32[8,1024]{1,0:T(8,128)S(1)}, u32[]{:S(2)}, u32[]{:S(2)}) collective-permute-start(f32[8,1024]{1,0:T(8,128)S(1)} %get-tuple-element.22), channel_id=1, source_target_pairs={{0,8},{4,12},{8,16},{12,20},{16,24},{20,28},{24,0},{28,4},{1,9},{5... | collective-permute-start | bytes 98312 | tf_op jit(solution)/shard_map/ppermute | solution.py:251
  21.2 1.2 %collective-permute-start.12 = (f32[8,1152]{1,0:T(8,128)S(1)}, f32[8,1152]{1,0:T(8,128)S(1)}, u32[]{:S(2)}, u32[]{:S(2)}) collective-permute-start(f32[8,1152]{1,0:T(8,128)S(1)} %get-tuple-element.30), channel_id=1, source_target_pairs={{0,4},{4,0},{8,12},{12,8},{16,20},{20,16},{24,28},{28,24},{1,5},{5... | collective-permute-start | bytes 110600 | tf_op jit(solution)/shard_map/ppermute | solution.py:354
  21.2 6.2 %collective-permute-start.11 = (f32[8,1152]{1,0:T(8,128)S(1)}, f32[8,1152]{1,0:T(8,128)S(1)}, u32[]{:S(2)}, u32[]{:S(2)}) collective-permute-start(f32[8,1152]{1,0:T(8,128)S(1)} %get-tuple-element.30), channel_id=1, source_target_pairs={{0,2},{2,0},{1,3},{3,1},{4,6},{6,4},{5,7},{7,5},{8,10},{10,8},{9,1... | collective-permute-start | bytes 110600 | tf_op jit(solution)/shard_map/ppermute | solution.py:254
  22.4 5.4 %collective-permute-start.15 = (f32[8,16]{1,0:T(8,128)S(1)}, f32[8,16]{1,0:T(8,128)S(1)}, u32[]{:S(2)}, u32[]{:S(2)}) collective-permute-start(f32[8,16]{1,0:T(8,128)S(1)} %slice_add_fusion.2), channel_id=1, source_target_pairs={{0,24},{2,26},{4,30},{6,28},{8,16},{10,18},{12,22},{14,20},{16,8},... | collective-permute-start | bytes 1544 | tf_op jit(solution)/shard_map/ppermute | solution.py:351
  23.7 4.5 %collective-permute-start.14 = (f32[8,16]{1,0:T(8,128)S(1)}, f32[8,16]{1,0:T(8,128)S(1)}, u32[]{:S(2)}, u32[]{:S(2)}) collective-permute-start(f32[8,16]{1,0:T(8,128)S(1)} %slice_add_fusion.2), channel_id=1, source_target_pairs={{0,16},{2,18},{4,22},{6,20},{8,24},{10,26},{12,30},{14,28},{16,0},... | collective-permute-start | bytes 1544 | tf_op jit(solution)/shard_map/ppermute | solution.py:351
  23.7 4.7 %collective-permute-start.13 = (f32[8,16]{1,0:T(8,128)S(1)}, f32[8,16]{1,0:T(8,128)S(1)}, u32[]{:S(2)}, u32[]{:S(2)}) collective-permute-start(f32[8,16]{1,0:T(8,128)S(1)} %slice_add_fusion.2), channel_id=1, source_target_pairs={{0,8},{2,10},{4,14},{6,12},{8,0},{10,2},{12,6},{14,4},{16,24},{18,... | collective-permute-start | bytes 1544 | tf_op jit(solution)/shard_map/ppermute | solution.py:351
  26.8 1.6 %collective-permute-start.10 = (f32[8,1024]{1,0:T(8,128)S(1)}, f32[8,1024]{1,0:T(8,128)S(1)}, u32[]{:S(2)}, u32[]{:S(2)}) collective-permute-start(f32[8,1024]{1,0:T(8,128)S(1)} %get-tuple-element.29), channel_id=1, source_target_pairs={{0,4},{4,0},{8,12},{12,8},{16,20},{20,16},{24,28},{28,24},{1,5},{5... | collective-permute-start | bytes 98312 | tf_op jit(solution)/shard_map/ppermute | solution.py:248
  28.4 1.2 %collective-permute-start.16 = (f32[8,16]{1,0:T(8,128)S(1)}, f32[8,16]{1,0:T(8,128)S(1)}, u32[]{:S(2)}, u32[]{:S(2)}) collective-permute-start(f32[8,16]{1,0:T(8,128)S(1)} %fusion.2), channel_id=1, source_target_pairs={{0,4},{4,0},{8,12},{12,8},{16,20},{20,16},{24,28},{28,24},{1,5},{5... | collective-permute-start | bytes 1544 | tf_op jit(solution)/shard_map/ppermute | solution.py:354

commit v8 on v7

--- a/solution.py
+++ b/solution.py
@@ -127,7 +127,7 @@
     for out, c in ((mine, core), (other, 1 - core)):
         wanted = [(z, c)]
         for p in range((nz - 2) // 2):
-            wanted += [(z + nz - (2 * p + 1 + c), 0), (z + nz - (2 * p + 1 + c), 1)]
+            wanted += [(z + nz - (2 * p + 2 - c), 0), (z + nz - (2 * p + 2 - c), 1)]
         wanted += [(z + 1, c)]
         for n, (to, half) in enumerate(wanted):
             for q in range(stretch):
@@ -181,7 +181,7 @@
 def gram_kernel(nz, ncol, nvec, scale, *refs):
     cols, doubles, refs = refs[:2], refs[2 : 2 + (nz - 2) // 2], refs[2 + (nz - 2) // 2 :]
     parts, refs = refs[:ncol], refs[ncol:]
-    xs, (image, give, share, *messages) = refs[:nvec], refs[nvec:]
+    xs, (image, share, give, *messages) = refs[:nvec], refs[nvec:]
     width = image.shape[1]
     core = lax.rem(lax.axis_index("row"), 2)
     kept = pl.ds(pl.multiple_of(core * width, width), width)
@@ -194,7 +194,6 @@
         total += ref[:, kept]
         away += ref[:, given]
     image[...] = total
-    give[...] = away
     terms = jnp.concatenate([total] + [parts[ncol - t][...] for t in range(1, ncol)] + [away], axis=1)
     split = []
     rest = terms
@@ -214,9 +213,8 @@
         for k in range(1, nvec):
             picked = jnp.where(lax.rem(me + nvec - a, nvec) == k, products[k], picked)
         share[:, a * picked.shape[1] : (a + 1) * picked.shape[1]] = picked
-    for t in range(1, ncol):
-        message = messages[t - 1]
-        message[:, :width] = parts[t][...]
+    for message, rows in zip((give, *messages), (away, *(ref[...] for ref in parts[1:]))):
+        message[:, :width] = rows
         message[:, width:] = jnp.zeros_like(message[:, width:])
         message[:, width : width + share.shape[1]] = share[...]
 
@@ -303,7 +301,7 @@
     last = z_shift(pieces[-1], 1)
     doubles = []
     for p in range(pairs):
-        perm = [(a, (a - 2 * (2 * p + 1 + a % 2)) % nrow) for a in range(nrow)]
+        perm = [(a, (a - 2 * (2 * p + 2 - a % 2)) % nrow) for a in range(nrow)]
         doubles.append(lax.ppermute(pieces[1 + p], "row", perm))
     col_parts = [pieces[0], last] + doubles
     row_parts = pl.pallas_call(
@@ -319,28 +317,30 @@
     every_x = [wide] + [vec_shift(wide, t) for t in range(1, nvec)]
     pad = -(-nvec * vlocal // tile) * tile
     message = jax.ShapeDtypeStruct((vlocal, width + pad), F32)
-    image, give, share, *messages = pl.pallas_call(
+    image, share, give, *messages = pl.pallas_call(
         functools.partial(gram_kernel, nz, ncol, nvec, 1.0 / math.sqrt(width * nrow * ncol)),
-        out_shape=[block, block, jax.ShapeDtypeStruct((vlocal, nvec * vlocal), F32)] + [message] * (ncol - 1),
+        out_shape=[block, jax.ShapeDtypeStruct((vlocal, nvec * vlocal), F32)] + [message] * ncol,
         in_specs=[VMEM] * (2 + pairs + ncol + nvec),
         out_specs=[VMEM] * (ncol + 2),
         compiler_params=params(6),
         name="gram",
     )(*col_parts, *row_parts, *every_x)
-    image = image + core_swap(give)
+    swapped = core_swap(give)
+    image = image + swapped[:, :width]
+    share = share + swapped[:, width : width + share.shape[1]]
     got = jnp.zeros_like(share)
     for t in range(1, ncol):
         message = col_shift(messages[t - 1], t)
         image = image + message[:, :width]
         got = got + message[:, width : width + share.shape[1]]
-    share = all_sum(share, got, nz, ncol, messages[0])
+    share = all_sum(share, got, nz, ncol)
     gram = share.T
     return (image.astype(jnp.bfloat16), gram)
 
 
-def all_sum(share, got, nz, ncol, message):
+def all_sum(share, got, nz, ncol):
     if nz * ncol > 8 or nz & (nz - 1) or ncol % 2:
-        return lax.psum(share, ("row", "col"))
+        return 0.5 * lax.psum(share, ("row", "col"))
     nrow = 2 * nz
 
     def send(x, s, t):
@@ -353,7 +353,6 @@
     def swap(x):
         return lax.ppermute(x, "row", [(a, a ^ 1) for a in range(nrow)])
 
-    share = share + swap(message)[:, -(-share.shape[1] // 128) * 128 * -1 :][:, : share.shape[1]]
     for s in range(1, nz):
         for t in range(0, ncol, 2):
             got = got + send(share, s, t)

time: 30.4 us -> 30.2 us (level)
    ppermute x2 -> x1, waiting for transfers between devices: 1.21 us -> 0.51 us  [swap(): return lax.ppermute(x, 'row', [(a, a ^ 1) for a in range(nrow)])]
    ppermute x3, waiting for transfers between devices: 1.04 us -> 1.72 us  [send(): return lax.ppermute(x, ('row', 'col'), perm)]
    ppermute x4, waiting for transfers between devices: 0.01 us -> 0.68 us  [core_swap(): return lax.ppermute(x, 'row', [(a, a ^ 1) for a in range(nrow)])]
    ppermute x4, starting transfers between devices: 6 us -> 6.57 us  [z_shift(): lax.ppermute(x, 'row', [(a, (a + 2 * s) % nrow) for a in range(nrow)])]
    ppermute x4, starting transfers between devices: 1.35 us -> 0.81 us  [core_swap(): return lax.ppermute(x, 'row', [(a, a ^ 1) for a in range(nrow)])]
    ppermute x1, starting transfers between devices: 1.59 us -> 1.1 us  [shards(): doubles.append(lax.ppermute(pieces[1 + p], 'row', perm))]
    ppermute x4, waiting for transfers between devices: 3.28 us -> 2.8 us  [z_shift(): lax.ppermute(x, 'row', [(a, (a + 2 * s) % nrow) for a in range(nrow)])]
  transfers between devices with their start and end apart: 17 -> 16, of which waited for: 6 -> 5; matrix products, arithmetic and copies ran while one was open for 2% -> 2% of each run, Pallas kernels for 12% -> 12%
where the time goes in v8:
time: 30.2 us; the launch traced here: 29.9 us
  starting transfers between devices  17.7 us (59%)
  waiting for transfers between devices  5.72 us (19%)
  Pallas kernels  3.86 us (13%)
  between operations  1.44 us (5%)
  other arithmetic  1.22 us (4%)
    ppermute x4, starting transfers between devices, z_shift(): lax.ppermute(x, 'row', [(a, (a + 2 * s) % nrow) for a in range(nrow)])  6.57 us
    ppermute x3, starting transfers between devices, send(): return lax.ppermute(x, ('row', 'col'), perm)  4.39 us
    ppermute x2, starting transfers between devices, col_shift(): return lax.ppermute(x, 'col', [(a, (a + t) % ncol) for a in range(ncol)])  3.11 us
    ppermute x4, waiting for transfers between devices, z_shift(): lax.ppermute(x, 'row', [(a, (a + 2 * s) % nrow) for a in range(nrow)])  2.8 us
    pallas_call x1, Pallas kernels, shards(): pl.pallas_call(functools.partial(forward_kernel, step), out_shape=[block]...  1.94 us
    ppermute x3, waiting for transfers between devices, send(): return lax.ppermute(x, ('row', 'col'), perm)  1.72 us
    ppermute x1, starting transfers between devices, vec_shift(): return lax.ppermute(x, 'vec', [(a, (a + t) % nvec) for a in range(nvec)])  1.58 us
    pallas_call x1, Pallas kernels, shards(): pl.pallas_call(functools.partial(mirror_kernel, step), out_shape=[ring, r...  1.56 us
  transfers between devices with their start and end apart: 16, of which 5 were waited for; matrix products, arithmetic and copies ran while one was open for 2% of the time, Pallas kernels for 12%

profile of v8, /device:TPU:0, one launch (start us, length us, event | category | flops | bytes accessed | tf_op | source)
XLA Modules:
  0.0 29.9 jit_solution(1485829557413829382)
XLA Ops:
  0.7 0.5 %collective-permute-start = (bf16[8,1024]{1,0:T(8,128)(2,1)}, bf16[8,1024]{1,0:T(8,128)(2,1)S(1)}, u32[]{:S(2)}, u32[]{:S(2)}) collective-permute-start(bf16[8,1024]{1,0:T(8,128)(2,1)} %x_hbm.1), channel_id=1, source_target_pairs={{0,4},{4,0},{8,12},{12,8},{16,20},{20,16},{24,28},{28,24},{1,5},{5... | collective-permute-start | bytes 49160 | tf_op jit(solution)/shard_map/ppermute | solution.py:246
  1.2 2.6 %collective-permute-start.1 = (bf16[8,1024]{1,0:T(8,128)(2,1)}, bf16[8,1024]{1,0:T(8,128)(2,1)S(1)}, u32[]{:S(2)}, u32[]{:S(2)}) collective-permute-start(bf16[8,1024]{1,0:T(8,128)(2,1)} %x_hbm.1), channel_id=1, source_target_pairs={{0,2},{2,0},{1,3},{3,1},{4,6},{6,4},{5,7},{7,5},{8,10},{10,8},{9,1... | collective-permute-start | bytes 49160 | tf_op jit(solution)/shard_map/ppermute | solution.py:252
  3.8 1.6 %collective-permute-start.5 = (bf16[8,1024]{1,0:T(8,128)(2,1)}, bf16[8,1024]{1,0:T(8,128)(2,1)S(1)}, u32[]{:S(2)}, u32[]{:S(2)}) collective-permute-start(bf16[8,1024]{1,0:T(8,128)(2,1)} %x_hbm.1), channel_id=1, source_target_pairs={{0,8},{4,12},{8,16},{12,20},{16,24},{20,28},{24,0},{28,4},{1,9},{5... | collective-permute-start | bytes 49160 | tf_op jit(solution)/shard_map/ppermute | solution.py:249
  5.3 2.6 %collective-permute-start.6 = (bf16[8,1024]{1,0:T(8,128)(2,1)}, bf16[8,1024]{1,0:T(8,128)(2,1)S(1)}, u32[]{:S(2)}, u32[]{:S(2)}) collective-permute-start(bf16[8,1024]{1,0:T(8,128)(2,1)} %x_hbm.1), channel_id=1, source_target_pairs={{0,16},{4,20},{8,24},{12,28},{16,0},{20,4},{24,8},{28,12},{1,17},{... | collective-permute-start | bytes 49160 | tf_op jit(solution)/shard_map/ppermute | solution.py:249
  7.9 1.3 %collective-permute-start.7 = (bf16[8,1024]{1,0:T(8,128)(2,1)}, bf16[8,1024]{1,0:T(8,128)(2,1)S(1)}, u32[]{:S(2)}, u32[]{:S(2)}) collective-permute-start(bf16[8,1024]{1,0:T(8,128)(2,1)} %x_hbm.1), channel_id=1, source_target_pairs={{0,24},{4,28},{8,0},{12,4},{16,8},{20,12},{24,16},{28,20},{1,25},{... | collective-permute-start | bytes 49160 | tf_op jit(solution)/shard_map/ppermute | solution.py:249
  9.9 0.0 collective-permute-done.sibling
  9.9 0.0 collective-permute-done.1.refs_0_
  10.0 1.6 %mirror.1 = (f32[8,4096]{1,0:T(8,128)S(1)}, f32[8,4096]{1,0:T(8,128)S(1)}, bf16[8,1024]{1,0:T(8,128)(2,1)S(1)}, bf16[8,8192]{1,0:T(8,128)(2,1)S(1)}) custom-call(s32[1,1]{1,0:T(1,128)S(6)} %copy.10.counts, s32[1,256]{1,0:T(1,128)S(1)} %bitcast.8, s32[1,256]{1,0:T(1,128)S(1)} %bitcast.10, bf16[256,128,128]{2,1,0:T(8,128)(2,1)S(1)} %bitcast.6, ...), custom_call_target="tpu_custom_call" | custom-call | flops 134217728 | bytes 8388608 | tf_op jit(solution)/shard_map/mirror/pallas_call | solution.py:275
  11.5 0.1 collective-permute-start.2
  11.6 1.6 %collective-permute-start.9 = (bf16[8,8192]{1,0:T(8,128)(2,1)S(1)}, bf16[8,8192]{1,0:T(8,128)(2,1)S(1)}, u32[]{:S(2)}, u32[]{:S(2)}) collective-permute-start(bf16[8,8192]{1,0:T(8,128)(2,1)S(1)} %get-tuple-element.27.refs_5_), channel_id=1, source_target_pairs={{0,1},{1,0},{2,3},{3,2},{4,5},{5,4},{6,7},{7,6},{8,9},{9,8},{10,11... | collective-permute-start | bytes 393224 | tf_op jit(solution)/shard_map/ppermute | solution.py:255
  13.2 0.0 collective-permute-done.5
  13.2 0.0 collective-permute-done.6
  13.2 0.0 collective-permute-done.7
  13.3 0.2 collective-permute-start.8
  13.5 0.0 collective-permute-done.2.theirs
  13.5 1.1 %collective-permute-start.4 = (f32[8,2048]{1,0:T(8,128)S(1)}, f32[8,2048]{1,0:T(8,128)S(1)}, u32[]{:S(2)}, u32[]{:S(2)}) collective-permute-start(f32[8,2048]{1,0:T(8,128)S(1)} %get-tuple-element.23), channel_id=1, source_target_pairs={{0,16},{4,28},{8,24},{12,4},{16,0},{20,12},{24,8},{28,20},{1,17},{... | collective-permute-start | bytes 196616 | tf_op jit(solution)/shard_map/ppermute | solution.py:305
  14.6 1.1 %collective-permute-start.3 = (f32[8,1024]{1,0:T(8,128)S(1)}, f32[8,1024]{1,0:T(8,128)S(1)}, u32[]{:S(2)}, u32[]{:S(2)}) collective-permute-start(f32[8,1024]{1,0:T(8,128)S(1)} %get-tuple-element.22), channel_id=1, source_target_pairs={{0,8},{4,12},{8,16},{12,20},{16,24},{20,28},{24,0},{28,4},{1,9},{5... | collective-permute-start | bytes 98312 | tf_op jit(solution)/shard_map/ppermute | solution.py:249
  15.7 0.0 collective-permute-done.8.far
  15.7 1.9 %forward.1 = (f32[8,1024]{1,0:T(8,128)S(1)}, f32[8,1024]{1,0:T(8,128)S(1)}) custom-call(s32[1,1]{1,0:T(1,128)S(6)} %copy.10.counts, s32[1,256]{1,0:T(1,128)S(1)} %bitcast.9, s32[1,256]{1,0:T(1,128)S(1)} %bitcast.11, bf16[256,128,128]{2,1,0:T(8,128)(2,1)S(1)} %bitcast.7, bf16[8,4096]{1,0:T(8,128)(2,1)S(1)} %constant_dynamic-update-slice_fusion.near, ...), custom_call_target="tpu_custom_call" | custom-call | flops 134217728 | bytes 8388608 | tf_op jit(solution)/shard_map/forward/pallas_call | solution.py:307
  17.6 0.0 collective-permute-done.9.refs_6_
  17.6 2.8 %collective-permute-done.3.refs_1_ = f32[8,1024]{1,0:T(8,128)S(1)} collective-permute-done((f32[8,1024]{1,0:T(8,128)S(1)}, f32[8,1024]{1,0:T(8,128)S(1)}, u32[]{:S(2)}, u32[]{:S(2)}) %collective-permute-start.3) | collective-permute-done | bytes 32800 | tf_op jit(solution)/shard_map/ppermute | solution.py:249
  20.4 0.3 %gram.1 = (f32[8,1024]{1,0:T(8,128)S(1)}, f32[8,16]{1,0:T(8,128)S(1)}, f32[8,1152]{1,0:T(8,128)S(1)}, f32[8,1152]{1,0:T(8,128)S(1)}) custom-call(f32[8,1024]{1,0:T(8,128)S(1)} %get-tuple-element.21.refs_0_, f32[8,1024]{1,0:T(8,128)S(1)} %collective-permute-done.3.refs_1_, f32[8,2048]{1,0:T(8,128)S(1)} %collective-permute-done.4.refs_2_, ...), custom_call_target="tpu_custom_call" | custom-call | tf_op jit(solution)/shard_map/gram/pallas_call | solution.py:320
  20.8 0.5 %collective-permute-start.11 = (f32[8,1152]{1,0:T(8,128)S(1)}, f32[8,1152]{1,0:T(8,128)S(1)}, u32[]{:S(2)}, u32[]{:S(2)}) collective-permute-start(f32[8,1152]{1,0:T(8,128)S(1)} %get-tuple-element.30), channel_id=1, source_target_pairs={{0,2},{2,0},{1,3},{3,1},{4,6},{6,4},{5,7},{7,5},{8,10},{10,8},{9,1... | collective-permute-start | bytes 110600 | tf_op jit(solution)/shard_map/ppermute | solution.py:252
  21.3 0.7 %collective-permute-done.10 = f32[8,1152]{1,0:T(8,128)S(1)} collective-permute-done((f32[8,1152]{1,0:T(8,128)S(1)}, f32[8,1152]{1,0:T(8,128)S(1)}, u32[]{:S(2)}, u32[]{:S(2)}) %collective-permute-start.10) | collective-permute-done | bytes 36896 | tf_op jit(solution)/shard_map/ppermute | solution.py:246
  22.0 1.6 %collective-permute-start.14 = (f32[8,16]{1,0:T(8,128)S(1)}, f32[8,16]{1,0:T(8,128)S(1)}, u32[]{:S(2)}, u32[]{:S(2)}) collective-permute-start(f32[8,16]{1,0:T(8,128)S(1)} %slice_add_fusion.3), channel_id=1, source_target_pairs={{0,24},{2,26},{4,30},{6,28},{8,16},{10,18},{12,22},{14,20},{16,8},... | collective-permute-start | bytes 1544 | tf_op jit(solution)/shard_map/ppermute | solution.py:351
  23.6 2.8 %collective-permute-start.12 = (f32[8,16]{1,0:T(8,128)S(1)}, f32[8,16]{1,0:T(8,128)S(1)}, u32[]{:S(2)}, u32[]{:S(2)}) collective-permute-start(f32[8,16]{1,0:T(8,128)S(1)} %slice_add_fusion.3), channel_id=1, source_target_pairs={{0,8},{2,10},{4,14},{6,12},{8,0},{10,2},{12,6},{14,4},{16,24},{18,... | collective-permute-start | bytes 1544 | tf_op jit(solution)/shard_map/ppermute | solution.py:351
  26.4 1.0 %collective-permute-done.14 = f32[8,16]{1,0:T(8,128)S(1)} collective-permute-done((f32[8,16]{1,0:T(8,128)S(1)}, f32[8,16]{1,0:T(8,128)S(1)}, u32[]{:S(2)}, u32[]{:S(2)}) %collective-permute-start.14) | collective-permute-done | bytes 544 | tf_op jit(solution)/shard_map/ppermute | solution.py:351
  27.4 0.7 %collective-permute-done.13 = f32[8,16]{1,0:T(8,128)S(1)} collective-permute-done((f32[8,16]{1,0:T(8,128)S(1)}, f32[8,16]{1,0:T(8,128)S(1)}, u32[]{:S(2)}, u32[]{:S(2)}) %collective-permute-start.13) | collective-permute-done | bytes 544 | tf_op jit(solution)/shard_map/ppermute | solution.py:351
  28.1 0.1 collective-permute-start.15
  28.2 0.6 %fusion = bf16[8,1024]{1,0:T(8,128)(2,1)} fusion(f32[8,1152]{1,0:T(8,128)S(1)} %collective-permute-done.11, f32[8,1024]{1,0:T(8,128)S(1)} %get-tuple-element.28, f32[8,1152]{1,0:T(8,128)S(1)} %collective-permute-done.10), kind=kLoop, calls=%fused_computation.1 | loop fusion | flops 24576 | bytes 114688 | tf_op jit(solution)/shard_map/convert_element_type | solution.py:338
  28.8 0.5 %collective-permute-done.15 = f32[8,16]{1,0:T(8,128)S(1)} collective-permute-done((f32[8,16]{1,0:T(8,128)S(1)}, f32[8,16]{1,0:T(8,128)S(1)}, u32[]{:S(2)}, u32[]{:S(2)}) %collective-permute-start.15) | collective-permute-done | bytes 544 | tf_op jit(solution)/shard_map/ppermute | solution.py:354
  29.3 0.6 %add_bitcast_fusion = f32[16,8]{0,1:T(8,128)} fusion(f32[8,16]{1,0:T(8,128)S(1)} %collective-permute-done.15, f32[8,16]{1,0:T(8,128)S(1)} %slice_add_fusion.3, f32[8,16]{1,0:T(8,128)S(1)} %fusion.2), kind=kLoop, calls=%fused_computation.11 | loop fusion | flops 256 | bytes 2048 | tf_op jit(solution)/shard_map/transpose | solution.py:337
  (19 shorter events, 0.1 us)
Async XLA Ops:
  0.6 9.3 %copy-start = (bf16[1,1,256,128,128]{4,3,2,1,0:T(8,128)(2,1)S(1)}, bf16[1,1,256,128,128]{4,3,2,1,0:T(8,128)(2,1)}, u32[]{:S(2)}) copy-start(bf16[1,1,256,128,128]{4,3,2,1,0:T(8,128)(2,1)} %param.6) | copy-start | bytes 25165828
  0.6 9.3 %copy-start.1 = (s32[1,1,256]{2,1,0:T(1,128)S(1)}, s32[1,1,256]{2,1,0:T(1,128)}, u32[]{:S(2)}) copy-start(s32[1,1,256]{2,1,0:T(1,128)} %param.7) | copy-start | bytes 3076
  0.7 9.3 %copy-start.2 = (s32[1,1,256]{2,1,0:T(1,128)S(1)}, s32[1,1,256]{2,1,0:T(1,128)}, u32[]{:S(2)}) copy-start(s32[1,1,256]{2,1,0:T(1,128)} %param.8) | copy-start | bytes 3076
  0.7 9.3 %collective-permute-start = (bf16[8,1024]{1,0:T(8,128)(2,1)}, bf16[8,1024]{1,0:T(8,128)(2,1)S(1)}, u32[]{:S(2)}, u32[]{:S(2)}) collective-permute-start(bf16[8,1024]{1,0:T(8,128)(2,1)} %x_hbm.1), channel_id=1, source_target_pairs={{0,4},{4,0},{8,12},{12,8},{16,20},{20,16},{24,28},{28,24},{1,5},{5... | collective-permute-start | bytes 49160 | tf_op jit(solution)/shard_map/ppermute | solution.py:246
  1.2 8.7 %collective-permute-start.1 = (bf16[8,1024]{1,0:T(8,128)(2,1)}, bf16[8,1024]{1,0:T(8,128)(2,1)S(1)}, u32[]{:S(2)}, u32[]{:S(2)}) collective-permute-start(bf16[8,1024]{1,0:T(8,128)(2,1)} %x_hbm.1), channel_id=1, source_target_pairs={{0,2},{2,0},{1,3},{3,1},{4,6},{6,4},{5,7},{7,5},{8,10},{10,8},{9,1... | collective-permute-start | bytes 49160 | tf_op jit(solution)/shard_map/ppermute | solution.py:252
  3.8 9.5 %collective-permute-start.5 = (bf16[8,1024]{1,0:T(8,128)(2,1)}, bf16[8,1024]{1,0:T(8,128)(2,1)S(1)}, u32[]{:S(2)}, u32[]{:S(2)}) collective-permute-start(bf16[8,1024]{1,0:T(8,128)(2,1)} %x_hbm.1), channel_id=1, source_target_pairs={{0,8},{4,12},{8,16},{12,20},{16,24},{20,28},{24,0},{28,4},{1,9},{5... | collective-permute-start | bytes 49160 | tf_op jit(solution)/shard_map/ppermute | solution.py:249
  5.3 7.9 %collective-permute-start.6 = (bf16[8,1024]{1,0:T(8,128)(2,1)}, bf16[8,1024]{1,0:T(8,128)(2,1)S(1)}, u32[]{:S(2)}, u32[]{:S(2)}) collective-permute-start(bf16[8,1024]{1,0:T(8,128)(2,1)} %x_hbm.1), channel_id=1, source_target_pairs={{0,16},{4,20},{8,24},{12,28},{16,0},{20,4},{24,8},{28,12},{1,17},{... | collective-permute-start | bytes 49160 | tf_op jit(solution)/shard_map/ppermute | solution.py:249
  7.9 5.3 %collective-permute-start.7 = (bf16[8,1024]{1,0:T(8,128)(2,1)}, bf16[8,1024]{1,0:T(8,128)(2,1)S(1)}, u32[]{:S(2)}, u32[]{:S(2)}) collective-permute-start(bf16[8,1024]{1,0:T(8,128)(2,1)} %x_hbm.1), channel_id=1, source_target_pairs={{0,24},{4,28},{8,0},{12,4},{16,8},{20,12},{24,16},{28,20},{1,25},{... | collective-permute-start | bytes 49160 | tf_op jit(solution)/shard_map/ppermute | solution.py:249
  11.5 1.9 %collective-permute-start.2 = (f32[8,4096]{1,0:T(8,128)S(1)}, f32[8,4096]{1,0:T(8,128)S(1)}, u32[]{:S(2)}, u32[]{:S(2)}) collective-permute-start(f32[8,4096]{1,0:T(8,128)S(1)} %get-tuple-element.20), channel_id=1, source_target_pairs={{0,4},{4,0},{8,12},{12,8},{16,20},{20,16},{24,28},{28,24},{1,5},{5... | collective-permute-start | bytes 393224 | tf_op jit(solution)/shard_map/ppermute | solution.py:246
  11.6 6.0 %collective-permute-start.9 = (bf16[8,8192]{1,0:T(8,128)(2,1)S(1)}, bf16[8,8192]{1,0:T(8,128)(2,1)S(1)}, u32[]{:S(2)}, u32[]{:S(2)}) collective-permute-start(bf16[8,8192]{1,0:T(8,128)(2,1)S(1)} %get-tuple-element.27.refs_5_), channel_id=1, source_target_pairs={{0,1},{1,0},{2,3},{3,2},{4,5},{5,4},{6,7},{7,6},{8,9},{9,8},{10,11... | collective-permute-start | bytes 393224 | tf_op jit(solution)/shard_map/ppermute | solution.py:255
  13.3 2.4 %collective-permute-start.8 = (bf16[8,4096]{1,0:T(8,128)(2,1)S(1)}, bf16[8,4096]{1,0:T(8,128)(2,1)S(1)}, u32[]{:S(2)}, u32[]{:S(2)}) collective-permute-start(bf16[8,4096]{1,0:T(8,128)(2,1)S(1)} %constant_dynamic-update-slice_fusion.near), channel_id=1, source_target_pairs={{0,4},{4,0},{8,12},{12,8},{16,20},{20,16},{24,28},{28,24},{1,5},{5... | collective-permute-start | bytes 196616 | tf_op jit(solution)/shard_map/ppermute | solution.py:246
  13.5 6.9 %collective-permute-start.4 = (f32[8,2048]{1,0:T(8,128)S(1)}, f32[8,2048]{1,0:T(8,128)S(1)}, u32[]{:S(2)}, u32[]{:S(2)}) collective-permute-start(f32[8,2048]{1,0:T(8,128)S(1)} %get-tuple-element.23), channel_id=1, source_target_pairs={{0,16},{4,28},{8,24},{12,4},{16,0},{20,12},{24,8},{28,20},{1,17},{... | collective-permute-start | bytes 196616 | tf_op jit(solution)/shard_map/ppermute | solution.py:305
  14.6 5.8 %collective-permute-start.3 = (f32[8,1024]{1,0:T(8,128)S(1)}, f32[8,1024]{1,0:T(8,128)S(1)}, u32[]{:S(2)}, u32[]{:S(2)}) collective-permute-start(f32[8,1024]{1,0:T(8,128)S(1)} %get-tuple-element.22), channel_id=1, source_target_pairs={{0,8},{4,12},{8,16},{12,20},{16,24},{20,28},{24,0},{28,4},{1,9},{5... | collective-permute-start | bytes 98312 | tf_op jit(solution)/shard_map/ppermute | solution.py:249
  20.8 1.2 %collective-permute-start.10 = (f32[8,1152]{1,0:T(8,128)S(1)}, f32[8,1152]{1,0:T(8,128)S(1)}, u32[]{:S(2)}, u32[]{:S(2)}) collective-permute-start(f32[8,1152]{1,0:T(8,128)S(1)} %get-tuple-element.29), channel_id=1, source_target_pairs={{0,4},{4,0},{8,12},{12,8},{16,20},{20,16},{24,28},{28,24},{1,5},{5... | collective-permute-start | bytes 110600 | tf_op jit(solution)/shard_map/ppermute | solution.py:246
  20.8 5.6 %collective-permute-start.11 = (f32[8,1152]{1,0:T(8,128)S(1)}, f32[8,1152]{1,0:T(8,128)S(1)}, u32[]{:S(2)}, u32[]{:S(2)}) collective-permute-start(f32[8,1152]{1,0:T(8,128)S(1)} %get-tuple-element.30), channel_id=1, source_target_pairs={{0,2},{2,0},{1,3},{3,1},{4,6},{6,4},{5,7},{7,5},{8,10},{10,8},{9,1... | collective-permute-start | bytes 110600 | tf_op jit(solution)/shard_map/ppermute | solution.py:252
  22.0 5.4 %collective-permute-start.14 = (f32[8,16]{1,0:T(8,128)S(1)}, f32[8,16]{1,0:T(8,128)S(1)}, u32[]{:S(2)}, u32[]{:S(2)}) collective-permute-start(f32[8,16]{1,0:T(8,128)S(1)} %slice_add_fusion.3), channel_id=1, source_target_pairs={{0,24},{2,26},{4,30},{6,28},{8,16},{10,18},{12,22},{14,20},{16,8},... | collective-permute-start | bytes 1544 | tf_op jit(solution)/shard_map/ppermute | solution.py:351
  23.6 4.5 %collective-permute-start.13 = (f32[8,16]{1,0:T(8,128)S(1)}, f32[8,16]{1,0:T(8,128)S(1)}, u32[]{:S(2)}, u32[]{:S(2)}) collective-permute-start(f32[8,16]{1,0:T(8,128)S(1)} %slice_add_fusion.3), channel_id=1, source_target_pairs={{0,16},{2,18},{4,22},{6,20},{8,24},{10,26},{12,30},{14,28},{16,0},... | collective-permute-start | bytes 1544 | tf_op jit(solution)/shard_map/ppermute | solution.py:351
  23.6 4.5 %collective-permute-start.12 = (f32[8,16]{1,0:T(8,128)S(1)}, f32[8,16]{1,0:T(8,128)S(1)}, u32[]{:S(2)}, u32[]{:S(2)}) collective-permute-start(f32[8,16]{1,0:T(8,128)S(1)} %slice_add_fusion.3), channel_id=1, source_target_pairs={{0,8},{2,10},{4,14},{6,12},{8,0},{10,2},{12,6},{14,4},{16,24},{18,... | collective-permute-start | bytes 1544 | tf_op jit(solution)/shard_map/ppermute | solution.py:351
  28.1 1.2 %collective-permute-start.15 = (f32[8,16]{1,0:T(8,128)S(1)}, f32[8,16]{1,0:T(8,128)S(1)}, u32[]{:S(2)}, u32[]{:S(2)}) collective-permute-start(f32[8,16]{1,0:T(8,128)S(1)} %fusion.2), channel_id=1, source_target_pairs={{0,4},{4,0},{8,12},{12,8},{16,20},{20,16},{24,28},{28,24},{1,5},{5... | collective-permute-start | bytes 1544 | tf_op jit(solution)/shard_map/ppermute | solution.py:354

commit v9 on v8

--- a/solution.py
+++ b/solution.py
@@ -93,25 +93,23 @@
     token[...] = jnp.zeros_like(token)
 
 
-def mirror_kernel(sizes, counts, rows, cols, tiles, x_hbm, token, sibling, *refs):
+def mirror_kernel(sizes, counts, rows, cols, tiles, x, token, sibling, *refs):
     nz, ncol, stretch = sizes
     span = ncol * stretch
-    blocks, (mine, other, x, wide), refs = refs[: ncol - 1], refs[ncol - 1 : ncol + 3], refs[ncol + 3 :]
-    vector, scalar, sems, low, high, *sums = refs
+    blocks, (mine, other, own, wide), refs = refs[: ncol - 1], refs[ncol - 1 : ncol + 3], refs[ncol + 3 :]
+    vector, scalar, sem, low, high, *sums = refs
     tile = tiles.shape[-1]
     width = stretch * tile
     count = counts[0, 0]
-    own = pltpu.make_async_copy(x_hbm, x, sems.at[0])
-    own.start()
     slot = lax.broadcasted_iota(jnp.int32, rows.shape, 1)
     row_place, col_place = places(rows, cols, span, stretch)
     used = jnp.where((slot < count) & (rows[...] != cols[...]), row_place, span)
-    indices = hand_scalars((vector, scalar), sems.at[1], used, col_place)
+    indices = hand_scalars((vector, scalar), sem, used, col_place)
     z, core, j = position()
     for t in range(1, ncol):
         wide[:, t * width : (t + 1) * width] = blocks[t - 1][...]
         place_block(low, high, blocks[t - 1], lax.rem(j + ncol - t, ncol) * stretch, stretch, tile)
-    own.wait()
+    own[...] = x[...]
     wide[:, :width] = x[...]
     wide[:, ncol * width : (ncol + 1) * width] = sibling[...]
     wide[:, (ncol + 1) * width :] = jnp.zeros_like(wide[:, (ncol + 1) * width :])
@@ -226,10 +224,7 @@
     slots, tile = tile_vals.shape[2], tile_vals.shape[-1]
     stretch = width // tile
     span = ncol * stretch
-    x_hbm, tiles_hbm = (
-        pltpu.with_memory_space_constraint(a, pltpu.HBM)
-        for a in (vectors, tile_vals[0, 0])
-    )
+    tiles_hbm = pltpu.with_memory_space_constraint(tile_vals[0, 0], pltpu.HBM)
     tiles, rows, cols = tile_vals[0, 0], tile_rows[0], tile_cols[0]
     token = pl.pallas_call(
         stage_kernel,
@@ -275,16 +270,16 @@
     mine, other, x, wide = pl.pallas_call(
         functools.partial(mirror_kernel, step),
         out_shape=[ring, ring, jax.ShapeDtypeStruct(vectors.shape, vectors.dtype), jax.ShapeDtypeStruct((vlocal, LONGER * ncol * width), vectors.dtype)],
-        in_specs=[SMEM] + [VMEM] * 3 + [HBM] + [VMEM] * (1 + ncol),
+        in_specs=[SMEM] + [VMEM] * 3 + [VMEM] * (2 + ncol),
         out_specs=[VMEM] * 4,
         scratch_shapes=lists
-        + [pltpu.SemaphoreType.DMA((2,))]
+        + [pltpu.SemaphoreType.DMA]
         + tables(span)
         + sums(nrow * stretch),
         compiler_params=params(6),
         cost_estimate=cost,
         name="mirror",
-    )(tile_counts, rows, cols, tiles, x_hbm, token, sibling, *row_x[1:])
+    )(tile_counts, rows, cols, tiles, vectors, token, sibling, *row_x[1:])
     near = jnp.concatenate([x] + ring_x, axis=1)
     far = core_swap(near)
     theirs = core_swap(other)

time: 30.2 us -> 30.4 us (level)
  local copies, waits for them, and re-layouts: 0.03 us -> 0.74 us
  starting transfers between devices: 17.7 us -> 17.2 us
    unnamed x9 -> x11, local copies, waits for them, and re-layouts: 0.02 us -> 0.73 us
    ppermute x4, starting transfers between devices: 6.57 us -> 6.2 us  [z_shift(): lax.ppermute(x, 'row', [(a, (a + 2 * s) % nrow) for a in range(nrow)])]
  transfers between devices with their start and end apart: 16 -> 16, of which waited for: 5 -> 7; matrix products, arithmetic and copies ran while one was open for 2% -> 2% of each run, Pallas kernels for 12% -> 11%
where the time goes in v9:
time: 30.4 us; the launch traced here: 30.2 us
  starting transfers between devices  17.2 us (57%)
  waiting for transfers between devices  5.89 us (19%)
  Pallas kernels  3.69 us (12%)
  between operations  1.44 us (5%)
  other arithmetic  1.22 us (4%)
  local copies, waits for them, and re-layouts  0.74 us (2%)
    ppermute x4, starting transfers between devices, z_shift(): lax.ppermute(x, 'row', [(a, (a + 2 * s) % nrow) for a in range(nrow)])  6.2 us
    ppermute x3, starting transfers between devices, send(): return lax.ppermute(x, ('row', 'col'), perm)  4.39 us
    ppermute x2, starting transfers between devices, col_shift(): return lax.ppermute(x, 'col', [(a, (a + t) % ncol) for a in range(ncol)])  3.12 us
    ppermute x4, waiting for transfers between devices, z_shift(): lax.ppermute(x, 'row', [(a, (a + 2 * s) % nrow) for a in range(nrow)])  2.79 us
    pallas_call x1, Pallas kernels, shards(): pl.pallas_call(functools.partial(forward_kernel, step), out_shape=[block]...  1.94 us
    ppermute x1, starting transfers between devices, vec_shift(): return lax.ppermute(x, 'vec', [(a, (a + t) % nvec) for a in range(nvec)])  1.58 us
    ppermute x3, waiting for transfers between devices, send(): return lax.ppermute(x, ('row', 'col'), perm)  1.58 us
    pallas_call x1, Pallas kernels, shards(): pl.pallas_call(functools.partial(mirror_kernel, step), out_shape=[ring, r...  1.39 us
  transfers between devices with their start and end apart: 16, of which 7 were waited for; matrix products, arithmetic and copies ran while one was open for 2% of the time, Pallas kernels for 11%

profile of v9, /device:TPU:0, one launch (start us, length us, event | category | flops | bytes accessed | tf_op | source)
XLA Modules:
  0.0 30.2 jit_solution(9690861520162994629)
XLA Ops:
  0.7 0.5 %collective-permute-start = (bf16[8,1024]{1,0:T(8,128)(2,1)}, bf16[8,1024]{1,0:T(8,128)(2,1)S(1)}, u32[]{:S(2)}, u32[]{:S(2)}) collective-permute-start(bf16[8,1024]{1,0:T(8,128)(2,1)} %x), channel_id=1, source_target_pairs={{0,4},{4,0},{8,12},{12,8},{16,20},{20,16},{24,28},{28,24},{1,5},{5... | collective-permute-start | bytes 49160 | tf_op jit(solution)/shard_map/ppermute | solution.py:241
  1.2 2.6 %collective-permute-start.1 = (bf16[8,1024]{1,0:T(8,128)(2,1)}, bf16[8,1024]{1,0:T(8,128)(2,1)S(1)}, u32[]{:S(2)}, u32[]{:S(2)}) collective-permute-start(bf16[8,1024]{1,0:T(8,128)(2,1)} %x), channel_id=1, source_target_pairs={{0,2},{2,0},{1,3},{3,1},{4,6},{6,4},{5,7},{7,5},{8,10},{10,8},{9,1... | collective-permute-start | bytes 49160 | tf_op jit(solution)/shard_map/ppermute | solution.py:247
  3.8 1.6 %collective-permute-start.5 = (bf16[8,1024]{1,0:T(8,128)(2,1)}, bf16[8,1024]{1,0:T(8,128)(2,1)S(1)}, u32[]{:S(2)}, u32[]{:S(2)}) collective-permute-start(bf16[8,1024]{1,0:T(8,128)(2,1)} %x), channel_id=1, source_target_pairs={{0,8},{4,12},{8,16},{12,20},{16,24},{20,28},{24,0},{28,4},{1,9},{5... | collective-permute-start | bytes 49160 | tf_op jit(solution)/shard_map/ppermute | solution.py:244
  5.3 2.6 %collective-permute-start.6 = (bf16[8,1024]{1,0:T(8,128)(2,1)}, bf16[8,1024]{1,0:T(8,128)(2,1)S(1)}, u32[]{:S(2)}, u32[]{:S(2)}) collective-permute-start(bf16[8,1024]{1,0:T(8,128)(2,1)} %x), channel_id=1, source_target_pairs={{0,16},{4,20},{8,24},{12,28},{16,0},{20,4},{24,8},{28,12},{1,17},{... | collective-permute-start | bytes 49160 | tf_op jit(solution)/shard_map/ppermute | solution.py:244
  7.9 1.3 %collective-permute-start.7 = (bf16[8,1024]{1,0:T(8,128)(2,1)}, bf16[8,1024]{1,0:T(8,128)(2,1)S(1)}, u32[]{:S(2)}, u32[]{:S(2)}) collective-permute-start(bf16[8,1024]{1,0:T(8,128)(2,1)} %x), channel_id=1, source_target_pairs={{0,24},{4,28},{8,0},{12,4},{16,8},{20,12},{24,16},{28,20},{1,25},{... | collective-permute-start | bytes 49160 | tf_op jit(solution)/shard_map/ppermute | solution.py:244
  9.9 0.0 collective-permute-done.1.refs_0_
  10.0 0.7 %copy-done.1 = bf16[8,1024]{1,0:T(8,128)(2,1)S(1)} copy-done((bf16[8,1024]{1,0:T(8,128)(2,1)S(1)}, bf16[8,1024]{1,0:T(8,128)(2,1)}, u32[]{:S(2)}) %copy-start.1) | copy-done | bytes 16408
  10.7 1.4 %mirror.1 = (f32[8,4096]{1,0:T(8,128)S(1)}, f32[8,4096]{1,0:T(8,128)S(1)}, bf16[8,1024]{1,0:T(8,128)(2,1)S(1)}, bf16[8,8192]{1,0:T(8,128)(2,1)S(1)}) custom-call(s32[1,1]{1,0:T(1,128)S(6)} %copy.10.counts, s32[1,256]{1,0:T(1,128)S(1)} %bitcast.8, s32[1,256]{1,0:T(1,128)S(1)} %bitcast.10, bf16[256,128,128]{2,1,0:T(8,128)(2,1)S(1)} %bitcast.6, ...), custom_call_target="tpu_custom_call" | custom-call | flops 134217728 | bytes 8388608 | tf_op jit(solution)/shard_map/mirror/pallas_call | solution.py:270
  12.1 0.1 collective-permute-start.2
  12.2 1.6 %collective-permute-start.9 = (bf16[8,8192]{1,0:T(8,128)(2,1)S(1)}, bf16[8,8192]{1,0:T(8,128)(2,1)S(1)}, u32[]{:S(2)}, u32[]{:S(2)}) collective-permute-start(bf16[8,8192]{1,0:T(8,128)(2,1)S(1)} %get-tuple-element.27.refs_5_), channel_id=1, source_target_pairs={{0,1},{1,0},{2,3},{3,2},{4,5},{5,4},{6,7},{7,6},{8,9},{9,8},{10,11... | collective-permute-start | bytes 393224 | tf_op jit(solution)/shard_map/ppermute | solution.py:250
  13.8 0.0 collective-permute-done.5
  13.8 0.0 collective-permute-done.7
  13.8 0.2 collective-permute-start.8
  14.0 0.0 collective-permute-done.2.theirs
  14.1 1.1 %collective-permute-start.4 = (f32[8,2048]{1,0:T(8,128)S(1)}, f32[8,2048]{1,0:T(8,128)S(1)}, u32[]{:S(2)}, u32[]{:S(2)}) collective-permute-start(f32[8,2048]{1,0:T(8,128)S(1)} %get-tuple-element.23), channel_id=1, source_target_pairs={{0,16},{4,28},{8,24},{12,4},{16,0},{20,12},{24,8},{28,20},{1,17},{... | collective-permute-start | bytes 196616 | tf_op jit(solution)/shard_map/ppermute | solution.py:300
  15.2 0.7 %collective-permute-start.3 = (f32[8,1024]{1,0:T(8,128)S(1)}, f32[8,1024]{1,0:T(8,128)S(1)}, u32[]{:S(2)}, u32[]{:S(2)}) collective-permute-start(f32[8,1024]{1,0:T(8,128)S(1)} %get-tuple-element.22), channel_id=1, source_target_pairs={{0,8},{4,12},{8,16},{12,20},{16,24},{20,28},{24,0},{28,4},{1,9},{5... | collective-permute-start | bytes 98312 | tf_op jit(solution)/shard_map/ppermute | solution.py:244
  15.8 0.0 collective-permute-done.8.far
  15.8 1.9 %forward.1 = (f32[8,1024]{1,0:T(8,128)S(1)}, f32[8,1024]{1,0:T(8,128)S(1)}) custom-call(s32[1,1]{1,0:T(1,128)S(6)} %copy.10.counts, s32[1,256]{1,0:T(1,128)S(1)} %bitcast.9, s32[1,256]{1,0:T(1,128)S(1)} %bitcast.11, bf16[256,128,128]{2,1,0:T(8,128)(2,1)S(1)} %bitcast.7, bf16[8,4096]{1,0:T(8,128)(2,1)S(1)} %constant_dynamic-update-slice_fusion.near, ...), custom_call_target="tpu_custom_call" | custom-call | flops 134217728 | bytes 8388608 | tf_op jit(solution)/shard_map/forward/pallas_call | solution.py:302
  17.8 0.3 collective-permute-done.9.refs_6_
  18.1 2.8 %collective-permute-done.3.refs_1_ = f32[8,1024]{1,0:T(8,128)S(1)} collective-permute-done((f32[8,1024]{1,0:T(8,128)S(1)}, f32[8,1024]{1,0:T(8,128)S(1)}, u32[]{:S(2)}, u32[]{:S(2)}) %collective-permute-start.3) | collective-permute-done | bytes 32800 | tf_op jit(solution)/shard_map/ppermute | solution.py:244
  20.9 0.3 %gram.1 = (f32[8,1024]{1,0:T(8,128)S(1)}, f32[8,16]{1,0:T(8,128)S(1)}, f32[8,1152]{1,0:T(8,128)S(1)}, f32[8,1152]{1,0:T(8,128)S(1)}) custom-call(f32[8,1024]{1,0:T(8,128)S(1)} %get-tuple-element.21.refs_0_, f32[8,1024]{1,0:T(8,128)S(1)} %collective-permute-done.3.refs_1_, f32[8,2048]{1,0:T(8,128)S(1)} %collective-permute-done.4.refs_2_, ...), custom_call_target="tpu_custom_call" | custom-call | tf_op jit(solution)/shard_map/gram/pallas_call | solution.py:315
  21.2 0.6 %collective-permute-start.11 = (f32[8,1152]{1,0:T(8,128)S(1)}, f32[8,1152]{1,0:T(8,128)S(1)}, u32[]{:S(2)}, u32[]{:S(2)}) collective-permute-start(f32[8,1152]{1,0:T(8,128)S(1)} %get-tuple-element.30), channel_id=1, source_target_pairs={{0,2},{2,0},{1,3},{3,1},{4,6},{6,4},{5,7},{7,5},{8,10},{10,8},{9,1... | collective-permute-start | bytes 110600 | tf_op jit(solution)/shard_map/ppermute | solution.py:247
  21.8 0.7 %collective-permute-done.10 = f32[8,1152]{1,0:T(8,128)S(1)} collective-permute-done((f32[8,1152]{1,0:T(8,128)S(1)}, f32[8,1152]{1,0:T(8,128)S(1)}, u32[]{:S(2)}, u32[]{:S(2)}) %collective-permute-start.10) | collective-permute-done | bytes 36896 | tf_op jit(solution)/shard_map/ppermute | solution.py:241
  22.4 1.3 %collective-permute-start.14 = (f32[8,16]{1,0:T(8,128)S(1)}, f32[8,16]{1,0:T(8,128)S(1)}, u32[]{:S(2)}, u32[]{:S(2)}) collective-permute-start(f32[8,16]{1,0:T(8,128)S(1)} %slice_add_fusion.3), channel_id=1, source_target_pairs={{0,24},{2,26},{4,30},{6,28},{8,16},{10,18},{12,22},{14,20},{16,8},... | collective-permute-start | bytes 1544 | tf_op jit(solution)/shard_map/ppermute | solution.py:346
  23.8 0.3 collective-permute-start.13
  24.0 2.8 %collective-permute-start.12 = (f32[8,16]{1,0:T(8,128)S(1)}, f32[8,16]{1,0:T(8,128)S(1)}, u32[]{:S(2)}, u32[]{:S(2)}) collective-permute-start(f32[8,16]{1,0:T(8,128)S(1)} %slice_add_fusion.3), channel_id=1, source_target_pairs={{0,8},{2,10},{4,14},{6,12},{8,0},{10,2},{12,6},{14,4},{16,24},{18,... | collective-permute-start | bytes 1544 | tf_op jit(solution)/shard_map/ppermute | solution.py:346
  26.8 1.0 %collective-permute-done.14 = f32[8,16]{1,0:T(8,128)S(1)} collective-permute-done((f32[8,16]{1,0:T(8,128)S(1)}, f32[8,16]{1,0:T(8,128)S(1)}, u32[]{:S(2)}, u32[]{:S(2)}) %collective-permute-start.14) | collective-permute-done | bytes 544 | tf_op jit(solution)/shard_map/ppermute | solution.py:346
  27.8 0.4 %collective-permute-done.13 = f32[8,16]{1,0:T(8,128)S(1)} collective-permute-done((f32[8,16]{1,0:T(8,128)S(1)}, f32[8,16]{1,0:T(8,128)S(1)}, u32[]{:S(2)}, u32[]{:S(2)}) %collective-permute-start.13) | collective-permute-done | bytes 544 | tf_op jit(solution)/shard_map/ppermute | solution.py:346
  28.3 0.1 collective-permute-done.12
  28.4 0.6 %fusion = bf16[8,1024]{1,0:T(8,128)(2,1)} fusion(f32[8,1152]{1,0:T(8,128)S(1)} %collective-permute-done.11, f32[8,1024]{1,0:T(8,128)S(1)} %get-tuple-element.28, f32[8,1152]{1,0:T(8,128)S(1)} %collective-permute-done.10), kind=kLoop, calls=%fused_computation.1 | loop fusion | flops 24576 | bytes 114688 | tf_op jit(solution)/shard_map/convert_element_type | solution.py:333
  29.0 0.5 %collective-permute-done.15 = f32[8,16]{1,0:T(8,128)S(1)} collective-permute-done((f32[8,16]{1,0:T(8,128)S(1)}, f32[8,16]{1,0:T(8,128)S(1)}, u32[]{:S(2)}, u32[]{:S(2)}) %collective-permute-start.15) | collective-permute-done | bytes 544 | tf_op jit(solution)/shard_map/ppermute | solution.py:349
  29.6 0.6 %add_bitcast_fusion = f32[16,8]{0,1:T(8,128)} fusion(f32[8,16]{1,0:T(8,128)S(1)} %collective-permute-done.15, f32[8,16]{1,0:T(8,128)S(1)} %slice_add_fusion.3, f32[8,16]{1,0:T(8,128)S(1)} %fusion.2), kind=kLoop, calls=%fused_computation.11 | loop fusion | flops 256 | bytes 2048 | tf_op jit(solution)/shard_map/transpose | solution.py:332
  (21 shorter events, 0.1 us)
Async XLA Ops:
  0.6 9.3 %copy-start = (bf16[1,1,256,128,128]{4,3,2,1,0:T(8,128)(2,1)S(1)}, bf16[1,1,256,128,128]{4,3,2,1,0:T(8,128)(2,1)}, u32[]{:S(2)}) copy-start(bf16[1,1,256,128,128]{4,3,2,1,0:T(8,128)(2,1)} %param.6) | copy-start | bytes 25165828
  0.6 9.3 %copy-start.2 = (s32[1,1,256]{2,1,0:T(1,128)S(1)}, s32[1,1,256]{2,1,0:T(1,128)}, u32[]{:S(2)}) copy-start(s32[1,1,256]{2,1,0:T(1,128)} %param.7) | copy-start | bytes 3076
  0.7 9.3 %copy-start.3 = (s32[1,1,256]{2,1,0:T(1,128)S(1)}, s32[1,1,256]{2,1,0:T(1,128)}, u32[]{:S(2)}) copy-start(s32[1,1,256]{2,1,0:T(1,128)} %param.8) | copy-start | bytes 3076
  0.7 9.3 %collective-permute-start = (bf16[8,1024]{1,0:T(8,128)(2,1)}, bf16[8,1024]{1,0:T(8,128)(2,1)S(1)}, u32[]{:S(2)}, u32[]{:S(2)}) collective-permute-start(bf16[8,1024]{1,0:T(8,128)(2,1)} %x), channel_id=1, source_target_pairs={{0,4},{4,0},{8,12},{12,8},{16,20},{20,16},{24,28},{28,24},{1,5},{5... | collective-permute-start | bytes 49160 | tf_op jit(solution)/shard_map/ppermute | solution.py:241
  1.2 8.7 %collective-permute-start.1 = (bf16[8,1024]{1,0:T(8,128)(2,1)}, bf16[8,1024]{1,0:T(8,128)(2,1)S(1)}, u32[]{:S(2)}, u32[]{:S(2)}) collective-permute-start(bf16[8,1024]{1,0:T(8,128)(2,1)} %x), channel_id=1, source_target_pairs={{0,2},{2,0},{1,3},{3,1},{4,6},{6,4},{5,7},{7,5},{8,10},{10,8},{9,1... | collective-permute-start | bytes 49160 | tf_op jit(solution)/shard_map/ppermute | solution.py:247
  3.8 10.0 %collective-permute-start.5 = (bf16[8,1024]{1,0:T(8,128)(2,1)}, bf16[8,1024]{1,0:T(8,128)(2,1)S(1)}, u32[]{:S(2)}, u32[]{:S(2)}) collective-permute-start(bf16[8,1024]{1,0:T(8,128)(2,1)} %x), channel_id=1, source_target_pairs={{0,8},{4,12},{8,16},{12,20},{16,24},{20,28},{24,0},{28,4},{1,9},{5... | collective-permute-start | bytes 49160 | tf_op jit(solution)/shard_map/ppermute | solution.py:244
  5.3 8.4 %collective-permute-start.6 = (bf16[8,1024]{1,0:T(8,128)(2,1)}, bf16[8,1024]{1,0:T(8,128)(2,1)S(1)}, u32[]{:S(2)}, u32[]{:S(2)}) collective-permute-start(bf16[8,1024]{1,0:T(8,128)(2,1)} %x), channel_id=1, source_target_pairs={{0,16},{4,20},{8,24},{12,28},{16,0},{20,4},{24,8},{28,12},{1,17},{... | collective-permute-start | bytes 49160 | tf_op jit(solution)/shard_map/ppermute | solution.py:244
  7.9 5.9 %collective-permute-start.7 = (bf16[8,1024]{1,0:T(8,128)(2,1)}, bf16[8,1024]{1,0:T(8,128)(2,1)S(1)}, u32[]{:S(2)}, u32[]{:S(2)}) collective-permute-start(bf16[8,1024]{1,0:T(8,128)(2,1)} %x), channel_id=1, source_target_pairs={{0,24},{4,28},{8,0},{12,4},{16,8},{20,12},{24,16},{28,20},{1,25},{... | collective-permute-start | bytes 49160 | tf_op jit(solution)/shard_map/ppermute | solution.py:244
  10.0 0.7 %copy-start.1 = (bf16[8,1024]{1,0:T(8,128)(2,1)S(1)}, bf16[8,1024]{1,0:T(8,128)(2,1)}, u32[]{:S(2)}) copy-start(bf16[8,1024]{1,0:T(8,128)(2,1)} %x) | copy-start | bytes 49156
  12.1 1.9 %collective-permute-start.2 = (f32[8,4096]{1,0:T(8,128)S(1)}, f32[8,4096]{1,0:T(8,128)S(1)}, u32[]{:S(2)}, u32[]{:S(2)}) collective-permute-start(f32[8,4096]{1,0:T(8,128)S(1)} %get-tuple-element.20), channel_id=1, source_target_pairs={{0,4},{4,0},{8,12},{12,8},{16,20},{20,16},{24,28},{28,24},{1,5},{5... | collective-permute-start | bytes 393224 | tf_op jit(solution)/shard_map/ppermute | solution.py:241
  12.2 5.9 %collective-permute-start.9 = (bf16[8,8192]{1,0:T(8,128)(2,1)S(1)}, bf16[8,8192]{1,0:T(8,128)(2,1)S(1)}, u32[]{:S(2)}, u32[]{:S(2)}) collective-permute-start(bf16[8,8192]{1,0:T(8,128)(2,1)S(1)} %get-tuple-element.27.refs_5_), channel_id=1, source_target_pairs={{0,1},{1,0},{2,3},{3,2},{4,5},{5,4},{6,7},{7,6},{8,9},{9,8},{10,11... | collective-permute-start | bytes 393224 | tf_op jit(solution)/shard_map/ppermute | solution.py:250
  13.8 2.0 %collective-permute-start.8 = (bf16[8,4096]{1,0:T(8,128)(2,1)S(1)}, bf16[8,4096]{1,0:T(8,128)(2,1)S(1)}, u32[]{:S(2)}, u32[]{:S(2)}) collective-permute-start(bf16[8,4096]{1,0:T(8,128)(2,1)S(1)} %constant_dynamic-update-slice_fusion.near), channel_id=1, source_target_pairs={{0,4},{4,0},{8,12},{12,8},{16,20},{20,16},{24,28},{28,24},{1,5},{5... | collective-permute-start | bytes 196616 | tf_op jit(solution)/shard_map/ppermute | solution.py:241
  14.1 6.8 %collective-permute-start.4 = (f32[8,2048]{1,0:T(8,128)S(1)}, f32[8,2048]{1,0:T(8,128)S(1)}, u32[]{:S(2)}, u32[]{:S(2)}) collective-permute-start(f32[8,2048]{1,0:T(8,128)S(1)} %get-tuple-element.23), channel_id=1, source_target_pairs={{0,16},{4,28},{8,24},{12,4},{16,0},{20,12},{24,8},{28,20},{1,17},{... | collective-permute-start | bytes 196616 | tf_op jit(solution)/shard_map/ppermute | solution.py:300
  15.2 5.7 %collective-permute-start.3 = (f32[8,1024]{1,0:T(8,128)S(1)}, f32[8,1024]{1,0:T(8,128)S(1)}, u32[]{:S(2)}, u32[]{:S(2)}) collective-permute-start(f32[8,1024]{1,0:T(8,128)S(1)} %get-tuple-element.22), channel_id=1, source_target_pairs={{0,8},{4,12},{8,16},{12,20},{16,24},{20,28},{24,0},{28,4},{1,9},{5... | collective-permute-start | bytes 98312 | tf_op jit(solution)/shard_map/ppermute | solution.py:244
  21.2 1.2 %collective-permute-start.10 = (f32[8,1152]{1,0:T(8,128)S(1)}, f32[8,1152]{1,0:T(8,128)S(1)}, u32[]{:S(2)}, u32[]{:S(2)}) collective-permute-start(f32[8,1152]{1,0:T(8,128)S(1)} %get-tuple-element.29), channel_id=1, source_target_pairs={{0,4},{4,0},{8,12},{12,8},{16,20},{20,16},{24,28},{28,24},{1,5},{5... | collective-permute-start | bytes 110600 | tf_op jit(solution)/shard_map/ppermute | solution.py:241
  21.2 5.6 %collective-permute-start.11 = (f32[8,1152]{1,0:T(8,128)S(1)}, f32[8,1152]{1,0:T(8,128)S(1)}, u32[]{:S(2)}, u32[]{:S(2)}) collective-permute-start(f32[8,1152]{1,0:T(8,128)S(1)} %get-tuple-element.30), channel_id=1, source_target_pairs={{0,2},{2,0},{1,3},{3,1},{4,6},{6,4},{5,7},{7,5},{8,10},{10,8},{9,1... | collective-permute-start | bytes 110600 | tf_op jit(solution)/shard_map/ppermute | solution.py:247
  22.4 5.4 %collective-permute-start.14 = (f32[8,16]{1,0:T(8,128)S(1)}, f32[8,16]{1,0:T(8,128)S(1)}, u32[]{:S(2)}, u32[]{:S(2)}) collective-permute-start(f32[8,16]{1,0:T(8,128)S(1)} %slice_add_fusion.3), channel_id=1, source_target_pairs={{0,24},{2,26},{4,30},{6,28},{8,16},{10,18},{12,22},{14,20},{16,8},... | collective-permute-start | bytes 1544 | tf_op jit(solution)/shard_map/ppermute | solution.py:346
  23.8 4.5 %collective-permute-start.13 = (f32[8,16]{1,0:T(8,128)S(1)}, f32[8,16]{1,0:T(8,128)S(1)}, u32[]{:S(2)}, u32[]{:S(2)}) collective-permute-start(f32[8,16]{1,0:T(8,128)S(1)} %slice_add_fusion.3), channel_id=1, source_target_pairs={{0,16},{2,18},{4,22},{6,20},{8,24},{10,26},{12,30},{14,28},{16,0},... | collective-permute-start | bytes 1544 | tf_op jit(solution)/shard_map/ppermute | solution.py:346
  24.0 4.4 %collective-permute-start.12 = (f32[8,16]{1,0:T(8,128)S(1)}, f32[8,16]{1,0:T(8,128)S(1)}, u32[]{:S(2)}, u32[]{:S(2)}) collective-permute-start(f32[8,16]{1,0:T(8,128)S(1)} %slice_add_fusion.3), channel_id=1, source_target_pairs={{0,8},{2,10},{4,14},{6,12},{8,0},{10,2},{12,6},{14,4},{16,24},{18,... | collective-permute-start | bytes 1544 | tf_op jit(solution)/shard_map/ppermute | solution.py:346
  28.4 1.2 %collective-permute-start.15 = (f32[8,16]{1,0:T(8,128)S(1)}, f32[8,16]{1,0:T(8,128)S(1)}, u32[]{:S(2)}, u32[]{:S(2)}) collective-permute-start(f32[8,16]{1,0:T(8,128)S(1)} %fusion.2), channel_id=1, source_target_pairs={{0,4},{4,0},{8,12},{12,8},{16,20},{20,16},{24,28},{28,24},{1,5},{5... | collective-permute-start | bytes 1544 | tf_op jit(solution)/shard_map/ppermute | solution.py:349

commit v10 on v9

--- a/solution.py
+++ b/solution.py
@@ -348,7 +348,7 @@
     def swap(x):
         return lax.ppermute(x, "row", [(a, a ^ 1) for a in range(nrow)])
 
-    for s in range(1, nz):
+    for s in [*range(min(2, nz - 1), 0, -1), *range(3, nz)]:
         for t in range(0, ncol, 2):
             got = got + send(share, s, t)
     return share + got + swap(got)

time: 30.4 us -> 30.4 us (level)
  transfers between devices with their start and end apart: 16 -> 16, of which waited for: 7 -> 6; matrix products, arithmetic and copies ran while one was open for 2% -> 2% of each run, Pallas kernels for 11% -> 11%
where the time goes in v10:
time: 30.4 us; the launch traced here: 30.2 us
  starting transfers between devices  17.3 us (57%)
  waiting for transfers between devices  5.76 us (19%)
  Pallas kernels  3.68 us (12%)
  between operations  1.44 us (5%)
  other arithmetic  1.22 us (4%)
  local copies, waits for them, and re-layouts  0.74 us (2%)
    ppermute x4, starting transfers between devices, z_shift(): lax.ppermute(x, 'row', [(a, (a + 2 * s) % nrow) for a in range(nrow)])  6.21 us
    ppermute x3, starting transfers between devices, send(): return lax.ppermute(x, ('row', 'col'), perm)  4.39 us
    ppermute x2, starting transfers between devices, col_shift(): return lax.ppermute(x, 'col', [(a, (a + t) % ncol) for a in range(ncol)])  3.12 us
    ppermute x4, waiting for transfers between devices, z_shift(): lax.ppermute(x, 'row', [(a, (a + 2 * s) % nrow) for a in range(nrow)])  2.79 us
    pallas_call x1, Pallas kernels, shards(): pl.pallas_call(functools.partial(forward_kernel, step), out_shape=[block]...  1.94 us
    ppermute x1, starting transfers between devices, vec_shift(): return lax.ppermute(x, 'vec', [(a, (a + t) % nvec) for a in range(nvec)])  1.58 us
    ppermute x3, waiting for transfers between devices, send(): return lax.ppermute(x, ('row', 'col'), perm)  1.58 us
    pallas_call x1, Pallas kernels, shards(): pl.pallas_call(functools.partial(mirror_kernel, step), out_shape=[ring, r...  1.39 us
  transfers between devices with their start and end apart: 16, of which 6 were waited for; matrix products, arithmetic and copies ran while one was open for 2% of the time, Pallas kernels for 11%

profile of v10, /device:TPU:0, one launch (start us, length us, event | category | flops | bytes accessed | tf_op | source)
XLA Modules:
  0.0 30.2 jit_solution(336863973286073869)
XLA Ops:
  0.7 0.5 %collective-permute-start = (bf16[8,1024]{1,0:T(8,128)(2,1)}, bf16[8,1024]{1,0:T(8,128)(2,1)S(1)}, u32[]{:S(2)}, u32[]{:S(2)}) collective-permute-start(bf16[8,1024]{1,0:T(8,128)(2,1)} %x), channel_id=1, source_target_pairs={{0,4},{4,0},{8,12},{12,8},{16,20},{20,16},{24,28},{28,24},{1,5},{5... | collective-permute-start | bytes 49160 | tf_op jit(solution)/shard_map/ppermute | solution.py:241
  1.2 2.6 %collective-permute-start.1 = (bf16[8,1024]{1,0:T(8,128)(2,1)}, bf16[8,1024]{1,0:T(8,128)(2,1)S(1)}, u32[]{:S(2)}, u32[]{:S(2)}) collective-permute-start(bf16[8,1024]{1,0:T(8,128)(2,1)} %x), channel_id=1, source_target_pairs={{0,2},{2,0},{1,3},{3,1},{4,6},{6,4},{5,7},{7,5},{8,10},{10,8},{9,1... | collective-permute-start | bytes 49160 | tf_op jit(solution)/shard_map/ppermute | solution.py:247
  3.8 1.6 %collective-permute-start.5 = (bf16[8,1024]{1,0:T(8,128)(2,1)}, bf16[8,1024]{1,0:T(8,128)(2,1)S(1)}, u32[]{:S(2)}, u32[]{:S(2)}) collective-permute-start(bf16[8,1024]{1,0:T(8,128)(2,1)} %x), channel_id=1, source_target_pairs={{0,8},{4,12},{8,16},{12,20},{16,24},{20,28},{24,0},{28,4},{1,9},{5... | collective-permute-start | bytes 49160 | tf_op jit(solution)/shard_map/ppermute | solution.py:244
  5.3 2.6 %collective-permute-start.6 = (bf16[8,1024]{1,0:T(8,128)(2,1)}, bf16[8,1024]{1,0:T(8,128)(2,1)S(1)}, u32[]{:S(2)}, u32[]{:S(2)}) collective-permute-start(bf16[8,1024]{1,0:T(8,128)(2,1)} %x), channel_id=1, source_target_pairs={{0,16},{4,20},{8,24},{12,28},{16,0},{20,4},{24,8},{28,12},{1,17},{... | collective-permute-start | bytes 49160 | tf_op jit(solution)/shard_map/ppermute | solution.py:244
  7.9 1.3 %collective-permute-start.7 = (bf16[8,1024]{1,0:T(8,128)(2,1)}, bf16[8,1024]{1,0:T(8,128)(2,1)S(1)}, u32[]{:S(2)}, u32[]{:S(2)}) collective-permute-start(bf16[8,1024]{1,0:T(8,128)(2,1)} %x), channel_id=1, source_target_pairs={{0,24},{4,28},{8,0},{12,4},{16,8},{20,12},{24,16},{28,20},{1,25},{... | collective-permute-start | bytes 49160 | tf_op jit(solution)/shard_map/ppermute | solution.py:244
  9.9 0.0 collective-permute-done.sibling
  9.9 0.0 collective-permute-done.1.refs_0_
  10.0 0.7 %copy-done.1 = bf16[8,1024]{1,0:T(8,128)(2,1)S(1)} copy-done((bf16[8,1024]{1,0:T(8,128)(2,1)S(1)}, bf16[8,1024]{1,0:T(8,128)(2,1)}, u32[]{:S(2)}) %copy-start.1) | copy-done | bytes 16408
  10.7 1.4 %mirror.1 = (f32[8,4096]{1,0:T(8,128)S(1)}, f32[8,4096]{1,0:T(8,128)S(1)}, bf16[8,1024]{1,0:T(8,128)(2,1)S(1)}, bf16[8,8192]{1,0:T(8,128)(2,1)S(1)}) custom-call(s32[1,1]{1,0:T(1,128)S(6)} %copy.10.counts, s32[1,256]{1,0:T(1,128)S(1)} %bitcast.8, s32[1,256]{1,0:T(1,128)S(1)} %bitcast.10, bf16[256,128,128]{2,1,0:T(8,128)(2,1)S(1)} %bitcast.6, ...), custom_call_target="tpu_custom_call" | custom-call | flops 134217728 | bytes 8388608 | tf_op jit(solution)/shard_map/mirror/pallas_call | solution.py:270
  12.1 0.1 collective-permute-start.2
  12.2 1.6 %collective-permute-start.9 = (bf16[8,8192]{1,0:T(8,128)(2,1)S(1)}, bf16[8,8192]{1,0:T(8,128)(2,1)S(1)}, u32[]{:S(2)}, u32[]{:S(2)}) collective-permute-start(bf16[8,8192]{1,0:T(8,128)(2,1)S(1)} %get-tuple-element.27.refs_5_), channel_id=1, source_target_pairs={{0,1},{1,0},{2,3},{3,2},{4,5},{5,4},{6,7},{7,6},{8,9},{9,8},{10,11... | collective-permute-start | bytes 393224 | tf_op jit(solution)/shard_map/ppermute | solution.py:250
  13.8 0.0 collective-permute-done.5
  13.8 0.0 collective-permute-done.6
  13.8 0.0 collective-permute-done.7
  13.8 0.2 collective-permute-start.8
  14.1 1.1 %collective-permute-start.4 = (f32[8,2048]{1,0:T(8,128)S(1)}, f32[8,2048]{1,0:T(8,128)S(1)}, u32[]{:S(2)}, u32[]{:S(2)}) collective-permute-start(f32[8,2048]{1,0:T(8,128)S(1)} %get-tuple-element.23), channel_id=1, source_target_pairs={{0,16},{4,28},{8,24},{12,4},{16,0},{20,12},{24,8},{28,20},{1,17},{... | collective-permute-start | bytes 196616 | tf_op jit(solution)/shard_map/ppermute | solution.py:300
  15.2 0.7 %collective-permute-start.3 = (f32[8,1024]{1,0:T(8,128)S(1)}, f32[8,1024]{1,0:T(8,128)S(1)}, u32[]{:S(2)}, u32[]{:S(2)}) collective-permute-start(f32[8,1024]{1,0:T(8,128)S(1)} %get-tuple-element.22), channel_id=1, source_target_pairs={{0,8},{4,12},{8,16},{12,20},{16,24},{20,28},{24,0},{28,4},{1,9},{5... | collective-permute-start | bytes 98312 | tf_op jit(solution)/shard_map/ppermute | solution.py:244
  15.9 1.9 %forward.1 = (f32[8,1024]{1,0:T(8,128)S(1)}, f32[8,1024]{1,0:T(8,128)S(1)}) custom-call(s32[1,1]{1,0:T(1,128)S(6)} %copy.10.counts, s32[1,256]{1,0:T(1,128)S(1)} %bitcast.9, s32[1,256]{1,0:T(1,128)S(1)} %bitcast.11, bf16[256,128,128]{2,1,0:T(8,128)(2,1)S(1)} %bitcast.7, bf16[8,4096]{1,0:T(8,128)(2,1)S(1)} %constant_dynamic-update-slice_fusion.near, ...), custom_call_target="tpu_custom_call" | custom-call | flops 134217728 | bytes 8388608 | tf_op jit(solution)/shard_map/forward/pallas_call | solution.py:302
  17.8 0.3 collective-permute-done.9.refs_6_
  18.1 2.8 %collective-permute-done.3.refs_1_ = f32[8,1024]{1,0:T(8,128)S(1)} collective-permute-done((f32[8,1024]{1,0:T(8,128)S(1)}, f32[8,1024]{1,0:T(8,128)S(1)}, u32[]{:S(2)}, u32[]{:S(2)}) %collective-permute-start.3) | collective-permute-done | bytes 32800 | tf_op jit(solution)/shard_map/ppermute | solution.py:244
  20.9 0.3 %gram.1 = (f32[8,1024]{1,0:T(8,128)S(1)}, f32[8,16]{1,0:T(8,128)S(1)}, f32[8,1152]{1,0:T(8,128)S(1)}, f32[8,1152]{1,0:T(8,128)S(1)}) custom-call(f32[8,1024]{1,0:T(8,128)S(1)} %get-tuple-element.21.refs_0_, f32[8,1024]{1,0:T(8,128)S(1)} %collective-permute-done.3.refs_1_, f32[8,2048]{1,0:T(8,128)S(1)} %collective-permute-done.4.refs_2_, ...), custom_call_target="tpu_custom_call" | custom-call | tf_op jit(solution)/shard_map/gram/pallas_call | solution.py:315
  21.2 0.6 %collective-permute-start.11 = (f32[8,1152]{1,0:T(8,128)S(1)}, f32[8,1152]{1,0:T(8,128)S(1)}, u32[]{:S(2)}, u32[]{:S(2)}) collective-permute-start(f32[8,1152]{1,0:T(8,128)S(1)} %get-tuple-element.30), channel_id=1, source_target_pairs={{0,2},{2,0},{1,3},{3,1},{4,6},{6,4},{5,7},{7,5},{8,10},{10,8},{9,1... | collective-permute-start | bytes 110600 | tf_op jit(solution)/shard_map/ppermute | solution.py:247
  21.8 0.7 %collective-permute-done.10 = f32[8,1152]{1,0:T(8,128)S(1)} collective-permute-done((f32[8,1152]{1,0:T(8,128)S(1)}, f32[8,1152]{1,0:T(8,128)S(1)}, u32[]{:S(2)}, u32[]{:S(2)}) %collective-permute-start.10) | collective-permute-done | bytes 36896 | tf_op jit(solution)/shard_map/ppermute | solution.py:241
  22.4 1.3 %collective-permute-start.14 = (f32[8,16]{1,0:T(8,128)S(1)}, f32[8,16]{1,0:T(8,128)S(1)}, u32[]{:S(2)}, u32[]{:S(2)}) collective-permute-start(f32[8,16]{1,0:T(8,128)S(1)} %slice_add_fusion.3), channel_id=1, source_target_pairs={{0,24},{2,26},{4,30},{6,28},{8,16},{10,18},{12,22},{14,20},{16,8},... | collective-permute-start | bytes 1544 | tf_op jit(solution)/shard_map/ppermute | solution.py:346
  23.8 0.0 collective-permute-start.13
  23.8 3.0 %collective-permute-start.12 = (f32[8,16]{1,0:T(8,128)S(1)}, f32[8,16]{1,0:T(8,128)S(1)}, u32[]{:S(2)}, u32[]{:S(2)}) collective-permute-start(f32[8,16]{1,0:T(8,128)S(1)} %slice_add_fusion.3), channel_id=1, source_target_pairs={{0,16},{2,18},{4,22},{6,20},{8,24},{10,26},{12,30},{14,28},{16,0},... | collective-permute-start | bytes 1544 | tf_op jit(solution)/shard_map/ppermute | solution.py:346
  26.8 1.0 %collective-permute-done.14 = f32[8,16]{1,0:T(8,128)S(1)} collective-permute-done((f32[8,16]{1,0:T(8,128)S(1)}, f32[8,16]{1,0:T(8,128)S(1)}, u32[]{:S(2)}, u32[]{:S(2)}) %collective-permute-start.14) | collective-permute-done | bytes 544 | tf_op jit(solution)/shard_map/ppermute | solution.py:346
  27.8 0.6 %collective-permute-done.12 = f32[8,16]{1,0:T(8,128)S(1)} collective-permute-done((f32[8,16]{1,0:T(8,128)S(1)}, f32[8,16]{1,0:T(8,128)S(1)}, u32[]{:S(2)}, u32[]{:S(2)}) %collective-permute-start.12) | collective-permute-done | bytes 544 | tf_op jit(solution)/shard_map/ppermute | solution.py:346
  28.4 0.1 collective-permute-start.15
  28.5 0.6 %fusion = bf16[8,1024]{1,0:T(8,128)(2,1)} fusion(f32[8,1152]{1,0:T(8,128)S(1)} %collective-permute-done.11, f32[8,1024]{1,0:T(8,128)S(1)} %get-tuple-element.28, f32[8,1152]{1,0:T(8,128)S(1)} %collective-permute-done.10), kind=kLoop, calls=%fused_computation.1 | loop fusion | flops 24576 | bytes 114688 | tf_op jit(solution)/shard_map/convert_element_type | solution.py:333
  29.2 0.4 %collective-permute-done.15 = f32[8,16]{1,0:T(8,128)S(1)} collective-permute-done((f32[8,16]{1,0:T(8,128)S(1)}, f32[8,16]{1,0:T(8,128)S(1)}, u32[]{:S(2)}, u32[]{:S(2)}) %collective-permute-start.15) | collective-permute-done | bytes 544 | tf_op jit(solution)/shard_map/ppermute | solution.py:349
  29.6 0.6 %add_bitcast_fusion = f32[16,8]{0,1:T(8,128)} fusion(f32[8,16]{1,0:T(8,128)S(1)} %collective-permute-done.15, f32[8,16]{1,0:T(8,128)S(1)} %slice_add_fusion.3, f32[8,16]{1,0:T(8,128)S(1)} %fusion.2), kind=kLoop, calls=%fused_computation.11 | loop fusion | flops 256 | bytes 2048 | tf_op jit(solution)/shard_map/transpose | solution.py:332
  (21 shorter events, 0.1 us)
Async XLA Ops:
  0.6 9.3 %copy-start = (bf16[1,1,256,128,128]{4,3,2,1,0:T(8,128)(2,1)S(1)}, bf16[1,1,256,128,128]{4,3,2,1,0:T(8,128)(2,1)}, u32[]{:S(2)}) copy-start(bf16[1,1,256,128,128]{4,3,2,1,0:T(8,128)(2,1)} %param.6) | copy-start | bytes 25165828
  0.6 9.3 %copy-start.2 = (s32[1,1,256]{2,1,0:T(1,128)S(1)}, s32[1,1,256]{2,1,0:T(1,128)}, u32[]{:S(2)}) copy-start(s32[1,1,256]{2,1,0:T(1,128)} %param.7) | copy-start | bytes 3076
  0.7 9.3 %copy-start.3 = (s32[1,1,256]{2,1,0:T(1,128)S(1)}, s32[1,1,256]{2,1,0:T(1,128)}, u32[]{:S(2)}) copy-start(s32[1,1,256]{2,1,0:T(1,128)} %param.8) | copy-start | bytes 3076
  0.7 9.3 %collective-permute-start = (bf16[8,1024]{1,0:T(8,128)(2,1)}, bf16[8,1024]{1,0:T(8,128)(2,1)S(1)}, u32[]{:S(2)}, u32[]{:S(2)}) collective-permute-start(bf16[8,1024]{1,0:T(8,128)(2,1)} %x), channel_id=1, source_target_pairs={{0,4},{4,0},{8,12},{12,8},{16,20},{20,16},{24,28},{28,24},{1,5},{5... | collective-permute-start | bytes 49160 | tf_op jit(solution)/shard_map/ppermute | solution.py:241
  1.2 8.7 %collective-permute-start.1 = (bf16[8,1024]{1,0:T(8,128)(2,1)}, bf16[8,1024]{1,0:T(8,128)(2,1)S(1)}, u32[]{:S(2)}, u32[]{:S(2)}) collective-permute-start(bf16[8,1024]{1,0:T(8,128)(2,1)} %x), channel_id=1, source_target_pairs={{0,2},{2,0},{1,3},{3,1},{4,6},{6,4},{5,7},{7,5},{8,10},{10,8},{9,1... | collective-permute-start | bytes 49160 | tf_op jit(solution)/shard_map/ppermute | solution.py:247
  3.8 10.0 %collective-permute-start.5 = (bf16[8,1024]{1,0:T(8,128)(2,1)}, bf16[8,1024]{1,0:T(8,128)(2,1)S(1)}, u32[]{:S(2)}, u32[]{:S(2)}) collective-permute-start(bf16[8,1024]{1,0:T(8,128)(2,1)} %x), channel_id=1, source_target_pairs={{0,8},{4,12},{8,16},{12,20},{16,24},{20,28},{24,0},{28,4},{1,9},{5... | collective-permute-start | bytes 49160 | tf_op jit(solution)/shard_map/ppermute | solution.py:244
  5.3 8.4 %collective-permute-start.6 = (bf16[8,1024]{1,0:T(8,128)(2,1)}, bf16[8,1024]{1,0:T(8,128)(2,1)S(1)}, u32[]{:S(2)}, u32[]{:S(2)}) collective-permute-start(bf16[8,1024]{1,0:T(8,128)(2,1)} %x), channel_id=1, source_target_pairs={{0,16},{4,20},{8,24},{12,28},{16,0},{20,4},{24,8},{28,12},{1,17},{... | collective-permute-start | bytes 49160 | tf_op jit(solution)/shard_map/ppermute | solution.py:244
  7.9 5.9 %collective-permute-start.7 = (bf16[8,1024]{1,0:T(8,128)(2,1)}, bf16[8,1024]{1,0:T(8,128)(2,1)S(1)}, u32[]{:S(2)}, u32[]{:S(2)}) collective-permute-start(bf16[8,1024]{1,0:T(8,128)(2,1)} %x), channel_id=1, source_target_pairs={{0,24},{4,28},{8,0},{12,4},{16,8},{20,12},{24,16},{28,20},{1,25},{... | collective-permute-start | bytes 49160 | tf_op jit(solution)/shard_map/ppermute | solution.py:244
  10.0 0.7 %copy-start.1 = (bf16[8,1024]{1,0:T(8,128)(2,1)S(1)}, bf16[8,1024]{1,0:T(8,128)(2,1)}, u32[]{:S(2)}) copy-start(bf16[8,1024]{1,0:T(8,128)(2,1)} %x) | copy-start | bytes 49156
  12.1 1.9 %collective-permute-start.2 = (f32[8,4096]{1,0:T(8,128)S(1)}, f32[8,4096]{1,0:T(8,128)S(1)}, u32[]{:S(2)}, u32[]{:S(2)}) collective-permute-start(f32[8,4096]{1,0:T(8,128)S(1)} %get-tuple-element.20), channel_id=1, source_target_pairs={{0,4},{4,0},{8,12},{12,8},{16,20},{20,16},{24,28},{28,24},{1,5},{5... | collective-permute-start | bytes 393224 | tf_op jit(solution)/shard_map/ppermute | solution.py:241
  12.2 5.9 %collective-permute-start.9 = (bf16[8,8192]{1,0:T(8,128)(2,1)S(1)}, bf16[8,8192]{1,0:T(8,128)(2,1)S(1)}, u32[]{:S(2)}, u32[]{:S(2)}) collective-permute-start(bf16[8,8192]{1,0:T(8,128)(2,1)S(1)} %get-tuple-element.27.refs_5_), channel_id=1, source_target_pairs={{0,1},{1,0},{2,3},{3,2},{4,5},{5,4},{6,7},{7,6},{8,9},{9,8},{10,11... | collective-permute-start | bytes 393224 | tf_op jit(solution)/shard_map/ppermute | solution.py:250
  13.8 2.0 %collective-permute-start.8 = (bf16[8,4096]{1,0:T(8,128)(2,1)S(1)}, bf16[8,4096]{1,0:T(8,128)(2,1)S(1)}, u32[]{:S(2)}, u32[]{:S(2)}) collective-permute-start(bf16[8,4096]{1,0:T(8,128)(2,1)S(1)} %constant_dynamic-update-slice_fusion.near), channel_id=1, source_target_pairs={{0,4},{4,0},{8,12},{12,8},{16,20},{20,16},{24,28},{28,24},{1,5},{5... | collective-permute-start | bytes 196616 | tf_op jit(solution)/shard_map/ppermute | solution.py:241
  14.1 6.8 %collective-permute-start.4 = (f32[8,2048]{1,0:T(8,128)S(1)}, f32[8,2048]{1,0:T(8,128)S(1)}, u32[]{:S(2)}, u32[]{:S(2)}) collective-permute-start(f32[8,2048]{1,0:T(8,128)S(1)} %get-tuple-element.23), channel_id=1, source_target_pairs={{0,16},{4,28},{8,24},{12,4},{16,0},{20,12},{24,8},{28,20},{1,17},{... | collective-permute-start | bytes 196616 | tf_op jit(solution)/shard_map/ppermute | solution.py:300
  15.2 5.7 %collective-permute-start.3 = (f32[8,1024]{1,0:T(8,128)S(1)}, f32[8,1024]{1,0:T(8,128)S(1)}, u32[]{:S(2)}, u32[]{:S(2)}) collective-permute-start(f32[8,1024]{1,0:T(8,128)S(1)} %get-tuple-element.22), channel_id=1, source_target_pairs={{0,8},{4,12},{8,16},{12,20},{16,24},{20,28},{24,0},{28,4},{1,9},{5... | collective-permute-start | bytes 98312 | tf_op jit(solution)/shard_map/ppermute | solution.py:244
  21.2 1.2 %collective-permute-start.10 = (f32[8,1152]{1,0:T(8,128)S(1)}, f32[8,1152]{1,0:T(8,128)S(1)}, u32[]{:S(2)}, u32[]{:S(2)}) collective-permute-start(f32[8,1152]{1,0:T(8,128)S(1)} %get-tuple-element.29), channel_id=1, source_target_pairs={{0,4},{4,0},{8,12},{12,8},{16,20},{20,16},{24,28},{28,24},{1,5},{5... | collective-permute-start | bytes 110600 | tf_op jit(solution)/shard_map/ppermute | solution.py:241
  21.2 5.6 %collective-permute-start.11 = (f32[8,1152]{1,0:T(8,128)S(1)}, f32[8,1152]{1,0:T(8,128)S(1)}, u32[]{:S(2)}, u32[]{:S(2)}) collective-permute-start(f32[8,1152]{1,0:T(8,128)S(1)} %get-tuple-element.30), channel_id=1, source_target_pairs={{0,2},{2,0},{1,3},{3,1},{4,6},{6,4},{5,7},{7,5},{8,10},{10,8},{9,1... | collective-permute-start | bytes 110600 | tf_op jit(solution)/shard_map/ppermute | solution.py:247
  22.4 5.4 %collective-permute-start.14 = (f32[8,16]{1,0:T(8,128)S(1)}, f32[8,16]{1,0:T(8,128)S(1)}, u32[]{:S(2)}, u32[]{:S(2)}) collective-permute-start(f32[8,16]{1,0:T(8,128)S(1)} %slice_add_fusion.3), channel_id=1, source_target_pairs={{0,24},{2,26},{4,30},{6,28},{8,16},{10,18},{12,22},{14,20},{16,8},... | collective-permute-start | bytes 1544 | tf_op jit(solution)/shard_map/ppermute | solution.py:346
  23.8 4.1 %collective-permute-start.13 = (f32[8,16]{1,0:T(8,128)S(1)}, f32[8,16]{1,0:T(8,128)S(1)}, u32[]{:S(2)}, u32[]{:S(2)}) collective-permute-start(f32[8,16]{1,0:T(8,128)S(1)} %slice_add_fusion.3), channel_id=1, source_target_pairs={{0,8},{2,10},{4,14},{6,12},{8,0},{10,2},{12,6},{14,4},{16,24},{18,... | collective-permute-start | bytes 1544 | tf_op jit(solution)/shard_map/ppermute | solution.py:346
  23.8 4.6 %collective-permute-start.12 = (f32[8,16]{1,0:T(8,128)S(1)}, f32[8,16]{1,0:T(8,128)S(1)}, u32[]{:S(2)}, u32[]{:S(2)}) collective-permute-start(f32[8,16]{1,0:T(8,128)S(1)} %slice_add_fusion.3), channel_id=1, source_target_pairs={{0,16},{2,18},{4,22},{6,20},{8,24},{10,26},{12,30},{14,28},{16,0},... | collective-permute-start | bytes 1544 | tf_op jit(solution)/shard_map/ppermute | solution.py:346
  28.4 1.2 %collective-permute-start.15 = (f32[8,16]{1,0:T(8,128)S(1)}, f32[8,16]{1,0:T(8,128)S(1)}, u32[]{:S(2)}, u32[]{:S(2)}) collective-permute-start(f32[8,16]{1,0:T(8,128)S(1)} %fusion.2), channel_id=1, source_target_pairs={{0,4},{4,0},{8,12},{12,8},{16,20},{20,16},{24,28},{28,24},{1,5},{5... | collective-permute-start | bytes 1544 | tf_op jit(solution)/shard_map/ppermute | solution.py:349
